TPU v7x, 512 devices: a whole 4x4x16 slice. The times are simulated.
512 devices in a mesh: tm: 16 (over z), req: 32 (over y, x, core).
Axes of the slice: x: 4, y: 4, z: 16, core: 2. Of those that a mesh axis runs over, the one named last changes fastest.
Arguments:
- latents: float32 [16, 64, 4096], P('tm', None, 'req'), may hold values from -6 to 6
- time_terms: float32 [16, 4, 3072], replicated, may hold values from -4 to 4
- step_sizes: float32 [16], replicated, may hold values from 0.05 to 0.25
- doc_embed: bfloat16 [256, 3072], P('req', 'tm'), may hold values from -6 to 6
- pack_docs: int32 [256], P('req'), may hold values from 0 to 255, each once
- segment_ids: int32 [32, 128], P('req'), may hold values from 0 to 7, never falling along the last dimension, each value on 1 to 64 neighbouring positions
- w_in: bfloat16 [64, 3072], replicated, may hold values from -0.75 to 0.75
- w_qkv: bfloat16 [3072, 3, 16, 128], P(None, None, 'tm')
- query_gain: float32 [16, 128], P('tm'), may hold values from 0.5 to 6, as said below
- key_gain: float32 [16, 128], P('tm'), may hold values from 0.5 to 6, as said below
- w_proj: bfloat16 [16, 128, 3072], P('tm'), may hold values from -0.125 to 0.125
- w_final: bfloat16 [3072, 64], replicated, may hold values from -0.109375 to 0.109375
Outputs:
- new_latents: float32 [16, 64, 4096], P('tm', None, 'req')
Inputs may be any that keep to these rules, and one draw needn't show every extreme that they name: `pack_docs`: a permutation of the documents; pack r holds the documents at positions r * 8 to (r + 1) * 8 - 1. `segment_ids`: in each pack the segment numbers never fall, every segment 0 to 7 is present with 1 to 64 slots, and one has exactly 64. `query_gain`: positive gains. `key_gain`: positive gains.
All inputs are finite; a program needn't handle non-finite values.
Results may differ from a plain program's by a relative error of at most 0.004.
Values may be sent and summed in bfloat16 or wider, within the bound.
No kernel may reach another device: no remote copies, remote signals or barrier semaphores. Data moves between devices by JAX's collectives and lax.ppermute only.
A program may use at most 64 MiB of HBM per device.

v0:
```python
import jax
import jax.numpy as jnp
from jax import lax
from jax.sharding import PartitionSpec as P

EPS = 1e-06
MASKED = -1e30


def entering(part, axis, combine, identity):
    place = lax.axis_index(axis)
    gathered = lax.all_gather(part, axis)
    state = jnp.zeros_like(part) + jnp.asarray(identity, part.dtype)

    def one(hop, state):
        return combine(state, lax.dynamic_index_in_dim(gathered, hop, 0, False))

    return lax.fori_loop(0, place, one, state)


def layer_norm(values):
    mean = jnp.mean(values, axis=-1, keepdims=True)
    centred = values - mean
    spread = jnp.mean(centred * centred, axis=-1, keepdims=True)
    return centred * lax.rsqrt(spread + EPS)


def rms_scale(values, gains):
    power = jnp.mean(values * values, axis=-1, keepdims=True)
    return (values * lax.rsqrt(power + EPS) * gains).astype(jnp.bfloat16)


def hidden_state(latent_block, terms, token_vectors, w_in):
    lowered = latent_block.astype(jnp.bfloat16)
    hidden = lax.dot_general(
        lowered, w_in, (((0,), (0,)), ((), ())), preferred_element_type=jnp.float32
    )
    hidden = hidden + terms[0] + token_vectors
    modulated = layer_norm(hidden) * (1.0 + terms[2]) + terms[1]
    return (hidden, modulated.astype(jnp.bfloat16))


def head_parts(normed, gates, same_doc, w_qkv, query_gain, key_gain, w_proj, w_final):
    projected = jnp.einsum("tnd,dche->tnche", normed, w_qkv, preferred_element_type=jnp.float32)
    queries = rms_scale(projected[:, :, 0], query_gain)
    keys = rms_scale(projected[:, :, 1], key_gain)
    values = projected[:, :, 2].astype(jnp.bfloat16)
    scale = queries.shape[-1] ** (-0.5)
    scores = (
        jnp.einsum("tqhe,tphe->thqp", queries, keys, preferred_element_type=jnp.float32) * scale
    )
    scores = jnp.where(same_doc[None, None], scores, MASKED)
    top = jnp.max(scores, axis=-1, keepdims=True)
    raised = jnp.exp(scores - top)
    weights = (raised / jnp.sum(raised, axis=-1, keepdims=True)).astype(jnp.bfloat16)
    attended = jnp.einsum(
        "thqp,tphe->tqhe", weights, values, preferred_element_type=jnp.float32
    ).astype(jnp.bfloat16)

    def project(pair):
        rows, gate = pair
        outer = (
            jnp.einsum("qhe,hed->hqd", rows, w_proj, preferred_element_type=jnp.float32) * gate
        ).astype(jnp.bfloat16)
        return jnp.einsum("dc,hqd->cq", w_final, outer, preferred_element_type=jnp.float32)

    return lax.map(project, (attended, gates))


def add_terms(earlier, later):
    return earlier + later


def local(
    latents,
    time_terms,
    step_sizes,
    doc_embed,
    pack_docs,
    segment_ids,
    w_in,
    w_qkv,
    query_gain,
    key_gain,
    w_proj,
    w_final,
):
    here = lax.axis_index("tm")
    columns = lax.all_gather(doc_embed, "tm", axis=1, tiled=True)
    table = lax.all_gather(columns, "req", axis=0, tiled=True)
    chosen = jnp.take(table, pack_docs, axis=0)
    segments = segment_ids[0]
    docs_here = chosen.shape[0]
    member = (segments[:, None] == jnp.arange(docs_here, dtype=jnp.int32)[None, :]).astype(
        jnp.bfloat16
    )
    token_vectors = jnp.dot(member, chosen, preferred_element_type=jnp.float32)
    same_doc = segments[:, None] == segments[None, :]
    w_final_wide = w_final.astype(jnp.float32)
    own_terms = time_terms[here]
    own_hidden, own_normed = hidden_state(latents[0], own_terms, token_vectors, w_in)
    residual = lax.dot_general(
        w_final_wide, own_hidden, (((0,), (1,)), ((), ())), precision=lax.Precision.HIGHEST
    )
    parts = head_parts(
        lax.all_gather(own_normed[None], "tm", axis=0, tiled=True),
        time_terms[:, 3],
        same_doc,
        w_qkv,
        query_gain,
        key_gain,
        w_proj,
        w_final,
    )
    first_latent = jnp.where(here == 0, latents[0], 0.0)
    total = lax.psum_scatter(
        parts.astype(jnp.bfloat16), "tm", scatter_dimension=0, tiled=True
    ).astype(jnp.float32)[0]
    drift = residual + total
    term = step_sizes[here] * drift + first_latent
    before = entering(term, "tm", add_terms, jnp.zeros_like(term))
    updated = jnp.where(here == 0, latents[0], before)
    return updated[None]


def solution(mesh):
    in_specs = (
        P("tm", None, "req"),
        P(),
        P(),
        P("req", "tm"),
        P("req"),
        P("req", None),
        P(),
        P(None, None, "tm", None),
        P("tm", None),
        P("tm", None),
        P("tm", None, None),
        P(),
    )
    out_specs = P("tm", None, "req")
    return jax.shard_map(local, mesh=mesh, in_specs=in_specs, out_specs=out_specs, check_vma=False)
```

profile of v0, /device:TPU:2, one launch (start us, length us, event | category | flops | bytes accessed | tf_op | source)
XLA Modules:
  0.0 422.6 jit_solution(2574984636731162408)
XLA Ops:
  6.5 36.1 %all-gather.2 = bf16[16,192,8]{1,2,0:T(8,128)(2,1)S(1)} all-gather(bf16[1,192,8]{1,2,0:T(8,128)(2,1)} %bitcast.129), channel_id=1, replica_groups=mesh['tm'=16,'req'=32] {'tm'}, dimensions={0}, use_global_device_ids=true | all-gather | bytes 52224 | tf_op jit(solution)/shard_map/all_gather | solution.py:89
  42.7 0.7 reshape.195
  43.4 0.0 all-gather.8.cloned.1.call-start
  43.5 0.7 compare_select_fusion
  44.1 0.7 compare_and_fusion
  44.8 0.9 dynamic-slice_add_fusion
  45.7 2.6 convolution_add_fusion.1
  48.3 49.5 %all-gather.6.cloned.1.call-done = bf16[256,3072]{1,0:T(8,128)(2,1)} async-done(((bf16[8,3072]{1,0:T(8,128)(2,1)}), bf16[256,3072]{1,0:T(8,128)(2,1)}) %all-gather.6.cloned.1.call-update) | async-done | bytes 1572880 | tf_op jit(solution)/shard_map/all_gather | solution.py:90
  97.8 2.2 gather_fusion
  100.1 1.9 fusion.47
  102.0 0.3 multiply_reduce_fusion
  102.3 0.9 copy-done.1
  103.2 1.2 add_convert_fusion
  104.5 1.3 slice.31
  105.8 0.7 copy.43
  106.5 0.1 broadcast_compare_fusion
  106.6 145.8 %all-gather.8.cloned.1.call-done = bf16[2048,3072]{1,0:T(8,128)(2,1)} async-done(((bf16[128,3072]{1,0:T(8,128)(2,1)}), bf16[2048,3072]{1,0:T(8,128)(2,1)}) %all-gather.8.cloned.1.call-update) | async-done | bytes 12582928 | tf_op jit(solution)/shard_map/all_gather | solution.py:106
  252.4 8.1 %fusion.16 = f32[16,128,3,1,128]{1,4,2,0,3:T(8,128)S(1)} fusion(bf16[16,128,3072,1]{2,1,3,0:T(8,128)(2,1)} %bitcast.132, bf16[3072,3,1,128]{3,0,2,1:T(8,128)(2,1)S(1)} %copy-done), kind=kOutput, calls=%fused_computation.18 | convolution fusion | flops 4831838208 | bytes 18087936 | tf_op jit(solution)/shard_map/tnd,dche->tnche/dot_general | solution.py:44
  260.5 0.2 multiply_reduce_fusion.2
  260.7 0.5 copy-done.8
  261.2 0.1 copy-done.9
  261.3 0.5 fusion.21
  261.7 0.4 copy-done.4
  262.2 1.0 copy-done.5
  263.1 0.2 fusion.48
  263.4 3.2 fusion.22
  266.6 48.6 %while.20 = (s32[]{:T(128)}, bf16[16,64,128]{2,1,0:T(8,128)(2,1)}, bf16[16,128,1,128]{1,3,0,2:T(8,128)(2,1)}, bf16[1,128,3072]{2,1,0:T(8,128)(2,1)S(1)}, f32[16,...) while((s32[]{:T(128)}, bf16[16,64,128]{2,1,0:T(8,128)(2,1)}, ...), condition=%wide.region_7.8_spmd, body=%wide.region_6.7_spmd.sunk | while | flops 151781376 | bytes 1283153 | solution.py:67
  266.6 0.9 constant_dynamic-slice_fusion.4
  267.5 2.1 fusion.67
  269.6 0.9 constant_dynamic-slice_fusion.4
  270.5 2.1 fusion.67
  272.7 0.9 constant_dynamic-slice_fusion.4
  273.6 2.1 fusion.67
  275.7 0.9 constant_dynamic-slice_fusion.4
  276.6 2.1 fusion.67
  278.8 0.9 constant_dynamic-slice_fusion.4
  279.7 2.1 fusion.67
  281.8 0.9 constant_dynamic-slice_fusion.4
  282.7 2.1 fusion.67
  284.8 0.9 constant_dynamic-slice_fusion.4
  285.7 2.1 fusion.67
  287.9 0.9 constant_dynamic-slice_fusion.4
  288.8 2.1 fusion.67
  290.9 0.9 constant_dynamic-slice_fusion.4
  291.8 2.1 fusion.67
  293.9 0.9 constant_dynamic-slice_fusion.4
  294.9 2.1 fusion.67
  297.0 0.9 constant_dynamic-slice_fusion.4
  297.9 2.1 fusion.67
  300.0 0.9 constant_dynamic-slice_fusion.4
  300.9 2.1 fusion.67
  303.1 0.9 constant_dynamic-slice_fusion.4
  304.0 2.1 fusion.67
  306.1 0.9 constant_dynamic-slice_fusion.4
  307.0 2.1 fusion.67
  309.1 0.9 constant_dynamic-slice_fusion.4
  310.0 2.1 fusion.67
  312.2 0.9 constant_dynamic-slice_fusion.4
  313.1 2.1 fusion.67
  315.3 0.6 dynamic_slice.18
  315.8 66.3 %reduce-scatter.2.cloned.1.call-done = bf16[1,64,128]{2,1,0:T(8,128)(2,1)} async-done(((bf16[16,64,128]{2,1,0:T(8,128)(2,1)}), bf16[1,64,128]{2,1,0:T(8,128)(2,1)}) %reduce-scatter.2.cloned.1.call-update) | async-done | bytes 16400 | tf_op jit(solution)/shard_map/reduce_scatter | solution.py:116
  382.1 3.0 fusion.25
  385.2 30.3 %all-gather.1 = f32[1024,128]{1,0:T(8,128)S(1)} all-gather(f32[64,128]{1,0:T(8,128)S(1)} %fusion.25), channel_id=3, replica_groups=mesh['tm'=16,'req'=32] {'tm'}, dimensions={0}, use_global_device_ids=true | all-gather | bytes 557056 | tf_op jit(solution)/shard_map/all_gather | solution.py:12
  415.4 0.6 fusion.41
  (30 shorter events, 0.2 us)
Async XLA Ops:
  6.5 245.9 %copy-start = (bf16[3072,3,1,128]{3,0,2,1:T(8,128)(2,1)S(1)}, bf16[3072,3,1,128]{3,0,2,1:T(8,128)(2,1)}, u32[]{:S(2)}) copy-start(bf16[3072,3,1,128]{3,0,2,1:T(8,128)(2,1)} %param.23) | copy-start | bytes 7077892
  6.5 93.5 %copy-start.7 = (s32[1,128]{1,0:T(1,128)S(1)}, s32[1,128]{1,0:T(1,128)}, u32[]{:S(2)}) copy-start(s32[1,128]{1,0:T(1,128)} %param.21) | copy-start | bytes 1540
  6.5 91.3 %all-gather.6.cloned.1.call-start = ((), (), s32[]{:S(2)}) async-start(), calls=%async_computation.1 | async-start | bytes 1622016 | tf_op jit(solution)/shard_map/all_gather | solution.py:90
  43.4 209.0 %all-gather.8.cloned.1.call-start = ((), (), s32[]{:S(2)}) async-start(), calls=%async_computation.3 | async-start | bytes 13369344 | tf_op jit(solution)/shard_map/all_gather | solution.py:106
  102.0 1.2 copy-start.1
  104.4 277.7 %reduce-scatter.2.cloned.1.call-start = ((), (), s32[]{:S(2)}) async-start(), calls=%async_computation.2 | async-start | bytes 278528 | tf_op jit(solution)/shard_map/reduce_scatter | solution.py:116
  260.5 1.7 copy-start.4
  260.5 0.7 copy-start.8
  260.5 0.7 copy-start.9
  262.2 1.0 copy-start.5
  263.4 3.2 copy-start.2
  263.4 3.2 copy-start.3
  266.6 48.7 %copy-start.10 = (f32[16]{0:T(128)S(1)}, f32[16]{0:T(128)}, u32[]{:S(2)}) copy-start(f32[16]{0:T(128)} %param.18) | copy-start | bytes 196
  382.1 33.3 %copy-start.6 = (f32[1,64,128]{2,1,0:T(8,128)S(1)}, f32[1,64,128]{2,1,0:T(8,128)}, u32[]{:S(2)}) copy-start(f32[1,64,128]{2,1,0:T(8,128)} %param.16) | copy-start | bytes 98308
Sparse Core Ops, SparseCore 0:
  43.5 54.2 all-gather.5
  104.5 147.8 all-gather.7
  315.4 66.7 reduce-scatter.1
where the time goes:
time: 425 us; the launch traced here: 423 us
  waiting for transfers between devices  262 us (62%)
  blocking collectives  66.4 us (16%)
  matrix products  53.4 us (13%)
  local copies, waits for them, and re-layouts  22.9 us (5%)
  between operations  13.3 us (3%)
  other arithmetic  4.91 us (1%)
    all_gather x1, waiting for transfers between devices, local(): lax.all_gather(own_normed[None], 'tm', axis=0, tiled=True)  146 us
    reduce_scatter x1, waiting for transfers between devices, local(): lax.psum_scatter(parts.astype(jnp.bfloat16), 'tm', scatter_dimension=0, t...  66.3 us
    all_gather x1, waiting for transfers between devices, local(): table = lax.all_gather(columns, 'req', axis=0, tiled=True)  49.5 us
    all_gather x1, blocking collectives, local(): columns = lax.all_gather(doc_embed, 'tm', axis=1, tiled=True)  36.1 us
    dot_general x16, matrix products, project(): jnp.einsum('dc,hqd->cq', w_final, outer, preferred_element_type=jnp.float32)  34.1 us
    all_gather x1, blocking collectives, entering(): gathered = lax.all_gather(part, axis)  30.3 us
    dynamic_slice x16, local copies, waits for them, and re-layouts, head_parts(): return lax.map(project, (attended, gates))  14.4 us
  transfers between devices with their start and end apart: 3, of which 3 were waited for; matrix products, arithmetic and copies ran while one was open for 2% of the time, Pallas kernels for 0%

commit v1 on v0

v1 whole, which is shorter than its diff:
```python
import functools

import jax
import jax.numpy as jnp
from jax import lax
from jax.experimental import pallas as pl
from jax.experimental.pallas import tpu as pltpu
from jax.sharding import PartitionSpec as P

EPS = 1e-06
MASKED = -1e30
BF16, F32 = jnp.bfloat16, jnp.float32
HIGHEST = lax.Precision.HIGHEST
NN = (((1,), (0,)), ((), ()))
NT = (((1,), (1,)), ((), ()))
VMEM = pl.BlockSpec(memory_space=pltpu.VMEM)
SMEM = pl.BlockSpec(memory_space=pltpu.SMEM)
PARAMS = pltpu.CompilerParams(vmem_limit_bytes=48 * 2**20)


def dot(left, right, dims=NN, precision=None):
    return lax.dot_general(left, right, dims, precision=precision, preferred_element_type=F32)


def two_parts(values):
    high = values.astype(BF16)
    return high, (values - high.astype(F32)).astype(BF16)


def centre(values):
    return values - jnp.mean(values, axis=-1, keepdims=True)


def weights_kernel(
    steps, w_in, terms, w_qkv, w_final, w_proj, inward, shifts, outward, centred, rows, shift_rows
):
    times, chans = inward.shape[0], w_in.shape[0]
    wide, head = terms.shape[2], w_proj.shape[0]
    group = rows.shape[0] // chans
    centred[...] = centre(w_in[...].astype(F32))
    gram = dot(centred[...], centred[...], NT, HIGHEST)
    gram = jnp.concatenate(two_parts(gram), axis=0)
    gram = jnp.concatenate([gram, jnp.zeros_like(gram)], axis=1)

    def one(step, carry):
        for j in range(group):
            t = step * group + j
            scaled = centred[...] * (1.0 + terms[t, 2:3, :])
            rows[j * chans : (j + 1) * chans, :] = scaled.astype(BF16)
            shift_rows[pl.ds(t, 1), :] = terms[t, 1:2, :]
        for c in range(3):
            high, low = two_parts(dot(rows[...], w_qkv[c]))
            for j in range(group):
                t = step * group + j
                span = slice(j * chans, (j + 1) * chans)
                inward[t, :chans, c * head : (c + 1) * head] = high[span]
                inward[t, chans:, c * head : (c + 1) * head] = low[span]
        for j in range(group):
            t = step * group + j
            inward[t, :, 3 * head :] = gram
            gated = w_final[...].astype(F32) * terms[t, 3:4, :]
            rows[j * chans : (j + 1) * chans, :] = gated.astype(BF16)
        back = dot(rows[...], w_proj[...], NT)
        for j in range(group):
            t = step * group + j
            outward[t] = (back[j * chans : (j + 1) * chans] * steps[t]).astype(BF16)
        return carry

    lax.fori_loop(0, times // group, one, 0)
    high, low = two_parts(shift_rows[...])
    for c in range(3):
        shifts[:, c * head : (c + 1) * head] = dot(high, w_qkv[c]) + dot(low, w_qkv[c])


def heads_kernel(
    low,
    docs,
    terms,
    w_qkv,
    w_in,
    inward,
    outward,
    shifts,
    query_gain,
    key_gain,
    bias,
    member,
    start,
    sums,
    parts,
    scaled_rows,
    doc_terms,
):
    times, chans, tokens = low.shape
    wide, head = terms.shape[2], w_qkv.shape[2]
    count = docs.shape[1]
    documents = jnp.concatenate([docs[i].astype(F32) for i in range(docs.shape[0])], axis=1)

    def embed(pair, carry):
        whole, scaled = [], []
        for j in range(2):
            t = pair * 2 + j
            row = centre(documents + terms[t, 0:1, :])
            whole.append(row)
            scaled.append(row * (1.0 + terms[t, 2:3, :]))
        both = jnp.concatenate(whole, axis=0)
        at = pl.multiple_of(pair * 2 * count, 2 * count)
        scaled_rows[pl.ds(at, 2 * count), :] = jnp.concatenate(scaled, axis=0).astype(BF16)
        high, rest = two_parts(both)
        parts[0, pl.ds(at, 2 * count), :] = high
        parts[1, pl.ds(at, 2 * count), :] = rest
        power = jnp.sum(both * both, axis=-1, keepdims=True)
        lane = lax.broadcasted_iota(jnp.int32, (2 * count, head), 1)
        doc_terms[pl.ds(at, 2 * count), 3 * head :] = jnp.where(lane == chans, power, 0.0)
        return carry

    lax.fori_loop(0, times // 2, embed, 0, unroll=2)
    for c in range(3):
        doc_terms[:, c * head : (c + 1) * head] = dot(scaled_rows[...], w_qkv[c])
    cross = dot(parts[0], w_in[...], NT) + dot(parts[1], w_in[...], NT)
    doc_terms[:, 3 * head :] += jnp.concatenate([2.0 * cross, jnp.zeros_like(cross)], axis=1)

    lane = lax.broadcasted_iota(jnp.int32, (tokens, head - chans), 1)
    unit = jnp.where(lane == 0, 1.0, 0.0).astype(F32)
    scale = head**-0.5

    def one_time(t, total):
        sums[t] = total.astype(BF16)
        turned = low[t].astype(F32).T
        left = turned.astype(BF16)
        left = jnp.concatenate([left, left, member[...]], axis=1)
        at = pl.multiple_of(t * count, count)
        high, rest = two_parts(doc_terms[pl.ds(at, count), :])
        here = jnp.concatenate([high.astype(F32), rest.astype(F32)], axis=0).astype(BF16)
        right = jnp.concatenate([inward[t], here], axis=0)
        mixed = dot(left, right)
        spread = jnp.sum(
            mixed[:, 3 * head :] * jnp.concatenate([turned, unit], axis=1), axis=-1, keepdims=True
        )
        projected = mixed[:, : 3 * head] * lax.rsqrt(spread / wide + EPS) + shifts[pl.ds(t, 1), :]

        def normal(values, gains):
            power = jnp.mean(values * values, axis=-1, keepdims=True)
            return (values * lax.rsqrt(power + EPS) * gains).astype(BF16)

        queries = normal(projected[:, :head], query_gain[...])
        keys = normal(projected[:, head : 2 * head], key_gain[...])
        values = projected[:, 2 * head :].astype(BF16)
        scores = dot(queries, keys, NT) * scale + bias[...]
        raised = jnp.exp(scores - jnp.max(scores, axis=-1, keepdims=True))
        weights = (raised / jnp.sum(raised, axis=-1, keepdims=True)).astype(BF16)
        attended = dot(weights, values).astype(BF16)
        return total + dot(outward[t], attended, NT)

    def several(step, total):
        for j in range(4):
            total = one_time(step * 4 + j, total)
        return total

    lax.fori_loop(0, times // 4, several, start[...])


def residual_kernel(weights, low, docs, terms, w_in, w_final, member, out):
    times = low.shape[0]
    documents = jnp.concatenate([docs[i].astype(F32) for i in range(docs.shape[0])], axis=1)
    mixed = jnp.zeros(low.shape[1:], F32)
    embedded = jnp.zeros((1, terms.shape[2]), F32)
    whole = 0.0
    for t in range(times):
        mixed = mixed + weights[t] * low[t].astype(F32)
        embedded = embedded + weights[t] * terms[t, 0:1, :]
        whole = whole + weights[t]
    rows = embedded + whole * documents
    high = rows.astype(BF16)
    middle, rest = two_parts(rows - high.astype(F32))
    rows = jnp.concatenate(
        [high.astype(F32), middle.astype(F32), rest.astype(F32)], axis=0
    ).astype(BF16)
    narrow = dot(w_final[...], rows, NT)
    count = docs.shape[1]
    narrow = narrow[:, :count] + narrow[:, count : 2 * count] + narrow[:, 2 * count :]
    direct = dot(w_final[...], w_in[...], NT)
    chosen = dot(narrow, member[:, :count].astype(F32), NT, HIGHEST)
    out[...] = dot(direct, mixed, NN, HIGHEST) + chosen


def fold_weights(steps, w_in, terms, w_qkv, w_final, w_proj):
    times, wide, head, chans = terms.shape[0], terms.shape[2], w_proj.shape[0], w_in.shape[0]
    return pl.pallas_call(
        weights_kernel,
        out_shape=(
            jax.ShapeDtypeStruct((times, 2 * chans, 4 * head), BF16),
            jax.ShapeDtypeStruct((times, 3 * head), F32),
            jax.ShapeDtypeStruct((times, chans, head), BF16),
        ),
        in_specs=[SMEM] + [VMEM] * 5,
        out_specs=(VMEM, VMEM, VMEM),
        scratch_shapes=[
            pltpu.VMEM((chans, wide), F32),
            pltpu.VMEM((4 * chans, wide), BF16),
            pltpu.VMEM((times, wide), F32),
        ],
        compiler_params=PARAMS,
        name="fold_weights",
    )(steps, w_in, terms, w_qkv, w_final, w_proj)


def run_heads(low, docs, terms, w_qkv, *rest):
    rows = terms.shape[0] * docs.shape[1]
    wide, head = terms.shape[2], w_qkv.shape[2]
    return pl.pallas_call(
        heads_kernel,
        out_shape=jax.ShapeDtypeStruct(low.shape, BF16),
        in_specs=[VMEM] * 13,
        out_specs=VMEM,
        scratch_shapes=[
            pltpu.VMEM((2, rows, wide), BF16),
            pltpu.VMEM((rows, wide), BF16),
            pltpu.VMEM((rows, 4 * head), F32),
        ],
        compiler_params=PARAMS,
        name="run_heads",
    )(low, docs, terms, w_qkv, *rest)


def residual(weights, low, *rest):
    return pl.pallas_call(
        residual_kernel,
        out_shape=jax.ShapeDtypeStruct(low.shape[1:], F32),
        in_specs=[SMEM] + [VMEM] * 6,
        out_specs=VMEM,
        compiler_params=PARAMS,
        name="residual",
    )(weights, low, *rest)


def to_all(part, axis, size):
    copies = jnp.broadcast_to(part[None], (size,) + part.shape)
    return lax.all_to_all(copies, axis, 0, 0)


def local(
    latents,
    time_terms,
    step_sizes,
    doc_embed,
    pack_docs,
    segment_ids,
    w_in,
    w_qkv,
    query_gain,
    key_gain,
    w_proj,
    w_final,
):
    here = lax.axis_index("tm")
    times, owners = lax.axis_size("tm"), lax.axis_size("req")
    count, piece = doc_embed.shape
    lowered = latents[0].astype(BF16)
    w_heads = w_qkv[:, :, 0, :].transpose(1, 0, 2)
    w_last = w_final.T

    low = to_all(lowered, "tm", times)
    table = to_all(doc_embed, "req", owners).reshape(owners * count, piece)
    wanted = jnp.broadcast_to(pack_docs[None, :], (times, count)).reshape(-1)
    places = jnp.arange(owners * count, dtype=jnp.int32)
    pick = (wanted[:, None] == places[None, :]).astype(BF16)
    chosen = dot(pick, table).astype(BF16).reshape(times, count, piece)
    docs = lax.all_to_all(chosen, "tm", 0, 0)

    inward, shifts, outward = fold_weights(step_sizes, w_in, time_terms, w_heads, w_last, w_proj[0])
    segments = segment_ids[0]
    member = (segments[:, None] == jnp.arange(count, dtype=jnp.int32)[None, :]).astype(BF16)
    member = jnp.concatenate([member, member], axis=1)
    bias = jnp.where(segments[:, None] == segments[None, :], 0.0, MASKED).astype(F32)
    start = jnp.where(here == 0, latents[0] - lowered.astype(F32), 0.0)
    sums = run_heads(
        low,
        docs,
        time_terms,
        w_heads,
        w_in,
        inward,
        outward,
        shifts,
        query_gain,
        key_gain,
        bias,
        member,
        start,
    )
    arrived = lax.all_to_all(sums, "tm", 0, 0)
    weights = jnp.where(jnp.arange(times) < here, step_sizes, 0.0)
    direct = residual(weights, low, docs, time_terms, w_in, w_last, member)
    before = low[0].astype(F32) + direct + jnp.sum(arrived.astype(F32), axis=0)
    return jnp.where(here == 0, latents[0], before)[None]


def solution(mesh):
    in_specs = (
        P("tm", None, "req"),
        P(),
        P(),
        P("req", "tm"),
        P("req"),
        P("req", None),
        P(),
        P(None, None, "tm", None),
        P("tm", None),
        P("tm", None),
        P("tm", None, None),
        P(),
    )
    out_specs = P("tm", None, "req")
    return jax.shard_map(local, mesh=mesh, in_specs=in_specs, out_specs=out_specs, check_vma=False)
```

time: 425 us -> 124 us (0.29)
  the two profiles are of different devices: /device:TPU:2 before, /device:TPU:32 now
where the time goes in v1:
time: 124 us; the launch traced here: 122 us
  starting transfers between devices  39.1 us (32%)
  waiting for transfers between devices  32 us (26%)
  Pallas kernels  29.4 us (24%)
  local copies, waits for them, and re-layouts  17.6 us (14%)
  other arithmetic  4.04 us (3%)
    pallas_call x1, Pallas kernels, run_heads(): pl.pallas_call(heads_kernel, out_shape=jax.ShapeDtypeStruct(low.shape, BF...  17.4 us
    all_to_all x1, starting transfers between devices, local(): docs = lax.all_to_all(chosen, 'tm', 0, 0)  15.2 us
    unnamed x52, local copies, waits for them, and re-layouts  13.8 us
    all_to_all x1, waiting for transfers between devices, local(): arrived = lax.all_to_all(sums, 'tm', 0, 0)  13.6 us
    all_to_all x1, starting transfers between devices, local(): arrived = lax.all_to_all(sums, 'tm', 0, 0)  12.2 us
    all_to_all x2, starting transfers between devices, to_all(): return lax.all_to_all(copies, axis, 0, 0)  11.7 us
    all_to_all x1, waiting for transfers between devices, local(): docs = lax.all_to_all(chosen, 'tm', 0, 0)  11.3 us
    pallas_call x1, Pallas kernels, fold_weights(): pl.pallas_call(weights_kernel, out_shape=(jax.ShapeDtypeStruct((times, 2...  10.7 us
  transfers between devices with their start and end apart: 4, of which 3 were waited for; matrix products, arithmetic and copies ran while one was open for 3% of the time, Pallas kernels for 10%

profile of v1, /device:TPU:32, one launch (start us, length us, event | category | flops | bytes accessed | tf_op | source)
XLA Modules:
  0.0 122.5 jit_solution(16323749571179632554)
XLA Ops:
  0.0 1.3 %broadcast_in_dim.45 = bf16[32,8,192]{2,1,0:T(8,128)(2,1)} broadcast(bf16[8,192]{1,0:T(8,128)(2,1)} %param.15), dimensions={1,2} | broadcast | bytes 101376 | tf_op jit(solution)/shard_map/broadcast_in_dim | solution.py:238
  1.3 7.3 %all-to-all-start.1 = ((bf16[32,8,192]{2,1,0:T(8,128)(2,1)}), bf16[32,8,192]{2,1,0:T(8,128)(2,1)S(1)}, u32[]{:S(2)}, u32[]{:S(2)}) async-start(bf16[32,8,192]{2,1,0:T(8,128)(2,1)} %broadcast_in_dim.45), calls=%async_computation.1 | async-start | bytes 262144 | tf_op jit(solution)/shard_map/all_to_all | solution.py:239
  8.7 0.7 broadcast_in_dim.44
  9.3 0.1 eq.48
  9.4 7.0 %all-to-all-done.1 = bf16[32,8,192]{2,1,0:T(8,128)(2,1)S(1)} async-done(((bf16[32,8,192]{2,1,0:T(8,128)(2,1)}), bf16[32,8,192]{2,1,0:T(8,128)(2,1)S(1)}, u32[]{:S(2)}, u32[]{:S(2)}) %all-to-all-start.1) | async-done | bytes 98336 | tf_op jit(solution)/shard_map/all_to_all | solution.py:239
  16.5 0.3 convolution_convert_fusion
  16.7 0.8 copy.15
  17.5 15.2 %all-to-all-start.2 = ((bf16[16,8,192]{2,1,0:T(8,128)(2,1)}), bf16[16,8,192]{2,1,0:T(8,128)(2,1)S(1)}, u32[]{:S(2)}, u32[]{:S(2)}) async-start(bf16[16,8,192]{2,1,0:T(8,128)(2,1)} %bitcast.4), calls=%async_computation.2 | async-start | bytes 131072 | tf_op jit(solution)/shard_map/all_to_all | solution.py:269
  32.7 0.8 convert_bitcast_fusion
  33.5 11.3 %all-to-all-done.2.docs = bf16[16,8,192]{2,1,0:T(8,128)(2,1)S(1)} async-done(((bf16[16,8,192]{2,1,0:T(8,128)(2,1)}), bf16[16,8,192]{2,1,0:T(8,128)(2,1)S(1)}, u32[]{:S(2)}, u32[]{:S(2)}) %all-to-all-start.2) | async-done | bytes 49184 | tf_op jit(solution)/shard_map/all_to_all | solution.py:269
  44.8 0.0 copy-start.8
  44.8 0.8 broadcast_in_dim.42
  45.5 0.0 copy-done.8
  45.6 4.4 %all-to-all-start = ((bf16[16,64,128]{2,1,0:T(8,128)(2,1)}), bf16[16,64,128]{2,1,0:T(8,128)(2,1)S(1)}, u32[]{:S(2)}, u32[]{:S(2)}) async-start(bf16[16,64,128]{2,1,0:T(8,128)(2,1)} %broadcast_in_dim.42), calls=%async_computation | async-start | bytes 524288 | tf_op jit(solution)/shard_map/all_to_all | solution.py:239
  49.9 0.7 iota_compare_fusion.2
  50.6 0.1 copy.16
  50.7 0.6 concatenate.6.member
  51.3 0.0 copy-start
  51.3 1.1 copy-done
  52.5 0.0 copy-start.2
  52.5 1.0 copy-done.2
  53.5 0.0 copy-start.4
  53.5 1.0 copy-done.4
  54.5 0.0 copy-start.7
  54.5 1.1 copy-done.7
  55.6 0.0 copy-start.21
  55.6 0.7 copy-done.21
  56.3 0.0 copy-start.23
  56.3 0.0 copy-start.25
  56.3 0.0 copy-start.1
  56.3 0.0 copy-start.19
  56.3 0.0 copy-start.20
  56.3 10.7 %fold_weights.1 = (bf16[16,128,512]{2,1,0:T(8,128)(2,1)S(1)}, f32[16,384]{1,0:T(8,128)S(1)}, bf16[16,64,128]{2,1,0:T(8,128)(2,1)S(1)}) custom-call(f32[16]{0:T(128)S(1)} %copy-done.21, bf16[64,3072]{1,0:T(8,128)(2,1)S(1)} %copy-done.2, f32[16,4,3072]{2,1,0:T(4,128)S(1)} %copy-done, bf16[3,3072,128]{2,1,0:T(8,128)(2,1)} %bitcast.30, ...), custom_call_target="tpu_custom_call" | custom-call | tf_op jit(solution)/shard_map/fold_weights/pallas_call | solution.py:189
  67.0 0.0 copy-start.14
  67.0 0.7 copy-done.14
  67.7 0.0 copy-done.23
  67.7 0.6 fusion.5.start
  68.3 0.0 copy-done.17
  68.3 0.0 copy-done.25
  68.3 0.7 compare_select_fusion.bias
  69.0 0.0 all-to-all-done.low
  69.0 0.0 copy-done.1
  69.0 0.0 copy-done.3
  69.0 0.0 copy-done.19
  69.1 0.0 copy-done.20
  69.1 0.0 copy-start.9
  69.1 0.8 copy-done.9
  69.9 0.8 copy-done.11
  70.7 0.8 copy-done.13
  71.5 0.9 copy-done.15
  72.5 0.8 copy-done.16
  73.2 0.7 copy-done.18
  74.0 17.4 %run_heads.1 = bf16[16,64,128]{2,1,0:T(8,128)(2,1)S(1)} custom-call(bf16[16,64,128]{2,1,0:T(8,128)(2,1)S(1)} %all-to-all-done.low, bf16[16,8,192]{2,1,0:T(8,128)(2,1)S(1)} %copy-done.9, f32[16,4,3072]{2,1,0:T(4,128)S(1)} %copy-done.1, bf16[3,3072,128]{2,1,0:T(8,128)(2,1)} %bitcast.31, bf16[64,3072]{1,0:T(8,128)(2,1)S(1)} %copy-done.3, ...), custom_call_target="tpu_custom_call" | custom-call | tf_op jit(solution)/shard_map/run_heads/pallas_call | solution.py:211
  91.4 0.7 copy-done.6
  92.1 12.2 %all-to-all-start.3 = ((bf16[16,64,128]{2,1,0:T(8,128)(2,1)}), bf16[16,64,128]{2,1,0:T(8,128)(2,1)S(1)}, u32[]{:S(2)}, u32[]{:S(2)}) async-start(bf16[16,64,128]{2,1,0:T(8,128)(2,1)} %copy-done.6), calls=%async_computation.3 | async-start | bytes 524288 | tf_op jit(solution)/shard_map/all_to_all | solution.py:292
  104.3 0.0 copy-done.22
  104.3 0.0 copy-start.5
  104.3 1.0 copy-done.5
  105.3 0.8 copy-done.10
  106.1 0.8 copy-done.12
  106.9 1.2 %residual.1 = f32[64,128]{1,0:T(8,128)S(1)} custom-call(f32[16]{0:T(128)S(1)} %compare_select_fusion.1.weights, bf16[16,64,128]{2,1,0:T(8,128)(2,1)S(1)} %all-to-all-done.low, bf16[16,8,192]{2,1,0:T(8,128)(2,1)S(1)} %copy-done.10, f32[16,4,3072]{2,1,0:T(4,128)S(1)} %copy-done.1, bf16[64,3072]{1,0:T(8,128)(2,1)S(1)} %copy-done.3, ...), custom_call_target="tpu_custom_call" | custom-call | tf_op jit(solution)/shard_map/residual/pallas_call | solution.py:227
  108.2 13.6 %all-to-all-done.3 = bf16[16,64,128]{2,1,0:T(8,128)(2,1)S(1)} async-done(((bf16[16,64,128]{2,1,0:T(8,128)(2,1)}), bf16[16,64,128]{2,1,0:T(8,128)(2,1)S(1)}, u32[]{:S(2)}, u32[]{:S(2)}) %all-to-all-start.3) | async-done | bytes 262176 | tf_op jit(solution)/shard_map/all_to_all | solution.py:292
  121.8 0.0 copy-done.24
  121.8 0.6 fusion.4
  (15 shorter events, 0.1 us)
Async XLA Ops:
  1.3 15.1 %all-to-all-start.1 = ((bf16[32,8,192]{2,1,0:T(8,128)(2,1)}), bf16[32,8,192]{2,1,0:T(8,128)(2,1)S(1)}, u32[]{:S(2)}, u32[]{:S(2)}) async-start(bf16[32,8,192]{2,1,0:T(8,128)(2,1)} %broadcast_in_dim.45), calls=%async_computation.1 | async-start | bytes 262144 | tf_op jit(solution)/shard_map/all_to_all | solution.py:239
  17.5 27.3 %all-to-all-start.2 = ((bf16[16,8,192]{2,1,0:T(8,128)(2,1)}), bf16[16,8,192]{2,1,0:T(8,128)(2,1)S(1)}, u32[]{:S(2)}, u32[]{:S(2)}) async-start(bf16[16,8,192]{2,1,0:T(8,128)(2,1)} %bitcast.4), calls=%async_computation.2 | async-start | bytes 131072 | tf_op jit(solution)/shard_map/all_to_all | solution.py:269
  44.8 0.8 copy-start.8
  45.6 23.5 %all-to-all-start = ((bf16[16,64,128]{2,1,0:T(8,128)(2,1)}), bf16[16,64,128]{2,1,0:T(8,128)(2,1)S(1)}, u32[]{:S(2)}, u32[]{:S(2)}) async-start(bf16[16,64,128]{2,1,0:T(8,128)(2,1)} %broadcast_in_dim.42), calls=%async_computation | async-start | bytes 524288 | tf_op jit(solution)/shard_map/all_to_all | solution.py:239
  51.3 1.1 copy-start
  52.5 1.0 copy-start.2
  53.5 1.0 copy-start.4
  54.5 1.1 copy-start.7
  55.6 0.7 copy-start.21
  56.3 11.5 %copy-start.23 = (f32[1,64,128]{2,1,0:T(8,128)S(1)}, f32[1,64,128]{2,1,0:T(8,128)}, u32[]{:S(2)}) copy-start(f32[1,64,128]{2,1,0:T(8,128)} %param.12) | copy-start | bytes 98308
  56.3 12.1 %copy-start.25 = (s32[1,128]{1,0:T(1,128)S(1)}, s32[1,128]{1,0:T(1,128)}, u32[]{:S(2)}) copy-start(s32[1,128]{1,0:T(1,128)} %param.17) | copy-start | bytes 1540
  56.3 12.8 %copy-start.1 = (f32[16,4,3072]{2,1,0:T(4,128)S(1)}, f32[16,4,3072]{2,1,0:T(4,128)}, u32[]{:S(2)}) copy-start(f32[16,4,3072]{2,1,0:T(4,128)} %terms.5) | copy-start | bytes 2359300
  56.3 12.8 %copy-start.3 = (bf16[64,3072]{1,0:T(8,128)(2,1)S(1)}, bf16[64,3072]{1,0:T(8,128)(2,1)}, u32[]{:S(2)}) copy-start(bf16[64,3072]{1,0:T(8,128)(2,1)} %w_in.5) | copy-start | bytes 1179652
  56.3 12.8 %copy-start.19 = (f32[1,128]{1,0:T(1,128)S(1)}, f32[1,128]{1,0:T(1,128)}, u32[]{:S(2)}) copy-start(f32[1,128]{1,0:T(1,128)} %query_gain.1) | copy-start | bytes 1540
  56.3 12.8 %copy-start.20 = (f32[1,128]{1,0:T(1,128)S(1)}, f32[1,128]{1,0:T(1,128)}, u32[]{:S(2)}) copy-start(f32[1,128]{1,0:T(1,128)} %key_gain.1) | copy-start | bytes 1540
  67.0 0.7 copy-start.14
  67.7 0.6 copy-start.17
  69.1 0.8 copy-start.9
  69.9 0.8 copy-start.11
  70.7 0.8 copy-start.13
  71.5 0.9 copy-start.15
  72.5 0.8 copy-start.16
  73.2 0.7 copy-start.18
  74.0 30.3 %copy-start.22 = (f32[16]{0:T(128)S(1)}, f32[16]{0:T(128)}, u32[]{:S(2)}) copy-start(f32[16]{0:T(128)} %steps.1) | copy-start | bytes 196
  91.4 0.7 copy-start.6
  92.1 29.8 %copy-start.24 = (f32[1,64,128]{2,1,0:T(8,128)S(1)}, f32[1,64,128]{2,1,0:T(8,128)}, u32[]{:S(2)}) copy-start(f32[1,64,128]{2,1,0:T(8,128)} %param.12) | copy-start | bytes 98308
  92.1 29.7 %all-to-all-start.3 = ((bf16[16,64,128]{2,1,0:T(8,128)(2,1)}), bf16[16,64,128]{2,1,0:T(8,128)(2,1)S(1)}, u32[]{:S(2)}, u32[]{:S(2)}) async-start(bf16[16,64,128]{2,1,0:T(8,128)(2,1)} %copy-done.6), calls=%async_computation.3 | async-start | bytes 524288 | tf_op jit(solution)/shard_map/all_to_all | solution.py:292
  104.3 1.0 copy-start.5
  105.3 0.8 copy-start.10
  106.1 0.8 copy-start.12

commit v2 on v0

v2 whole, which is shorter than its diff:
```python
import jax
import jax.numpy as jnp
from jax import lax
from jax.experimental import pallas as pl
from jax.experimental.pallas import tpu as pltpu
from jax.sharding import PartitionSpec as P

EPS = 1e-06
MASKED = -1e30
LOG2E = 1.4426950408889634
BF16, F32 = jnp.bfloat16, jnp.float32
NN = (((1,), (0,)), ((), ()))
NT = (((1,), (1,)), ((), ()))
VMEM = pl.BlockSpec(memory_space=pltpu.VMEM)
SMEM = pl.BlockSpec(memory_space=pltpu.SMEM)
HBM = pl.BlockSpec(memory_space=pltpu.HBM)
PARAMS = pltpu.CompilerParams(vmem_limit_bytes=24 * 2**20)


def dot(left, right, dims=NN, precision=None):
    return lax.dot_general(left, right, dims, precision=precision, preferred_element_type=F32)


def two_parts(values):
    high = values.astype(BF16)
    return high, (values - high.astype(F32)).astype(BF16)


def stack_rows(*parts):
    return jnp.concatenate([p.astype(F32) for p in parts], axis=0).astype(BF16)


def centre(values):
    return values - jnp.mean(values, axis=-1, keepdims=True)


def fetch(pairs, sems):
    copies = [pltpu.make_async_copy(a, b, sems.at[i]) for i, (a, b) in enumerate(pairs)]
    for copy in copies:
        copy.start()
    return copies


def inward_kernel(
    w_in, terms, latents, pack_docs, w_qkv,
    inward, pieces, pick, lowered, rest,
    w_in_v, terms_v, latents_v, packs_v, centred, rows, sems,
):
    chans, wide = w_in_v.shape
    times = terms_v.shape[0]
    head = w_qkv.shape[2]
    copies = fetch(
        [(w_in, w_in_v), (terms, terms_v), (latents, latents_v), (pack_docs, packs_v)], sems
    )
    copies[0].wait()
    centred[...] = centre(w_in_v[...].astype(F32))
    high, low = two_parts(centred[...])
    pieces[:chans, :] = high
    pieces[chans:, :] = low
    copies[1].wait()
    for step in range(times // 4):
        for j in range(4):
            scaled = centred[...] * (1.0 + terms_v[step * 4 + j, 2:3, :])
            rows[step % 2, j * chans : (j + 1) * chans, :] = scaled.astype(BF16)
        for c in range(3):
            turned = dot(rows[step % 2], w_qkv[c]).T.astype(BF16)
            span = slice(c * head, (c + 1) * head)
            inward[2 * step, span, :] = turned[:, : 2 * chans]
            inward[2 * step + 1, span, :] = turned[:, 2 * chans :]
    copies[2].wait()
    values = latents_v[0]
    lowered[...] = values.astype(BF16)
    rest[...] = values - values.astype(BF16).astype(F32)
    copies[3].wait()
    count = packs_v.shape[1]
    column = jnp.broadcast_to(packs_v[...].astype(F32), (count, count))
    eye = lax.broadcasted_iota(jnp.int32, (count, count), 0) == lax.broadcasted_iota(
        jnp.int32, (count, count), 1
    )
    column = jnp.sum(jnp.where(eye, column, 0.0), axis=1, keepdims=True)
    places = lax.broadcasted_iota(jnp.int32, (count, pick.shape[1]), 1).astype(F32)
    chosen = jnp.where(places == column, 1.0, 0.0)
    pick[...] = stack_rows(chosen, jnp.zeros_like(chosen))


def select_kernel(table, pick, lowered, out, staged, sems):
    size, rows, lanes = out.shape
    chans = lowered.shape[0]
    owners, count, piece = table.shape
    flat = table[...].reshape(owners * count, piece)
    chosen = dot(pick[...], flat)[:count]
    tail = jnp.concatenate(
        [chosen[:, lanes:], jnp.zeros((count, 2 * lanes - piece), F32)], axis=1
    )
    staged[:chans, :] = lowered[...]
    staged[chans:, :] = stack_rows(chosen[:, :lanes], tail)
    copies = fetch([(staged, out.at[i]) for i in range(size)], sems)
    for copy in copies:
        copy.wait()


def outward_kernel(
    steps, terms, w_final, w_proj, query_gain, key_gain, segments, sent, pieces, w_qkv,
    outward, shifts, gram, cross, embedded, scales, gains, bias, member,
    terms_v, w_final_v, w_proj_v, gains_v, segments_v, rows, sems,
):
    del sent
    times, chans, head = outward.shape
    copies = fetch(
        [
            (terms, terms_v), (w_final, w_final_v), (w_proj, w_proj_v),
            (query_gain, gains_v.at[0]), (key_gain, gains_v.at[1]), (segments, segments_v),
        ],
        sems,
    )
    both = pieces[...]
    square = dot(both, both, NT)
    square = square[:chans, :chans] + square[chans:, :chans] + square[:chans, chans:]
    high, low = two_parts(square)
    gram[:chans, :] = high
    gram[chans:, :] = low
    copies[0].wait()
    moved, means = [], []
    for t in range(times):
        moved.append(terms_v[t, 1:2, :])
        means.append(centre(terms_v[t, 0:1, :]))
        scales[t : t + 1, :] = 1.0 + terms_v[t, 2:3, :]
    moved, means = jnp.concatenate(moved, axis=0), jnp.concatenate(means, axis=0)
    embedded[...] = means
    high, low = two_parts(moved)
    split = stack_rows(high, low)
    for c in range(3):
        shift = dot(split, w_qkv[c])
        shifts[:, c * head : (c + 1) * head] = shift[:times] + shift[times:]
    high, low = two_parts(means)
    mixed = dot(stack_rows(high, low), both, NT)
    cross[...] = mixed[:times, :chans] + mixed[times:, :chans] + mixed[:times, chans:]
    copies[1].wait()
    copies[2].wait()
    for step in range(times // 4):
        for j in range(4):
            gated = w_final_v[...].astype(F32) * terms_v[step * 4 + j, 3:4, :]
            rows[step % 2, j * chans : (j + 1) * chans, :] = gated.astype(BF16)
        back = dot(rows[step % 2], w_proj_v[...], NT)
        for j in range(4):
            t = step * 4 + j
            outward[t] = (back[j * chans : (j + 1) * chans] * steps[t]).astype(BF16)
    copies[3].wait()
    copies[4].wait()
    copies[5].wait()
    tokens = segments_v.shape[1]
    gains[0] = jnp.broadcast_to(gains_v[0] * (head**-0.5 * LOG2E), (head, head)).T
    gains[1] = jnp.broadcast_to(gains_v[1], (head, head)).T
    ids = jnp.broadcast_to(segments_v[...].astype(F32), (tokens, tokens))
    bias[...] = jnp.where(ids == ids.T, 0.0, MASKED)
    count = member.shape[0]
    numbers = lax.broadcasted_iota(jnp.int32, (count, tokens), 0).astype(F32)
    member[...] = jnp.where(numbers == ids[:count], 1.0, 0.0)


def gather_documents(arrived, chans, count, piece):
    parts = []
    for i in range(arrived.shape[0]):
        block = arrived[i, chans:, :].astype(F32)
        parts.append(block[:count])
        parts.append(block[count:, : piece - block.shape[1]])
    return jnp.concatenate(parts, axis=1)


def heads_kernel(
    here, arrived, w_qkv, inward, outward, shifts, gram, cross, pieces, embedded, scales, gains,
    bias, member, rest,
    out,
    rows, staged, sems,
):
    times, chans, head = outward.shape
    count, tokens = member.shape
    wide = pieces.shape[1]
    documents = gather_documents(arrived, chans, count, wide // times)
    near = dot(documents.astype(BF16), pieces[:chans, :], NT) + dot(
        documents.astype(BF16), pieces[chans:, :], NT
    )
    documents = centre(documents)
    powers = []
    for t in range(0, times, 2):
        pair = []
        for j in range(2):
            row = documents + embedded[t + j : t + j + 1, :]
            powers.append(jnp.sum(row * row, axis=-1, keepdims=True))
            pair.append(row * scales[t + j : t + j + 1, :])
        rows[t * count : (t + 2) * count, :] = jnp.concatenate(pair, axis=0).astype(BF16)
    base = jnp.concatenate([dot(rows[...], w_qkv[c]) for c in range(3)], axis=1)
    turned = []
    for half in range(2):
        span = slice(half * 8 * count, (half + 1) * 8 * count)
        block = [base[span], shifts[half * 8 : (half + 1) * 8, :]]
        left = head - 8 * count - 8
        block.append(jnp.zeros((left, 3 * head), F32))
        turned.append(jnp.concatenate(block, axis=0).T.astype(BF16))

    belongs = member[...]
    scaled_low, rates = [], []
    for t in range(times):
        mixed = 2.0 * (near + cross[t : t + 1, :])
        high, low = two_parts(mixed)
        left = jnp.concatenate([gram[...], stack_rows(high, low)], axis=0)
        values = arrived[t, :chans, :]
        whole = dot(left, values)
        both = whole[:chans] + whole[chans : 2 * chans]
        values = values.astype(F32)
        other = whole[2 * chans : 2 * chans + count] + whole[2 * chans + count :]
        spread = jnp.sum(both * values, axis=0, keepdims=True) + jnp.sum(
            belongs * (other + powers[t]), axis=0, keepdims=True
        )
        rate = lax.rsqrt(spread / wide + EPS)
        rates.append(rate)
        scaled_low.append((values * rate).astype(BF16))

    def unit(values, gain):
        power = jnp.mean(values * values, axis=0, keepdims=True)
        return values * lax.rsqrt(power + EPS) * gain

    total = jnp.where(here[0] == 0, rest[...], 0.0)
    empty = jnp.zeros((chans, tokens), BF16)
    for t in range(times):
        staged[t] = total.astype(BF16)
        half, j = divmod(t, 8)
        left = jnp.concatenate([inward[t // 2], turned[half]], axis=1)
        first = [scaled_low[t], empty] if t % 2 == 0 else [empty, scaled_low[t]]
        ones = lax.broadcasted_iota(jnp.int32, (8, tokens), 0) == j
        second = [jnp.zeros((j * count, tokens), F32)] if j else []
        second.append(belongs * rates[t])
        if j < 7:
            second.append(jnp.zeros(((7 - j) * count, tokens), F32))
        second.append(jnp.where(ones, 1.0, 0.0))
        second.append(jnp.zeros((head - 8 * count - 8, tokens), F32))
        second = jnp.concatenate(second, axis=0).astype(BF16)
        projected = dot(left, jnp.concatenate(first + [second], axis=0))
        queries = unit(projected[:head], gains[0]).astype(BF16)
        keys = unit(projected[head : 2 * head], gains[1]).T.astype(BF16)
        values = projected[2 * head :].astype(BF16)
        scores = dot(keys, queries) + bias[...]
        raised = jnp.exp2(scores - jnp.max(scores, axis=0, keepdims=True))
        mass = jnp.sum(raised, axis=0, keepdims=True)
        attended = (dot(values, raised.astype(BF16)) * (1.0 / mass)).astype(BF16)
        total = total + dot(outward[t], attended)
    copies = fetch([(staged, out)], sems)
    copies[0].wait()


def residual_kernel(
    here, steps, arrived, terms, w_in, w_final, member, sums,
    out,
    terms_v, w_in_v, w_final_v, sems,
):
    del sums
    times = terms_v.shape[0]
    chans, wide = w_in_v.shape
    count = member.shape[0]
    copies = fetch([(terms, terms_v), (w_in, w_in_v), (w_final, w_final_v)], sems)
    documents = gather_documents(arrived, chans, count, wide // times)
    mixed = jnp.zeros(out.shape, F32)
    weights, whole = [], 0.0
    for t in range(times):
        weights.append(jnp.where(t < here[0], steps[t], 0.0))
        mixed = mixed + weights[t] * arrived[t, :chans, :].astype(F32)
        whole = whole + weights[t]
    copies[0].wait()
    embedded = jnp.zeros((1, wide), F32)
    for t in range(times):
        embedded = embedded + weights[t] * terms_v[t, 0:1, :]
    rows = embedded + whole * documents
    high = rows.astype(BF16)
    middle, low = two_parts(rows - high.astype(F32))
    copies[1].wait()
    copies[2].wait()
    final = w_final_v[...]
    narrow = dot(final, high, NT) + dot(final, middle, NT) + dot(final, low, NT)
    direct = dot(final, w_in_v[...], NT)
    highest = lax.Precision.HIGHEST
    near = dot(direct, mixed, NN, highest) + dot(narrow, member[...], NN, highest)
    out[...] = near + arrived[0, :chans, :].astype(F32)


def fold_inward(w_in, terms, latents, pack_docs, w_qkv, documents):
    times, (chans, wide), head = terms.shape[0], w_in.shape, w_qkv.shape[2]
    return pl.pallas_call(
        inward_kernel,
        out_shape=(
            jax.ShapeDtypeStruct((times // 2, 3 * head, 2 * chans), BF16),
            jax.ShapeDtypeStruct((2 * chans, wide), BF16),
            jax.ShapeDtypeStruct((2 * pack_docs.shape[1], documents), BF16),
            jax.ShapeDtypeStruct(latents.shape[1:], BF16),
            jax.ShapeDtypeStruct(latents.shape[1:], F32),
        ),
        in_specs=[HBM, HBM, HBM, HBM, VMEM],
        out_specs=(VMEM,) * 5,
        scratch_shapes=[
            pltpu.VMEM(w_in.shape, BF16),
            pltpu.VMEM(terms.shape, F32),
            pltpu.VMEM(latents.shape, F32),
            pltpu.VMEM(pack_docs.shape, jnp.int32),
            pltpu.VMEM(w_in.shape, F32),
            pltpu.VMEM((2, 4 * chans, wide), BF16),
            pltpu.SemaphoreType.DMA((4,)),
        ],
        compiler_params=PARAMS,
        name="fold_inward",
    )(w_in, terms, latents, pack_docs, w_qkv)


def select(table, pick, lowered, size):
    rows = lowered.shape[0] + pick.shape[0]
    block = (rows, lowered.shape[1])
    return pl.pallas_call(
        select_kernel,
        out_shape=jax.ShapeDtypeStruct((size,) + block, BF16),
        in_specs=[VMEM] * 3,
        out_specs=HBM,
        scratch_shapes=[pltpu.VMEM(block, BF16), pltpu.SemaphoreType.DMA((size,))],
        compiler_params=PARAMS,
        name="select",
    )(table, pick, lowered)


def fold_outward(
    steps, terms, w_final, w_proj, query_gain, key_gain, segments, sent, pieces, w_qkv, count
):
    times, wide = terms.shape[0], terms.shape[2]
    chans, head, tokens = w_final.shape[0], w_proj.shape[0], segments.shape[1]
    return pl.pallas_call(
        outward_kernel,
        out_shape=(
            jax.ShapeDtypeStruct((times, chans, head), BF16),
            jax.ShapeDtypeStruct((times, 3 * head), F32),
            jax.ShapeDtypeStruct((2 * chans, chans), BF16),
            jax.ShapeDtypeStruct((times, chans), F32),
            jax.ShapeDtypeStruct((times, wide), F32),
            jax.ShapeDtypeStruct((times, wide), F32),
            jax.ShapeDtypeStruct((2, head, head), F32),
            jax.ShapeDtypeStruct((tokens, tokens), F32),
            jax.ShapeDtypeStruct((count, tokens), F32),
        ),
        in_specs=[SMEM] + [HBM] * 7 + [VMEM] * 2,
        out_specs=(VMEM,) * 9,
        scratch_shapes=[
            pltpu.VMEM(terms.shape, F32),
            pltpu.VMEM(w_final.shape, BF16),
            pltpu.VMEM(w_proj.shape, BF16),
            pltpu.VMEM((2,) + query_gain.shape, F32),
            pltpu.VMEM(segments.shape, jnp.int32),
            pltpu.VMEM((2, 4 * chans, wide), BF16),
            pltpu.SemaphoreType.DMA((6,)),
        ],
        compiler_params=PARAMS,
        name="fold_outward",
    )(steps, terms, w_final, w_proj, query_gain, key_gain, segments, sent, pieces, w_qkv)


def run_heads(here, arrived, w_qkv, inward, outward, shifts, gram, cross, pieces, embedded, *rest):
    rows = arrived.shape[0] * (arrived.shape[1] - outward.shape[1]) // 2
    return pl.pallas_call(
        heads_kernel,
        out_shape=jax.ShapeDtypeStruct(outward.shape, BF16),
        in_specs=[SMEM] + [VMEM] * 14,
        out_specs=HBM,
        scratch_shapes=[
            pltpu.VMEM((rows, embedded.shape[1]), BF16),
            pltpu.VMEM(outward.shape, BF16),
            pltpu.SemaphoreType.DMA((1,)),
        ],
        compiler_params=PARAMS,
        name="run_heads",
    )(here, arrived, w_qkv, inward, outward, shifts, gram, cross, pieces, embedded, *rest)


def residual(here, steps, arrived, terms, w_in, w_final, member, sums):
    return pl.pallas_call(
        residual_kernel,
        out_shape=jax.ShapeDtypeStruct(sums.shape[1:], F32),
        in_specs=[SMEM] * 2 + [VMEM, HBM, HBM, HBM, VMEM, HBM],
        out_specs=VMEM,
        scratch_shapes=[
            pltpu.VMEM(terms.shape, F32),
            pltpu.VMEM(w_in.shape, BF16),
            pltpu.VMEM(w_final.shape, BF16),
            pltpu.SemaphoreType.DMA((3,)),
        ],
        compiler_params=PARAMS,
        name="residual",
    )(here, steps, arrived, terms, w_in, w_final, member, sums)


def local(
    latents,
    time_terms,
    step_sizes,
    doc_embed,
    pack_docs,
    segment_ids,
    w_in,
    w_qkv,
    query_gain,
    key_gain,
    w_proj,
    w_final,
):
    here = lax.axis_index("tm")
    place = here.astype(jnp.int32).reshape(1)
    times, owners = lax.axis_size("tm"), lax.axis_size("req")
    count, piece = doc_embed.shape
    w_heads = w_qkv[:, :, 0, :].transpose(1, 0, 2)
    w_last = w_final.T

    copies = jnp.broadcast_to(doc_embed[None], (owners, count, piece))
    table = lax.all_to_all(copies, "req", 0, 0)
    inward, pieces, pick, lowered, rest = fold_inward(
        w_in, time_terms, latents, pack_docs[None], w_heads, owners * count
    )
    sent = select(table, pick, lowered, times)
    arrived = lax.all_to_all(sent, "tm", 0, 0)
    outward, shifts, gram, cross, embedded, scales, gains, bias, member = fold_outward(
        step_sizes, time_terms, w_last, w_proj[0], query_gain, key_gain, segment_ids, sent,
        pieces, w_heads, count,
    )
    sums = run_heads(
        place, arrived, w_heads, inward, outward, shifts, gram, cross, pieces, embedded, scales,
        gains, bias, member, rest,
    )
    parts = lax.all_to_all(sums, "tm", 0, 0)
    direct = residual(place, step_sizes, arrived, time_terms, w_in, w_last, member, sums)
    before = direct + jnp.sum(parts.astype(F32), axis=0)
    return jnp.where(here == 0, latents[0], before)[None]


def solution(mesh):
    in_specs = (
        P("tm", None, "req"),
        P(),
        P(),
        P("req", "tm"),
        P("req"),
        P("req", None),
        P(),
        P(None, None, "tm", None),
        P("tm", None),
        P("tm", None),
        P("tm", None, None),
        P(),
    )
    out_specs = P("tm", None, "req")
    return jax.shard_map(local, mesh=mesh, in_specs=in_specs, out_specs=out_specs, check_vma=False)
```

time: 425 us -> 106 us (0.25)
  waiting for transfers between devices: 262 us -> 20.7 us
  blocking collectives: 66.4 us -> 0 us
  matrix products: 53.4 us -> 0 us
  starting transfers between devices: 0.09 us -> 28.9 us
  Pallas kernels: 0 us -> 24.3 us
  between operations: 13.3 us -> 0.19 us
  local copies, waits for them, and re-layouts: 22.9 us -> 30 us
    all_gather x2 -> x0, waiting for transfers between devices: 195 us -> none  [the longest x1 146 us: local(): lax.all_gather(own_normed[None], 'tm', axis=0, tiled=True)]
    all_gather x2 -> x0, blocking collectives: 66.4 us -> none  [the longest x1 36.1 us: local(): columns = lax.all_gather(doc_embed, 'tm', axis=1, tiled=True)]
    reduce_scatter x1 -> x0, waiting for transfers between devices: 66.3 us -> none  [local(): lax.psum_scatter(parts.astype(jnp.bfloat16), 'tm', scatter_dimension=0, t...]
    dot_general x22 -> x0, matrix products: 53.4 us -> none  [the longest x16 34.1 us: project(): jnp.einsum('dc,hqd->cq', w_final, outer, preferred_element_type=jnp.float32)]
    all_to_all x0 -> x3, starting transfers between devices: none -> 28.9 us  [the longest x1 13.4 us: local(): arrived = lax.all_to_all(sent, 'tm', 0, 0)]
    unnamed x24 -> x74, local copies, waits for them, and re-layouts: 4.28 us -> 28.6 us
    pallas_call x0 -> x5, Pallas kernels: none -> 24.3 us  [the longest x1 10.6 us: run_heads(): pl.pallas_call(heads_kernel, out_shape=jax.ShapeDtypeStruct(outward.shape...]
    all_to_all x0 -> x3, waiting for transfers between devices: none -> 20.7 us  [the longest x1 13.4 us: local(): parts = lax.all_to_all(sums, 'tm', 0, 0)]
  transfers between devices with their start and end apart: 3 -> 3, of which waited for: 3 -> 2; matrix products, arithmetic and copies ran while one was open for 2% -> 0% of each run, Pallas kernels for 0% -> 12%
where the time goes in v2:
time: 106 us; the launch traced here: 105 us
  local copies, waits for them, and re-layouts  30 us (28%)
  starting transfers between devices  28.9 us (27%)
  Pallas kernels  24.3 us (23%)
  waiting for transfers between devices  20.7 us (20%)
    unnamed x74, local copies, waits for them, and re-layouts  28.6 us
    all_to_all x1, starting transfers between devices, local(): arrived = lax.all_to_all(sent, 'tm', 0, 0)  13.4 us
    all_to_all x1, waiting for transfers between devices, local(): parts = lax.all_to_all(sums, 'tm', 0, 0)  13.4 us
    pallas_call x1, Pallas kernels, run_heads(): pl.pallas_call(heads_kernel, out_shape=jax.ShapeDtypeStruct(outward.shape...  10.6 us
    all_to_all x1, starting transfers between devices, local(): table = lax.all_to_all(copies, 'req', 0, 0)  9.41 us
    all_to_all x1, waiting for transfers between devices, local(): arrived = lax.all_to_all(sent, 'tm', 0, 0)  7.32 us
    all_to_all x1, starting transfers between devices, local(): parts = lax.all_to_all(sums, 'tm', 0, 0)  6.02 us
    pallas_call x1, Pallas kernels, fold_inward(): pl.pallas_call(inward_kernel, out_shape=(jax.ShapeDtypeStruct((times // 2...  5.88 us
  transfers between devices with their start and end apart: 3, of which 2 were waited for; matrix products, arithmetic and copies ran while one was open for 0% of the time, Pallas kernels for 12%

profile of v2, /device:TPU:2, one launch (start us, length us, event | category | flops | bytes accessed | tf_op | source)
XLA Modules:
  0.0 104.6 jit_solution(17167641997880291994)
XLA Ops:
  0.0 1.3 %broadcast_in_dim.12 = bf16[32,8,192]{2,1,0:T(8,128)(2,1)} broadcast(bf16[8,192]{1,0:T(8,128)(2,1)} %param.15), dimensions={1,2} | broadcast | bytes 101376 | tf_op jit(solution)/shard_map/broadcast_in_dim | solution.py:415
  1.3 9.4 %all-to-all-start = ((bf16[32,8,192]{2,1,0:T(8,128)(2,1)}), bf16[32,8,192]{2,1,0:T(8,128)(2,1)S(1)}, u32[]{:S(2)}, u32[]{:S(2)}) async-start(bf16[32,8,192]{2,1,0:T(8,128)(2,1)} %broadcast_in_dim.12), calls=%async_computation | async-start | bytes 262144 | tf_op jit(solution)/shard_map/all_to_all | solution.py:416
  10.8 0.0 copy-start
  10.8 1.7 %copy-done = bf16[3072,3,1,128]{3,0,2,1:T(8,128)(2,1)S(1)} copy-done((bf16[3072,3,1,128]{3,0,2,1:T(8,128)(2,1)S(1)}, bf16[3072,3,1,128]{3,0,2,1:T(8,128)(2,1)}, u32[]{:S(2)}) %copy-start) | copy-done | bytes 2359320
  12.4 0.0 copy-start.2
  12.4 1.1 %copy-done.2 = f32[16,4,3072]{2,1,0:T(4,128)S(1)} copy-done((f32[16,4,3072]{2,1,0:T(4,128)S(1)}, f32[16,4,3072]{2,1,0:T(4,128)}, u32[]{:S(2)}) %copy-start.2) | copy-done | bytes 786456
  13.6 0.0 copy-start.11
  13.6 1.0 copy-done.11
  14.6 0.0 copy-start.22
  14.6 0.8 copy-done.22
  15.3 0.0 copy-start.36
  15.3 0.7 copy-done.36
  16.0 0.0 copy-start.1
  16.0 0.0 copy-start.3
  16.0 0.0 copy-start.32
  16.0 5.9 %fold_inward.1 = (bf16[8,384,128]{2,1,0:T(8,128)(2,1)S(1)}, bf16[128,3072]{1,0:T(8,128)(2,1)S(1)}, bf16[16,256]{1,0:T(8,128)(2,1)S(1)}, bf16[64,128]{1,0:T(8,128)(2,1)S(1)}, f32[64,128]{1,0:T(8,128)S(1)}) custom-call(bf16[64,3072]{1,0:T(8,128)(2,1)S(1)} %copy-done.11, f32[16,4,3072]{2,1,0:T(4,128)S(1)} %copy-done.2, f32[1,64,128]{2,1,0:T(8,128)S(1)} %copy-done.22, ...), custom_call_target="tpu_custom_call" | custom-call | tf_op jit(solution)/shard_map/fold_inward/pallas_call | solution.py:287
  21.9 0.0 copy-start.4
  21.9 0.9 copy-done.4
  22.8 0.0 copy-start.14
  22.8 0.9 copy-done.14
  23.7 0.6 copy-done.26
  24.3 0.0 all-to-all-done.table
  24.3 1.0 select.1.sent
  25.3 13.4 %all-to-all-start.1 = ((bf16[16,80,128]{2,1,0:T(8,128)(2,1)}), bf16[16,80,128]{2,1,0:T(8,128)(2,1)S(1)}, u32[]{:S(2)}, u32[]{:S(2)}) async-start(bf16[16,80,128]{2,1,0:T(8,128)(2,1)} %select.1.sent), calls=%async_computation.1 | async-start | bytes 655360 | tf_op jit(solution)/shard_map/all_to_all | solution.py:421
  38.7 0.0 copy-done.1
  38.8 0.0 copy-done.3
  38.8 0.0 copy-done.32
  38.8 0.0 copy-start.5
  38.8 1.1 %copy-done.5 = bf16[128,3072]{1,0:T(8,128)(2,1)S(1)} copy-done((bf16[128,3072]{1,0:T(8,128)(2,1)S(1)}, bf16[128,3072]{1,0:T(8,128)(2,1)}, u32[]{:S(2)}) %copy-start.5) | copy-done | bytes 786456
  39.9 1.0 copy-done.9
  40.9 1.1 %copy-done.13 = bf16[1,128,3072]{2,1,0:T(8,128)(2,1)S(1)} copy-done((bf16[1,128,3072]{2,1,0:T(8,128)(2,1)S(1)}, bf16[1,128,3072]{2,1,0:T(8,128)(2,1)}, u32[]{:S(2)}) %copy-start.13) | copy-done | bytes 786456
  42.0 0.7 copy-done.33
  42.7 0.7 copy-done.34
  43.4 0.7 copy-done.35
  44.0 4.8 %fold_outward.1 = (bf16[16,64,128]{2,1,0:T(8,128)(2,1)S(1)}, f32[16,384]{1,0:T(8,128)S(1)}, bf16[128,64]{1,0:T(8,128)(2,1)S(1)}, f32[16,64]{1,0:T(8,128)S(1)}, f...) custom-call(f32[16]{0:T(128)S(1)} %copy-done.32, ...), custom_call_target="tpu_custom_call" | custom-call | tf_op jit(solution)/shard_map/fold_outward/pallas_call | solution.py:331
  48.9 0.0 copy-start.16
  48.9 0.7 copy-done.16
  49.6 0.7 copy-done.18
  50.2 0.7 copy-done.20
  50.9 0.6 copy-done.24
  51.6 0.6 copy-done.28
  52.2 0.6 copy-done.30
  52.8 7.3 %all-to-all-done.1.arrived = bf16[16,80,128]{2,1,0:T(8,128)(2,1)S(1)} async-done(((bf16[16,80,128]{2,1,0:T(8,128)(2,1)}), bf16[16,80,128]{2,1,0:T(8,128)(2,1)S(1)}, u32[]{:S(2)}, u32[]{:S(2)}) %all-to-all-start.1) | async-done | bytes 327712 | tf_op jit(solution)/shard_map/all_to_all | solution.py:421
  60.1 1.1 %copy-done.6 = bf16[128,3072]{1,0:T(8,128)(2,1)S(1)} copy-done((bf16[128,3072]{1,0:T(8,128)(2,1)S(1)}, bf16[128,3072]{1,0:T(8,128)(2,1)}, u32[]{:S(2)}) %copy-start.6) | copy-done | bytes 786456
  61.3 1.1 %copy-done.15 = bf16[8,384,128]{2,1,0:T(8,128)(2,1)S(1)} copy-done((bf16[8,384,128]{2,1,0:T(8,128)(2,1)S(1)}, bf16[8,384,128]{2,1,0:T(8,128)(2,1)}, u32[]{:S(2)}) %copy-start.15) | copy-done | bytes 786456
  62.4 0.9 copy-done.17
  63.3 0.9 copy-done.19
  64.3 0.9 copy-done.21
  65.2 0.9 copy-done.25
  66.1 0.8 copy-done.27
  66.9 0.8 copy-done.29
  67.6 0.7 copy-done.31
  68.4 10.6 %run_heads.1.sums = bf16[16,64,128]{2,1,0:T(8,128)(2,1)S(1)} custom-call(s32[1]{0:T(128)} %bitcast.1.here, bf16[16,80,128]{2,1,0:T(8,128)(2,1)S(1)} %all-to-all-done.1.arrived, bf16[3,3072,128]{2,1,0:T(8,128)(2,1)S(1)} %bitcast.15, bf16[8,384,128]{2,1,0:T(8,128)(2,1)S(1)} %copy-done.15, bf16[16,64,128]{2,1,0:T(8,128)(2,1)S(1)} %copy-done.17, ...), custom_call_target="tpu_custom_call" | custom-call | tf_op jit(solution)/shard_map/run_heads/pallas_call | solution.py:362
  78.9 0.0 copy-start.7
  79.0 0.7 copy-done.7
  79.6 6.0 %all-to-all-start.2 = ((bf16[16,64,128]{2,1,0:T(8,128)(2,1)}), bf16[16,64,128]{2,1,0:T(8,128)(2,1)S(1)}, u32[]{:S(2)}, u32[]{:S(2)}) async-start(bf16[16,64,128]{2,1,0:T(8,128)(2,1)} %copy-done.7), calls=%async_computation.2 | async-start | bytes 524288 | tf_op jit(solution)/shard_map/all_to_all | solution.py:430
  85.7 0.0 copy-start.8
  85.7 1.0 copy-done.8
  86.7 1.0 copy-done.10
  87.7 1.0 copy-done.12
  88.7 2.0 %residual.1 = f32[64,128]{1,0:T(8,128)S(1)} custom-call(s32[1]{0:T(128)} %bitcast.1.here, f32[16]{0:T(128)S(1)} %copy-done.32, bf16[16,80,128]{2,1,0:T(8,128)(2,1)S(1)} %all-to-all-done.1.arrived, f32[16,4,3072]{2,1,0:T(4,128)S(1)} %copy-done.3, bf16[64,3072]{1,0:T(8,128)(2,1)S(1)} %copy-done.12, bf16[64,3072]{1,0:T(8,128)(2,1)S(1)} %bitcast.17, ...), custom_call_target="tpu_custom_call" | custom-call | tf_op jit(solution)/shard_map/residual/pallas_call | solution.py:378
  90.6 13.4 %all-to-all-done.2 = bf16[16,64,128]{2,1,0:T(8,128)(2,1)S(1)} async-done(((bf16[16,64,128]{2,1,0:T(8,128)(2,1)}), bf16[16,64,128]{2,1,0:T(8,128)(2,1)S(1)}, u32[]{:S(2)}, u32[]{:S(2)}) %all-to-all-start.2) | async-done | bytes 262176 | tf_op jit(solution)/shard_map/all_to_all | solution.py:430
  104.0 0.0 copy-done.23
  104.0 0.6 fusion
  (24 shorter events, 0.1 us)
Async XLA Ops:
  1.3 22.9 %all-to-all-start = ((bf16[32,8,192]{2,1,0:T(8,128)(2,1)}), bf16[32,8,192]{2,1,0:T(8,128)(2,1)S(1)}, u32[]{:S(2)}, u32[]{:S(2)}) async-start(bf16[32,8,192]{2,1,0:T(8,128)(2,1)} %broadcast_in_dim.12), calls=%async_computation | async-start | bytes 262144 | tf_op jit(solution)/shard_map/all_to_all | solution.py:416
  10.8 1.7 %copy-start = (bf16[3072,3,1,128]{3,0,2,1:T(8,128)(2,1)S(1)}, bf16[3072,3,1,128]{3,0,2,1:T(8,128)(2,1)}, u32[]{:S(2)}) copy-start(bf16[3072,3,1,128]{3,0,2,1:T(8,128)(2,1)} %param.19) | copy-start | bytes 7077892
  12.4 1.1 %copy-start.2 = (f32[16,4,3072]{2,1,0:T(4,128)S(1)}, f32[16,4,3072]{2,1,0:T(4,128)}, u32[]{:S(2)}) copy-start(f32[16,4,3072]{2,1,0:T(4,128)} %terms.5) | copy-start | bytes 2359300
  13.6 1.0 copy-start.11
  14.6 0.8 copy-start.22
  15.3 0.7 copy-start.36
  16.0 22.8 %copy-start.1 = (bf16[3072,3,1,128]{3,0,2,1:T(8,128)(2,1)S(1)}, bf16[3072,3,1,128]{3,0,2,1:T(8,128)(2,1)}, u32[]{:S(2)}) copy-start(bf16[3072,3,1,128]{3,0,2,1:T(8,128)(2,1)} %param.19) | copy-start | bytes 7077892
  16.0 22.8 %copy-start.3 = (f32[16,4,3072]{2,1,0:T(4,128)S(1)}, f32[16,4,3072]{2,1,0:T(4,128)}, u32[]{:S(2)}) copy-start(f32[16,4,3072]{2,1,0:T(4,128)} %terms.5) | copy-start | bytes 2359300
  16.0 22.8 %copy-start.32 = (f32[16]{0:T(128)S(1)}, f32[16]{0:T(128)}, u32[]{:S(2)}) copy-start(f32[16]{0:T(128)} %steps.3) | copy-start | bytes 196
  21.9 0.9 copy-start.4
  22.8 0.9 copy-start.14
  23.7 0.6 copy-start.26
  25.3 34.8 %all-to-all-start.1 = ((bf16[16,80,128]{2,1,0:T(8,128)(2,1)}), bf16[16,80,128]{2,1,0:T(8,128)(2,1)S(1)}, u32[]{:S(2)}, u32[]{:S(2)}) async-start(bf16[16,80,128]{2,1,0:T(8,128)(2,1)} %select.1.sent), calls=%async_computation.1 | async-start | bytes 655360 | tf_op jit(solution)/shard_map/all_to_all | solution.py:421
  38.8 1.1 %copy-start.5 = (bf16[128,3072]{1,0:T(8,128)(2,1)S(1)}, bf16[128,3072]{1,0:T(8,128)(2,1)}, u32[]{:S(2)}) copy-start(bf16[128,3072]{1,0:T(8,128)(2,1)} %copy-done.4) | copy-start | bytes 2359300
  39.9 1.0 copy-start.9
  40.9 1.1 %copy-start.13 = (bf16[1,128,3072]{2,1,0:T(8,128)(2,1)S(1)}, bf16[1,128,3072]{2,1,0:T(8,128)(2,1)}, u32[]{:S(2)}) copy-start(bf16[1,128,3072]{2,1,0:T(8,128)(2,1)} %param.22) | copy-start | bytes 2359300
  42.0 0.7 copy-start.33
  42.7 0.7 copy-start.34
  43.4 0.7 copy-start.35
  48.9 0.7 copy-start.16
  49.6 0.7 copy-start.18
  50.2 0.7 copy-start.20
  50.9 0.6 copy-start.24
  51.6 0.6 copy-start.28
  52.2 0.6 copy-start.30
  60.1 1.1 %copy-start.6 = (bf16[128,3072]{1,0:T(8,128)(2,1)S(1)}, bf16[128,3072]{1,0:T(8,128)(2,1)}, u32[]{:S(2)}) copy-start(bf16[128,3072]{1,0:T(8,128)(2,1)} %copy-done.4) | copy-start | bytes 2359300
  61.3 1.1 %copy-start.15 = (bf16[8,384,128]{2,1,0:T(8,128)(2,1)S(1)}, bf16[8,384,128]{2,1,0:T(8,128)(2,1)}, u32[]{:S(2)}) copy-start(bf16[8,384,128]{2,1,0:T(8,128)(2,1)} %copy-done.14) | copy-start | bytes 2359300
  62.4 0.9 copy-start.17
  63.3 0.9 copy-start.19
  64.3 0.9 copy-start.21
  65.2 0.9 copy-start.25
  66.1 0.8 copy-start.27
  66.9 0.8 copy-start.29
  67.6 0.7 copy-start.31
  78.9 0.7 copy-start.7
  79.6 24.4 %copy-start.23 = (f32[1,64,128]{2,1,0:T(8,128)S(1)}, f32[1,64,128]{2,1,0:T(8,128)}, u32[]{:S(2)}) copy-start(f32[1,64,128]{2,1,0:T(8,128)} %latents.1) | copy-start | bytes 98308
  79.6 24.3 %all-to-all-start.2 = ((bf16[16,64,128]{2,1,0:T(8,128)(2,1)}), bf16[16,64,128]{2,1,0:T(8,128)(2,1)S(1)}, u32[]{:S(2)}, u32[]{:S(2)}) async-start(bf16[16,64,128]{2,1,0:T(8,128)(2,1)} %copy-done.7), calls=%async_computation.2 | async-start | bytes 524288 | tf_op jit(solution)/shard_map/all_to_all | solution.py:430
  85.7 1.0 copy-start.8
  86.7 1.0 copy-start.10
  87.7 1.0 copy-start.12

commit v3 on v2

v3 whole, which is shorter than its diff:
```python
import jax
import jax.numpy as jnp
from jax import lax
from jax.experimental import pallas as pl
from jax.experimental.pallas import tpu as pltpu
from jax.sharding import PartitionSpec as P

EPS = 1e-06
MASKED = -1e30
LOG2E = 1.4426950408889634
BF16, F32 = jnp.bfloat16, jnp.float32
NN = (((1,), (0,)), ((), ()))
NT = (((1,), (1,)), ((), ()))
VMEM = pl.BlockSpec(memory_space=pltpu.VMEM)
SMEM = pl.BlockSpec(memory_space=pltpu.SMEM)
HBM = pl.BlockSpec(memory_space=pltpu.HBM)
PARAMS = pltpu.CompilerParams(vmem_limit_bytes=24 * 2**20)


def dot(left, right, dims=NN, precision=None):
    return lax.dot_general(left, right, dims, precision=precision, preferred_element_type=F32)


def two_parts(values):
    high = values.astype(BF16)
    return high, (values - high.astype(F32)).astype(BF16)


def stack_rows(*parts):
    return jnp.concatenate([p.astype(F32) for p in parts], axis=0).astype(BF16)


def centre(values):
    return values - jnp.mean(values, axis=-1, keepdims=True)


def pinned(*arrays):
    return tuple(pltpu.with_memory_space_constraint(a, pltpu.HBM) for a in arrays)


def fetch(pairs, sems):
    copies = [pltpu.make_async_copy(a, b, sems.at[i]) for i, (a, b) in enumerate(pairs)]
    for copy in copies:
        copy.start()
    return copies


def inward_kernel(
    w_in, terms, w_qkv, latents, pack_docs,
    inward, pieces, pick, rest, sent,
    w_in_v, terms_v, w_qkv_v, latents_v, packs_v, centred, rows, inward_v, pieces_v, pick_v, rest_v,
    lowered_v, sems, out_sems,
):
    chans, wide = w_in_v.shape
    times = terms_v.shape[0]
    head = w_qkv.shape[2]
    spans = [slice(c * head, (c + 1) * head) for c in range(3)]
    copies = fetch(
        [(w_in, w_in_v), (terms, terms_v)]
        + [(w_qkv.at[c], w_qkv_v.at[:, spans[c]]) for c in range(3)]
        + [(latents, latents_v), (pack_docs, packs_v)],
        sems,
    )
    copies[0].wait()
    centred[...] = centre(w_in_v[...].astype(F32))
    high, low = two_parts(centred[...])
    pieces_v[:chans, :] = high
    pieces_v[chans:, :] = low
    copies[5].wait()
    values = latents_v[0]
    high = values.astype(BF16)
    lowered_v[...] = high
    rest_v[...] = values - high.astype(F32)
    copies[6].wait()
    count = packs_v.shape[1]
    column = jnp.broadcast_to(packs_v[...].astype(F32), (count, count))
    eye = lax.broadcasted_iota(jnp.int32, (count, count), 0) == lax.broadcasted_iota(
        jnp.int32, (count, count), 1
    )
    column = jnp.sum(jnp.where(eye, column, 0.0), axis=1, keepdims=True)
    places = lax.broadcasted_iota(jnp.int32, (count, pick.shape[1]), 1).astype(F32)
    chosen = jnp.where(places == column, 1.0, 0.0)
    pick_v[...] = stack_rows(chosen, jnp.zeros_like(chosen))
    left = fetch(
        [(pieces_v, pieces), (rest_v, rest), (pick_v, pick)]
        + [(lowered_v, sent.at[i, pl.ds(0, chans)]) for i in range(times)],
        out_sems,
    )
    copies[1].wait()
    for step in range(times // 4):
        for j in range(4):
            scaled = centred[...] * (1.0 + terms_v[step * 4 + j, 2:3, :])
            rows[step % 2, j * chans : (j + 1) * chans, :] = scaled.astype(BF16)
        if step == 0:
            for c in range(3):
                copies[2 + c].wait()
        turned = dot(rows[step % 2], w_qkv_v[...]).T.astype(BF16)
        inward_v[2 * step] = turned[:, : 2 * chans]
        inward_v[2 * step + 1] = turned[:, 2 * chans :]
        copy = pltpu.make_async_copy(
            inward_v.at[pl.ds(2 * step, 2)],
            inward.at[pl.ds(2 * step, 2)],
            out_sems.at[3 + times + step],
        )
        copy.start()
        left.append(copy)
    for copy in left:
        copy.wait()


def select_kernel(table, pick, sent, out, pick_v, staged, sems):
    del sent
    size, rows, lanes = out.shape
    owners, count, piece = table.shape
    fetch([(pick, pick_v)], sems.at[pl.ds(size, 1)])[0].wait()
    chosen = dot(pick_v[...], table[...].reshape(owners * count, piece))[:count]
    tail = jnp.concatenate(
        [chosen[:, lanes:], jnp.zeros((count, 2 * lanes - piece), F32)], axis=1
    )
    staged[...] = stack_rows(chosen[:, :lanes], tail)
    head = rows - 2 * count
    copies = fetch([(staged, out.at[i, pl.ds(head, 2 * count)]) for i in range(size)], sems)
    for copy in copies:
        copy.wait()


def outward_kernel(
    steps, terms, w_final, w_proj, w_qkv, pieces, query_gain, key_gain, segments, sent,
    outward, shifts, gram, cross, embedded, scales, gains, bias, member,
    terms_v, w_final_v, w_proj_v, w_qkv_v, pieces_v, gains_v, segments_v, rows,
    outward_v, shifts_v, gram_v, cross_v, embedded_v, scales_v, gain_rows, bias_v, member_v,
    sems, out_sems,
):
    del sent
    times, chans, head = outward.shape
    spans = [slice(c * head, (c + 1) * head) for c in range(3)]
    copies = fetch(
        [
            (terms, terms_v), (w_final, w_final_v), (w_proj, w_proj_v), (pieces, pieces_v),
            (query_gain, gains_v.at[0]), (key_gain, gains_v.at[1]), (segments, segments_v),
        ]
        + [(w_qkv.at[c], w_qkv_v.at[:, spans[c]]) for c in range(3)],
        sems,
    )
    copies[0].wait()
    moved, means = [], []
    for t in range(times):
        moved.append(terms_v[t, 1:2, :])
        means.append(centre(terms_v[t, 0:1, :]))
        scales_v[t : t + 1, :] = 1.0 + terms_v[t, 2:3, :]
    moved, means = jnp.concatenate(moved, axis=0), jnp.concatenate(means, axis=0)
    embedded_v[...] = means
    copies[1].wait()
    copies[2].wait()
    for step in range(times // 4):
        for j in range(4):
            gated = w_final_v[...].astype(F32) * terms_v[step * 4 + j, 3:4, :]
            rows[step % 2, j * chans : (j + 1) * chans, :] = gated.astype(BF16)
        back = dot(rows[step % 2], w_proj_v[...], NT)
        for j in range(4):
            t = step * 4 + j
            outward_v[t] = (back[j * chans : (j + 1) * chans] * steps[t]).astype(BF16)
    copies[3].wait()
    both = pieces_v[...]
    square = dot(both, both, NT)
    square = square[:chans, :chans] + square[chans:, :chans] + square[:chans, chans:]
    high, low = two_parts(square)
    gram_v[:chans, :] = high
    gram_v[chans:, :] = low
    high, low = two_parts(means)
    mixed = dot(stack_rows(high, low), both, NT)
    cross_v[...] = mixed[:times, :chans] + mixed[times:, :chans] + mixed[:times, chans:]
    for copy in copies[4:]:
        copy.wait()
    high, low = two_parts(moved)
    shift = dot(stack_rows(high, low), w_qkv_v[...])
    shifts_v[...] = shift[:times] + shift[times:]
    tokens = segments_v.shape[1]
    gain_rows[0] = jnp.broadcast_to(gains_v[0] * (head**-0.5 * LOG2E), (head, head)).T
    gain_rows[1] = jnp.broadcast_to(gains_v[1], (head, head)).T
    ids = jnp.broadcast_to(segments_v[...].astype(F32), (tokens, tokens))
    bias_v[...] = jnp.where(ids == ids.T, 0.0, MASKED)
    count = member_v.shape[0]
    numbers = lax.broadcasted_iota(jnp.int32, (count, tokens), 0).astype(F32)
    member_v[...] = jnp.where(numbers == ids[:count], 1.0, 0.0)
    left = fetch(
        [
            (outward_v, outward), (shifts_v, shifts), (gram_v, gram), (cross_v, cross),
            (embedded_v, embedded), (scales_v, scales), (gain_rows, gains), (bias_v, bias),
            (member_v, member),
        ],
        out_sems,
    )
    for copy in left:
        copy.wait()


def gather_documents(arrived, chans, count, piece):
    parts = []
    for i in range(arrived.shape[0]):
        block = arrived[i, chans:, :].astype(F32)
        parts.append(block[:count])
        parts.append(block[count:, : piece - block.shape[1]])
    return jnp.concatenate(parts, axis=1)


def heads_kernel(
    here, arrived,
    embedded_h, scales_h, w_in_h, w_qkv_h, shifts_h, gram_h, cross_h, member_h, gains_h, bias_h,
    inward_h, outward_h, rest_h,
    out, kept,
    embedded, scales, w_in, w_qkv, shifts, gram, cross, member, gains, bias,
    inward, outward, rest,
    rows, staged, sems,
):
    times, chans, head = outward.shape
    count, tokens = member.shape
    wide = w_in.shape[1]
    spans = [slice(c * head, (c + 1) * head) for c in range(3)]
    copies = fetch(
        [(embedded_h, embedded), (scales_h, scales), (w_in_h, w_in)]
        + [(w_qkv_h.at[c], w_qkv.at[:, spans[c]]) for c in range(3)]
        + [
            (shifts_h, shifts), (gram_h, gram), (cross_h, cross), (member_h, member),
            (gains_h, gains), (bias_h, bias), (inward_h, inward), (outward_h, outward),
            (rest_h, rest), (arrived, kept),
        ],
        sems,
    )
    documents = centre(gather_documents(arrived, chans, count, wide // times))
    for copy in copies[:3]:
        copy.wait()
    high, low = two_parts(documents)
    near = dot(stack_rows(high, low), w_in[...], NT)
    near = near[:count] + near[count:]
    powers = []
    for t in range(0, times, 2):
        pair = []
        for j in range(2):
            row = documents + embedded[t + j : t + j + 1, :]
            powers.append(jnp.sum(row * row, axis=-1, keepdims=True))
            pair.append(row * scales[t + j : t + j + 1, :])
        rows[t * count : (t + 2) * count, :] = jnp.concatenate(pair, axis=0).astype(BF16)
    for copy in copies[3:7]:
        copy.wait()
    base = dot(rows[...], w_qkv[...])
    turned = []
    for half in range(2):
        span = slice(half * 8 * count, (half + 1) * 8 * count)
        block = [base[span], shifts[half * 8 : (half + 1) * 8, :]]
        left = head - 8 * count - 8
        block.append(jnp.zeros((left, 3 * head), F32))
        turned.append(jnp.concatenate(block, axis=0).T.astype(BF16))

    for copy in copies[7:-1]:
        copy.wait()
    belongs = member[...]
    scaled_low, rates = [], []
    for t in range(times):
        mixed = 2.0 * (near + cross[t : t + 1, :])
        high, low = two_parts(mixed)
        left = jnp.concatenate([gram[...], stack_rows(high, low)], axis=0)
        values = arrived[t, :chans, :]
        whole = dot(left, values)
        both = whole[:chans] + whole[chans : 2 * chans]
        values = values.astype(F32)
        other = whole[2 * chans : 2 * chans + count] + whole[2 * chans + count :]
        spread = jnp.sum(both * values, axis=0, keepdims=True) + jnp.sum(
            belongs * (other + powers[t]), axis=0, keepdims=True
        )
        rate = lax.rsqrt(spread / wide + EPS)
        rates.append(rate)
        scaled_low.append((values * rate).astype(BF16))

    def unit(values, gain):
        power = jnp.mean(values * values, axis=0, keepdims=True)
        return values * lax.rsqrt(power + EPS) * gain

    total = jnp.where(here[0] == 0, rest[...], 0.0)
    empty = jnp.zeros((chans, tokens), BF16)
    for t in range(times):
        staged[t] = total.astype(BF16)
        half, j = divmod(t, 8)
        left = jnp.concatenate([inward[t // 2], turned[half]], axis=1)
        first = [scaled_low[t], empty] if t % 2 == 0 else [empty, scaled_low[t]]
        ones = lax.broadcasted_iota(jnp.int32, (8, tokens), 0) == j
        second = [jnp.zeros((j * count, tokens), F32)] if j else []
        second.append(belongs * rates[t])
        if j < 7:
            second.append(jnp.zeros(((7 - j) * count, tokens), F32))
        second.append(jnp.where(ones, 1.0, 0.0))
        second.append(jnp.zeros((head - 8 * count - 8, tokens), F32))
        second = jnp.concatenate(second, axis=0).astype(BF16)
        projected = dot(left, jnp.concatenate(first + [second], axis=0))
        queries = unit(projected[:head], gains[0]).astype(BF16)
        keys = unit(projected[head : 2 * head], gains[1]).T.astype(BF16)
        values = projected[2 * head :].astype(BF16)
        scores = dot(keys, queries) + bias[...]
        raised = jnp.exp2(scores - jnp.max(scores, axis=0, keepdims=True))
        mass = jnp.sum(raised, axis=0, keepdims=True)
        attended = (dot(values, raised.astype(BF16)) * (1.0 / mass)).astype(BF16)
        total = total + dot(outward[t], attended)
    last = pltpu.make_async_copy(staged, out, sems.at[len(copies)])
    last.start()
    copies[-1].wait()
    last.wait()


def residual_kernel(
    here, steps, kept, terms, w_in, w_final, member_h,
    out,
    arrived, terms_v, w_in_v, w_final_v, member, sems,
):
    times = terms_v.shape[0]
    chans, wide = w_in_v.shape
    count = member.shape[0]
    copies = fetch(
        [
            (terms, terms_v), (w_in, w_in_v), (w_final, w_final_v), (kept, arrived),
            (member_h, member),
        ],
        sems,
    )
    copies[3].wait()
    copies[4].wait()
    documents = gather_documents(arrived, chans, count, wide // times)
    mixed = jnp.zeros(out.shape, F32)
    weights, whole = [], 0.0
    for t in range(times):
        weights.append(jnp.where(t < here[0], steps[t], 0.0))
        mixed = mixed + weights[t] * arrived[t, :chans, :].astype(F32)
        whole = whole + weights[t]
    copies[0].wait()
    embedded = jnp.zeros((1, wide), F32)
    for t in range(times):
        embedded = embedded + weights[t] * terms_v[t, 0:1, :]
    rows = embedded + whole * documents
    high = rows.astype(BF16)
    middle, low = two_parts(rows - high.astype(F32))
    copies[1].wait()
    copies[2].wait()
    final = w_final_v[...]
    narrow = dot(final, high, NT) + dot(final, middle, NT) + dot(final, low, NT)
    direct = dot(final, w_in_v[...], NT)
    highest = lax.Precision.HIGHEST
    near = dot(direct, mixed, NN, highest) + dot(narrow, member[...], NN, highest)
    out[...] = near + arrived[0, :chans, :].astype(F32)


def fold_inward(w_in, terms, w_qkv, latents, pack_docs, documents):
    times, (chans, wide), head = terms.shape[0], w_in.shape, w_qkv.shape[2]
    block, count = latents.shape[1:], pack_docs.shape[1]
    shapes = [
        ((times // 2, 3 * head, 2 * chans), BF16),
        ((2 * chans, wide), BF16),
        ((2 * count, documents), BF16),
        (block, F32),
    ]
    return pl.pallas_call(
        inward_kernel,
        out_shape=tuple(pltpu.HBM(*s) for s in shapes)
        + (pltpu.HBM((times, chans + 2 * count, block[1]), BF16),),
        in_specs=[HBM] * 5,
        out_specs=(HBM,) * 5,
        scratch_shapes=[
            pltpu.VMEM(w_in.shape, BF16),
            pltpu.VMEM(terms.shape, F32),
            pltpu.VMEM((wide, 3 * head), BF16),
            pltpu.VMEM(latents.shape, F32),
            pltpu.VMEM(pack_docs.shape, jnp.int32),
            pltpu.VMEM(w_in.shape, F32),
            pltpu.VMEM((2, 4 * chans, wide), BF16),
        ]
        + [pltpu.VMEM(*s) for s in shapes]
        + [
            pltpu.VMEM(block, BF16),
            pltpu.SemaphoreType.DMA((7,)),
            pltpu.SemaphoreType.DMA((3 + times + times // 4,)),
        ],
        compiler_params=PARAMS,
        name="fold_inward",
    )(*pinned(w_in, terms, w_qkv, latents, pack_docs))


def select(table, pick, sent):
    size = sent.shape[0]
    return pl.pallas_call(
        select_kernel,
        out_shape=pltpu.HBM(sent.shape, BF16),
        in_specs=[VMEM, HBM, HBM],
        out_specs=HBM,
        scratch_shapes=[
            pltpu.VMEM(pick.shape, BF16),
            pltpu.VMEM((pick.shape[0], sent.shape[2]), BF16),
            pltpu.SemaphoreType.DMA((size + 1,)),
        ],
        input_output_aliases={2: 0},
        compiler_params=PARAMS,
        name="select",
    )(table, *pinned(pick, sent))


def fold_outward(
    steps, terms, w_final, w_proj, w_qkv, pieces, query_gain, key_gain, segments, sent, count
):
    times, wide = terms.shape[0], terms.shape[2]
    chans, head, tokens = w_final.shape[0], w_proj.shape[0], segments.shape[1]
    shapes = [
        ((times, chans, head), BF16),
        ((times, 3 * head), F32),
        ((2 * chans, chans), BF16),
        ((times, chans), F32),
        ((times, wide), F32),
        ((times, wide), F32),
        ((2, head, head), F32),
        ((tokens, tokens), F32),
        ((count, tokens), F32),
    ]
    return pl.pallas_call(
        outward_kernel,
        out_shape=tuple(pltpu.HBM(*s) for s in shapes),
        in_specs=[SMEM] + [HBM] * 9,
        out_specs=(HBM,) * 9,
        scratch_shapes=[
            pltpu.VMEM(terms.shape, F32),
            pltpu.VMEM(w_final.shape, BF16),
            pltpu.VMEM(w_proj.shape, BF16),
            pltpu.VMEM((wide, 3 * head), BF16),
            pltpu.VMEM(pieces.shape, BF16),
            pltpu.VMEM((2,) + query_gain.shape, F32),
            pltpu.VMEM(segments.shape, jnp.int32),
            pltpu.VMEM((2, 4 * chans, wide), BF16),
        ]
        + [pltpu.VMEM(*s) for s in shapes]
        + [pltpu.SemaphoreType.DMA((10,)), pltpu.SemaphoreType.DMA((9,))],
        compiler_params=PARAMS,
        name="fold_outward",
    )(
        steps,
        *pinned(terms, w_final, w_proj, w_qkv, pieces, query_gain, key_gain, segments, sent),
    )


def run_heads(here, arrived, embedded, scales, w_in, w_qkv, *rest):
    outward = rest[-2]
    head = w_qkv.shape[2]
    rows = arrived.shape[0] * (arrived.shape[1] - outward.shape[1]) // 2
    held = [
        pltpu.VMEM(a.shape, a.dtype) for a in (embedded, scales, w_in)
    ] + [pltpu.VMEM((w_qkv.shape[1], 3 * head), BF16)]
    held += [pltpu.VMEM(a.shape, a.dtype) for a in rest]
    return pl.pallas_call(
        heads_kernel,
        out_shape=(pltpu.HBM(outward.shape, BF16), pltpu.HBM(arrived.shape, BF16)),
        in_specs=[SMEM, VMEM] + [HBM] * 13,
        out_specs=(HBM, HBM),
        scratch_shapes=held
        + [
            pltpu.VMEM((rows, embedded.shape[1]), BF16),
            pltpu.VMEM(outward.shape, BF16),
            pltpu.SemaphoreType.DMA((17,)),
        ],
        compiler_params=PARAMS,
        name="run_heads",
    )(here, arrived, *pinned(embedded, scales, w_in, w_qkv, *rest))


def residual(here, steps, kept, terms, w_in, w_final, member):
    return pl.pallas_call(
        residual_kernel,
        out_shape=jax.ShapeDtypeStruct((w_in.shape[0], kept.shape[2]), F32),
        in_specs=[SMEM] * 2 + [HBM] * 5,
        out_specs=VMEM,
        scratch_shapes=[
            pltpu.VMEM(kept.shape, BF16),
            pltpu.VMEM(terms.shape, F32),
            pltpu.VMEM(w_in.shape, BF16),
            pltpu.VMEM(w_final.shape, BF16),
            pltpu.VMEM(member.shape, F32),
            pltpu.SemaphoreType.DMA((5,)),
        ],
        compiler_params=PARAMS,
        name="residual",
    )(here, steps, *pinned(kept, terms, w_in, w_final, member))


def local(
    latents,
    time_terms,
    step_sizes,
    doc_embed,
    pack_docs,
    segment_ids,
    w_in,
    w_qkv,
    query_gain,
    key_gain,
    w_proj,
    w_final,
):
    here = lax.axis_index("tm")
    place = here.astype(jnp.int32).reshape(1)
    times, owners = lax.axis_size("tm"), lax.axis_size("req")
    count, piece = doc_embed.shape
    w_heads = w_qkv[:, :, 0, :].transpose(1, 0, 2)
    w_last = w_final.T

    copies = jnp.broadcast_to(doc_embed[None], (owners, count, piece))
    table = lax.all_to_all(copies, "req", 0, 0)
    inward, pieces, pick, rest, sent = fold_inward(
        w_in, time_terms, w_heads, latents, pack_docs[None], owners * count
    )
    sent = select(table, pick, sent)
    arrived = lax.all_to_all(sent, "tm", 0, 0)
    outward, shifts, gram, cross, embedded, scales, gains, bias, member = fold_outward(
        step_sizes, time_terms, w_last, w_proj[0], w_heads, pieces, query_gain, key_gain,
        segment_ids, sent, count,
    )
    sums, kept = run_heads(
        place, arrived, embedded, scales, w_in, w_heads, shifts, gram, cross, member, gains, bias,
        inward, outward, rest,
    )
    parts = lax.all_to_all(sums, "tm", 0, 0)
    direct = residual(place, step_sizes, kept, time_terms, w_in, w_last, member)
    before = direct + jnp.sum(parts.astype(F32), axis=0)
    return jnp.where(here == 0, latents[0], before)[None]


def solution(mesh):
    in_specs = (
        P("tm", None, "req"),
        P(),
        P(),
        P("req", "tm"),
        P("req"),
        P("req", None),
        P(),
        P(None, None, "tm", None),
        P("tm", None),
        P("tm", None),
        P("tm", None, None),
        P(),
    )
    out_specs = P("tm", None, "req")
    return jax.shard_map(local, mesh=mesh, in_specs=in_specs, out_specs=out_specs, check_vma=False)
```

time: 106 us -> 93.1 us (0.88)
  the two profiles are of different devices: /device:TPU:2 before, /device:TPU:32 now
where the time goes in v3:
time: 93.1 us; the launch traced here: 92.6 us
  Pallas kernels  30.7 us (33%)
  waiting for transfers between devices  30.5 us (33%)
  starting transfers between devices  29.3 us (31%)
  local copies, waits for them, and re-layouts  1.37 us (1%)
    all_to_all x1, starting transfers between devices, local(): arrived = lax.all_to_all(sent, 'tm', 0, 0)  15.2 us
    all_to_all x1, waiting for transfers between devices, local(): parts = lax.all_to_all(sums, 'tm', 0, 0)  15 us
    all_to_all x1, waiting for transfers between devices, local(): arrived = lax.all_to_all(sent, 'tm', 0, 0)  14.3 us
    pallas_call x1, Pallas kernels, run_heads(): pl.pallas_call(heads_kernel, out_shape=(pltpu.HBM(outward.shape, BF16), p...  13.3 us
    all_to_all x1, starting transfers between devices, local(): table = lax.all_to_all(copies, 'req', 0, 0)  7.32 us
    all_to_all x1, starting transfers between devices, local(): parts = lax.all_to_all(sums, 'tm', 0, 0)  6.73 us
    pallas_call x1, Pallas kernels, fold_inward(): pl.pallas_call(inward_kernel, out_shape=tuple((pltpu.HBM(*s) for s in sha...  6.63 us
    pallas_call x1, Pallas kernels, fold_outward(): pl.pallas_call(outward_kernel, out_shape=tuple((pltpu.HBM(*s) for s in sh...  6.16 us
  transfers between devices with their start and end apart: 3, of which 3 were waited for; matrix products, arithmetic and copies ran while one was open for 0% of the time, Pallas kernels for 17%

profile of v3, /device:TPU:32, one launch (start us, length us, event | category | flops | bytes accessed | tf_op | source)
XLA Modules:
  0.0 92.6 jit_solution(8586648410840274039)
XLA Ops:
  0.0 1.4 %broadcast_in_dim.12 = bf16[32,8,192]{2,1,0:T(8,128)(2,1)} broadcast(bf16[8,192]{1,0:T(8,128)(2,1)} %param.15), dimensions={1,2} | broadcast | bytes 101376 | tf_op jit(solution)/shard_map/broadcast_in_dim | solution.py:508
  1.4 7.3 %all-to-all-start = ((bf16[32,8,192]{2,1,0:T(8,128)(2,1)}), bf16[32,8,192]{2,1,0:T(8,128)(2,1)S(1)}, u32[]{:S(2)}, u32[]{:S(2)}) async-start(bf16[32,8,192]{2,1,0:T(8,128)(2,1)} %broadcast_in_dim.12), calls=%async_computation | async-start | bytes 262144 | tf_op jit(solution)/shard_map/all_to_all | solution.py:509
  8.7 0.0 copy-start
  8.7 6.6 %fold_inward.1 = (bf16[8,384,128]{2,1,0:T(8,128)(2,1)}, bf16[128,3072]{1,0:T(8,128)(2,1)}, bf16[16,256]{1,0:T(8,128)(2,1)}, f32[64,128]{1,0:T(8,128)}, bf16[16,80,128]{2,1,0:T(8,128)(2,1)}) custom-call(bf16[64,3072]{1,0:T(8,128)(2,1)} %w_in.3, f32[16,4,3072]{2,1,0:T(4,128)} %terms.5, bf16[3,3072,128]{2,1,0:T(8,128)(2,1)} %bitcast.13, f32[1,64,128]{2,1,0:T(8,128)} %latents.1, ...), custom_call_target="tpu_custom_call" | custom-call | tf_op jit(solution)/shard_map/fold_inward/pallas_call | solution.py:359
  15.3 1.2 %all-to-all-done.table = bf16[32,8,192]{2,1,0:T(8,128)(2,1)S(1)} async-done(((bf16[32,8,192]{2,1,0:T(8,128)(2,1)}), bf16[32,8,192]{2,1,0:T(8,128)(2,1)S(1)}, u32[]{:S(2)}, u32[]{:S(2)}) %all-to-all-start) | async-done | bytes 98336 | tf_op jit(solution)/shard_map/all_to_all | solution.py:509
  16.5 1.6 %select.1.sent = bf16[16,80,128]{2,1,0:T(8,128)(2,1)} custom-call(bf16[32,8,192]{2,1,0:T(8,128)(2,1)S(1)} %all-to-all-done.table, bf16[16,256]{1,0:T(8,128)(2,1)} %get-tuple-element.21.pick, bf16[16,80,128]{2,1,0:T(8,128)(2,1)} %get-tuple-element.22.sent), custom_call_target="tpu_custom_call", output_to_operand_aliasing={{}: (2, {})} | custom-call | tf_op jit(solution)/shard_map/select/pallas_call | solution.py:387
  18.1 15.2 %all-to-all-start.1 = ((bf16[16,80,128]{2,1,0:T(8,128)(2,1)}), bf16[16,80,128]{2,1,0:T(8,128)(2,1)S(1)}, u32[]{:S(2)}, u32[]{:S(2)}) async-start(bf16[16,80,128]{2,1,0:T(8,128)(2,1)} %select.1.sent), calls=%async_computation.1 | async-start | bytes 655360 | tf_op jit(solution)/shard_map/all_to_all | solution.py:514
  33.4 0.0 copy-done
  33.4 6.2 %fold_outward.1 = (bf16[16,64,128]{2,1,0:T(8,128)(2,1)}, f32[16,384]{1,0:T(8,128)}, bf16[128,64]{1,0:T(8,128)(2,1)}, f32[16,64]{1,0:T(8,128)}, f32[16,3072]{1,0:...) custom-call(f32[16]{0:T(128)S(1)} %copy-done, ...), custom_call_target="tpu_custom_call" | custom-call | tf_op jit(solution)/shard_map/fold_outward/pallas_call | solution.py:419
  39.5 14.3 %all-to-all-done.1.arrived = bf16[16,80,128]{2,1,0:T(8,128)(2,1)S(1)} async-done(((bf16[16,80,128]{2,1,0:T(8,128)(2,1)}), bf16[16,80,128]{2,1,0:T(8,128)(2,1)S(1)}, u32[]{:S(2)}, u32[]{:S(2)}) %all-to-all-start.1) | async-done | bytes 327712 | tf_op jit(solution)/shard_map/all_to_all | solution.py:514
  53.9 13.3 %run_heads.1 = (bf16[16,64,128]{2,1,0:T(8,128)(2,1)}, bf16[16,80,128]{2,1,0:T(8,128)(2,1)}) custom-call(s32[1]{0:T(128)} %bitcast.1.here, bf16[16,80,128]{2,1,0:T(8,128)(2,1)S(1)} %all-to-all-done.1.arrived, f32[16,3072]{1,0:T(8,128)} %get-tuple-element.24.embedded_h, f32[16,3072]{1,0:T(8,128)} %get-tuple-element.25.scales_h, bf16[64,3072]{1,0:T(8,128)(2,1)} %w_in.3, ...), custom_call_target="tpu_custom_call" | custom-call | tf_op jit(solution)/shard_map/run_heads/pallas_call | solution.py:452
  67.2 0.0 copy-start.1
  67.2 6.7 %all-to-all-start.2 = ((bf16[16,64,128]{2,1,0:T(8,128)(2,1)}), bf16[16,64,128]{2,1,0:T(8,128)(2,1)S(1)}, u32[]{:S(2)}, u32[]{:S(2)}) async-start(bf16[16,64,128]{2,1,0:T(8,128)(2,1)} %get-tuple-element.36), calls=%async_computation.2 | async-start | bytes 524288 | tf_op jit(solution)/shard_map/all_to_all | solution.py:523
  73.9 3.0 %residual.1 = f32[64,128]{1,0:T(8,128)S(1)} custom-call(s32[1]{0:T(128)} %bitcast.1.here, f32[16]{0:T(128)S(1)} %copy-done, bf16[16,80,128]{2,1,0:T(8,128)(2,1)} %get-tuple-element.35.kept, f32[16,4,3072]{2,1,0:T(4,128)} %terms.5, bf16[64,3072]{1,0:T(8,128)(2,1)} %w_in.3, bf16[64,3072]{1,0:T(8,128)(2,1)} %bitcast.17, f32[8,128]{1,0:T(8,128)} %get-tuple-element.29.member_h), custom_call_target="tpu_custom_call" | custom-call | tf_op jit(solution)/shard_map/residual/pallas_call | solution.py:469
  76.9 15.0 %all-to-all-done.2 = bf16[16,64,128]{2,1,0:T(8,128)(2,1)S(1)} async-done(((bf16[16,64,128]{2,1,0:T(8,128)(2,1)}), bf16[16,64,128]{2,1,0:T(8,128)(2,1)S(1)}, u32[]{:S(2)}, u32[]{:S(2)}) %all-to-all-start.2) | async-done | bytes 262176 | tf_op jit(solution)/shard_map/all_to_all | solution.py:523
  92.0 0.0 copy-done.1
  92.0 0.6 fusion
  (1 shorter events, 0.0 us)
Async XLA Ops:
  1.4 15.1 %all-to-all-start = ((bf16[32,8,192]{2,1,0:T(8,128)(2,1)}), bf16[32,8,192]{2,1,0:T(8,128)(2,1)S(1)}, u32[]{:S(2)}, u32[]{:S(2)}) async-start(bf16[32,8,192]{2,1,0:T(8,128)(2,1)} %broadcast_in_dim.12), calls=%async_computation | async-start | bytes 262144 | tf_op jit(solution)/shard_map/all_to_all | solution.py:509
  8.7 24.7 %copy-start = (f32[16]{0:T(128)S(1)}, f32[16]{0:T(128)}, u32[]{:S(2)}) copy-start(f32[16]{0:T(128)} %steps.3) | copy-start | bytes 196
  18.1 35.7 %all-to-all-start.1 = ((bf16[16,80,128]{2,1,0:T(8,128)(2,1)}), bf16[16,80,128]{2,1,0:T(8,128)(2,1)S(1)}, u32[]{:S(2)}, u32[]{:S(2)}) async-start(bf16[16,80,128]{2,1,0:T(8,128)(2,1)} %select.1.sent), calls=%async_computation.1 | async-start | bytes 655360 | tf_op jit(solution)/shard_map/all_to_all | solution.py:514
  67.2 24.8 %copy-start.1 = (f32[1,64,128]{2,1,0:T(8,128)S(1)}, f32[1,64,128]{2,1,0:T(8,128)}, u32[]{:S(2)}) copy-start(f32[1,64,128]{2,1,0:T(8,128)} %latents.1) | copy-start | bytes 98308
  67.2 24.8 %all-to-all-start.2 = ((bf16[16,64,128]{2,1,0:T(8,128)(2,1)}), bf16[16,64,128]{2,1,0:T(8,128)(2,1)S(1)}, u32[]{:S(2)}, u32[]{:S(2)}) async-start(bf16[16,64,128]{2,1,0:T(8,128)(2,1)} %get-tuple-element.36), calls=%async_computation.2 | async-start | bytes 524288 | tf_op jit(solution)/shard_map/all_to_all | solution.py:523

commit v4 on v3

--- a/solution.py
+++ b/solution.py
@@ -125,10 +125,11 @@
 
 
 def outward_kernel(
-    steps, terms, w_final, w_proj, w_qkv, pieces, query_gain, key_gain, segments, sent,
-    outward, shifts, gram, cross, embedded, scales, gains, bias, member,
-    terms_v, w_final_v, w_proj_v, w_qkv_v, pieces_v, gains_v, segments_v, rows,
+    here, steps, terms, w_final, w_proj, w_in, w_qkv, pieces, query_gain, key_gain, segments, sent,
+    outward, shifts, gram, cross, embedded, scales, gains, bias, member, direct, earlier,
+    terms_v, w_final_v, w_proj_v, w_in_v, w_qkv_v, pieces_v, gains_v, segments_v, rows,
     outward_v, shifts_v, gram_v, cross_v, embedded_v, scales_v, gain_rows, bias_v, member_v,
+    direct_v, earlier_v,
     sems, out_sems,
 ):
     del sent
@@ -138,6 +139,7 @@
         [
             (terms, terms_v), (w_final, w_final_v), (w_proj, w_proj_v), (pieces, pieces_v),
             (query_gain, gains_v.at[0]), (key_gain, gains_v.at[1]), (segments, segments_v),
+            (w_in, w_in_v),
         ]
         + [(w_qkv.at[c], w_qkv_v.at[:, spans[c]]) for c in range(3)],
         sems,
@@ -175,6 +177,17 @@
     high, low = two_parts(moved)
     shift = dot(stack_rows(high, low), w_qkv_v[...])
     shifts_v[...] = shift[:times] + shift[times:]
+    final = w_final_v[...]
+    direct_v[...] = dot(final, w_in_v[...], NT)
+    past = jnp.zeros((1, terms_v.shape[2]), F32)
+    for t in range(times):
+        past = past + jnp.where(t < here[0], steps[t], 0.0) * terms_v[t, 0:1, :]
+    high = past.astype(BF16)
+    middle, low = two_parts(past - high.astype(F32))
+    parts = stack_rows(high, middle, low, jnp.zeros((5, terms_v.shape[2]), F32))
+    earlier_v[...] = jnp.broadcast_to(
+        jnp.sum(dot(final, parts, NT), axis=-1, keepdims=True), earlier_v.shape
+    )
     tokens = segments_v.shape[1]
     gain_rows[0] = jnp.broadcast_to(gains_v[0] * (head**-0.5 * LOG2E), (head, head)).T
     gain_rows[1] = jnp.broadcast_to(gains_v[1], (head, head)).T
@@ -187,7 +200,7 @@
         [
             (outward_v, outward), (shifts_v, shifts), (gram_v, gram), (cross_v, cross),
             (embedded_v, embedded), (scales_v, scales), (gain_rows, gains), (bias_v, bias),
-            (member_v, member),
+            (member_v, member), (direct_v, direct), (earlier_v, earlier),
         ],
         out_sems,
     )
@@ -205,31 +218,34 @@
 
 
 def heads_kernel(
-    here, arrived,
-    embedded_h, scales_h, w_in_h, w_qkv_h, shifts_h, gram_h, cross_h, member_h, gains_h, bias_h,
-    inward_h, outward_h, rest_h,
-    out, kept,
-    embedded, scales, w_in, w_qkv, shifts, gram, cross, member, gains, bias,
-    inward, outward, rest,
-    rows, staged, sems,
+    here, steps, arrived,
+    embedded_h, scales_h, w_in_h, w_final_h, w_qkv_h, shifts_h, gram_h, cross_h, member_h, gains_h,
+    bias_h, direct_h, earlier_h, inward_h, outward_h, rest_h,
+    out, residual,
+    embedded, scales, w_in, w_final, w_qkv, shifts, gram, cross, member, gains,
+    bias, direct, earlier, inward, outward, rest,
+    rows, residual_v, sems,
 ):
     times, chans, head = outward.shape
     count, tokens = member.shape
     wide = w_in.shape[1]
     spans = [slice(c * head, (c + 1) * head) for c in range(3)]
     copies = fetch(
-        [(embedded_h, embedded), (scales_h, scales), (w_in_h, w_in)]
+        [(embedded_h, embedded), (scales_h, scales), (w_in_h, w_in), (w_final_h, w_final)]
         + [(w_qkv_h.at[c], w_qkv.at[:, spans[c]]) for c in range(3)]
         + [
             (shifts_h, shifts), (gram_h, gram), (cross_h, cross), (member_h, member),
-            (gains_h, gains), (bias_h, bias), (inward_h, inward), (outward_h, outward),
-            (rest_h, rest), (arrived, kept),
+            (gains_h, gains), (bias_h, bias), (direct_h, direct), (earlier_h, earlier),
+            (inward_h, inward), (outward_h, outward), (rest_h, rest),
         ],
         sems,
     )
-    documents = centre(gather_documents(arrived, chans, count, wide // times))
-    for copy in copies[:3]:
-        copy.wait()
+    documents = gather_documents(arrived, chans, count, wide // times)
+    exact = stack_rows(documents, jnp.zeros_like(documents))
+    documents = centre(documents)
+    for copy in copies[:4]:
+        copy.wait()
+    narrow = dot(w_final[...], exact, NT)[:, :count]
     high, low = two_parts(documents)
     near = dot(stack_rows(high, low), w_in[...], NT)
     near = near[:count] + near[count:]
@@ -241,7 +257,7 @@
             powers.append(jnp.sum(row * row, axis=-1, keepdims=True))
             pair.append(row * scales[t + j : t + j + 1, :])
         rows[t * count : (t + 2) * count, :] = jnp.concatenate(pair, axis=0).astype(BF16)
-    for copy in copies[3:7]:
+    for copy in copies[4:8]:
         copy.wait()
     base = dot(rows[...], w_qkv[...])
     turned = []
@@ -252,9 +268,21 @@
         block.append(jnp.zeros((left, 3 * head), F32))
         turned.append(jnp.concatenate(block, axis=0).T.astype(BF16))
 
-    for copy in copies[7:-1]:
+    for copy in copies[8:]:
         copy.wait()
     belongs = member[...]
+    past, whole = jnp.zeros((chans, tokens), F32), 0.0
+    for t in range(times):
+        weight = jnp.where(t < here[0], steps[t], 0.0)
+        past = past + weight * arrived[t, :chans, :].astype(F32)
+        whole = whole + weight
+    highest = lax.Precision.HIGHEST
+    near_docs = dot(whole * narrow + earlier[...], belongs, NN, highest)
+    residual_v[...] = (
+        dot(direct[...], past, NN, highest) + near_docs + arrived[0, :chans, :].astype(F32)
+    )
+    last = pltpu.make_async_copy(residual_v, residual, sems.at[len(copies)])
+    last.start()
     scaled_low, rates = [], []
     for t in range(times):
         mixed = 2.0 * (near + cross[t : t + 1, :])
@@ -279,7 +307,7 @@
     total = jnp.where(here[0] == 0, rest[...], 0.0)
     empty = jnp.zeros((chans, tokens), BF16)
     for t in range(times):
-        staged[t] = total.astype(BF16)
+        out[t] = total.astype(BF16)
         half, j = divmod(t, 8)
         left = jnp.concatenate([inward[t // 2], turned[half]], axis=1)
         first = [scaled_low[t], empty] if t % 2 == 0 else [empty, scaled_low[t]]
@@ -300,51 +328,7 @@
         mass = jnp.sum(raised, axis=0, keepdims=True)
         attended = (dot(values, raised.astype(BF16)) * (1.0 / mass)).astype(BF16)
         total = total + dot(outward[t], attended)
-    last = pltpu.make_async_copy(staged, out, sems.at[len(copies)])
-    last.start()
-    copies[-1].wait()
     last.wait()
-
-
-def residual_kernel(
-    here, steps, kept, terms, w_in, w_final, member_h,
-    out,
-    arrived, terms_v, w_in_v, w_final_v, member, sems,
-):
-    times = terms_v.shape[0]
-    chans, wide = w_in_v.shape
-    count = member.shape[0]
-    copies = fetch(
-        [
-            (terms, terms_v), (w_in, w_in_v), (w_final, w_final_v), (kept, arrived),
-            (member_h, member),
-        ],
-        sems,
-    )
-    copies[3].wait()
-    copies[4].wait()
-    documents = gather_documents(arrived, chans, count, wide // times)
-    mixed = jnp.zeros(out.shape, F32)
-    weights, whole = [], 0.0
-    for t in range(times):
-        weights.append(jnp.where(t < here[0], steps[t], 0.0))
-        mixed = mixed + weights[t] * arrived[t, :chans, :].astype(F32)
-        whole = whole + weights[t]
-    copies[0].wait()
-    embedded = jnp.zeros((1, wide), F32)
-    for t in range(times):
-        embedded = embedded + weights[t] * terms_v[t, 0:1, :]
-    rows = embedded + whole * documents
-    high = rows.astype(BF16)
-    middle, low = two_parts(rows - high.astype(F32))
-    copies[1].wait()
-    copies[2].wait()
-    final = w_final_v[...]
-    narrow = dot(final, high, NT) + dot(final, middle, NT) + dot(final, low, NT)
-    direct = dot(final, w_in_v[...], NT)
-    highest = lax.Precision.HIGHEST
-    near = dot(direct, mixed, NN, highest) + dot(narrow, member[...], NN, highest)
-    out[...] = near + arrived[0, :chans, :].astype(F32)
 
 
 def fold_inward(w_in, terms, w_qkv, latents, pack_docs, documents):
@@ -401,7 +385,8 @@
 
 
 def fold_outward(
-    steps, terms, w_final, w_proj, w_qkv, pieces, query_gain, key_gain, segments, sent, count
+    here, steps, terms, w_final, w_proj, w_in, w_qkv, pieces, query_gain, key_gain, segments, sent,
+    count,
 ):
     times, wide = terms.shape[0], terms.shape[2]
     chans, head, tokens = w_final.shape[0], w_proj.shape[0], segments.shape[1]
@@ -415,16 +400,19 @@
         ((2, head, head), F32),
         ((tokens, tokens), F32),
         ((count, tokens), F32),
+        ((chans, chans), F32),
+        ((chans, count), F32),
     ]
     return pl.pallas_call(
         outward_kernel,
         out_shape=tuple(pltpu.HBM(*s) for s in shapes),
-        in_specs=[SMEM] + [HBM] * 9,
-        out_specs=(HBM,) * 9,
+        in_specs=[SMEM] * 2 + [HBM] * 10,
+        out_specs=(HBM,) * 11,
         scratch_shapes=[
             pltpu.VMEM(terms.shape, F32),
             pltpu.VMEM(w_final.shape, BF16),
             pltpu.VMEM(w_proj.shape, BF16),
+            pltpu.VMEM(w_in.shape, BF16),
             pltpu.VMEM((wide, 3 * head), BF16),
             pltpu.VMEM(pieces.shape, BF16),
             pltpu.VMEM((2,) + query_gain.shape, F32),
@@ -432,56 +420,38 @@
             pltpu.VMEM((2, 4 * chans, wide), BF16),
         ]
         + [pltpu.VMEM(*s) for s in shapes]
-        + [pltpu.SemaphoreType.DMA((10,)), pltpu.SemaphoreType.DMA((9,))],
+        + [pltpu.SemaphoreType.DMA((11,)), pltpu.SemaphoreType.DMA((11,))],
         compiler_params=PARAMS,
         name="fold_outward",
     )(
+        here,
         steps,
-        *pinned(terms, w_final, w_proj, w_qkv, pieces, query_gain, key_gain, segments, sent),
-    )
-
-
-def run_heads(here, arrived, embedded, scales, w_in, w_qkv, *rest):
+        *pinned(terms, w_final, w_proj, w_in, w_qkv, pieces, query_gain, key_gain, segments, sent),
+    )
+
+
+def run_heads(here, steps, arrived, embedded, scales, w_in, w_final, w_qkv, *rest):
     outward = rest[-2]
-    head = w_qkv.shape[2]
+    wide, head = w_qkv.shape[1:]
     rows = arrived.shape[0] * (arrived.shape[1] - outward.shape[1]) // 2
-    held = [
-        pltpu.VMEM(a.shape, a.dtype) for a in (embedded, scales, w_in)
-    ] + [pltpu.VMEM((w_qkv.shape[1], 3 * head), BF16)]
+    held = [pltpu.VMEM(a.shape, a.dtype) for a in (embedded, scales, w_in, w_final)]
+    held += [pltpu.VMEM((wide, 3 * head), BF16)]
     held += [pltpu.VMEM(a.shape, a.dtype) for a in rest]
+    block = rest[-1].shape
     return pl.pallas_call(
         heads_kernel,
-        out_shape=(pltpu.HBM(outward.shape, BF16), pltpu.HBM(arrived.shape, BF16)),
-        in_specs=[SMEM, VMEM] + [HBM] * 13,
-        out_specs=(HBM, HBM),
+        out_shape=(jax.ShapeDtypeStruct(outward.shape, BF16), pltpu.HBM(block, F32)),
+        in_specs=[SMEM, SMEM, VMEM] + [HBM] * (5 + len(rest)),
+        out_specs=(VMEM, HBM),
         scratch_shapes=held
         + [
-            pltpu.VMEM((rows, embedded.shape[1]), BF16),
-            pltpu.VMEM(outward.shape, BF16),
-            pltpu.SemaphoreType.DMA((17,)),
+            pltpu.VMEM((rows, wide), BF16),
+            pltpu.VMEM(block, F32),
+            pltpu.SemaphoreType.DMA((8 + len(rest),)),
         ],
         compiler_params=PARAMS,
         name="run_heads",
-    )(here, arrived, *pinned(embedded, scales, w_in, w_qkv, *rest))
-
-
-def residual(here, steps, kept, terms, w_in, w_final, member):
-    return pl.pallas_call(
-        residual_kernel,
-        out_shape=jax.ShapeDtypeStruct((w_in.shape[0], kept.shape[2]), F32),
-        in_specs=[SMEM] * 2 + [HBM] * 5,
-        out_specs=VMEM,
-        scratch_shapes=[
-            pltpu.VMEM(kept.shape, BF16),
-            pltpu.VMEM(terms.shape, F32),
-            pltpu.VMEM(w_in.shape, BF16),
-            pltpu.VMEM(w_final.shape, BF16),
-            pltpu.VMEM(member.shape, F32),
-            pltpu.SemaphoreType.DMA((5,)),
-        ],
-        compiler_params=PARAMS,
-        name="residual",
-    )(here, steps, *pinned(kept, terms, w_in, w_final, member))
+    )(here, steps, arrived, *pinned(embedded, scales, w_in, w_final, w_qkv, *rest))
 
 
 def local(
@@ -512,17 +482,18 @@
     )
     sent = select(table, pick, sent)
     arrived = lax.all_to_all(sent, "tm", 0, 0)
-    outward, shifts, gram, cross, embedded, scales, gains, bias, member = fold_outward(
-        step_sizes, time_terms, w_last, w_proj[0], w_heads, pieces, query_gain, key_gain,
-        segment_ids, sent, count,
-    )
-    sums, kept = run_heads(
-        place, arrived, embedded, scales, w_in, w_heads, shifts, gram, cross, member, gains, bias,
-        inward, outward, rest,
+    outward, shifts, gram, cross, embedded, scales, gains, bias, member, direct, earlier = (
+        fold_outward(
+            place, step_sizes, time_terms, w_last, w_proj[0], w_in, w_heads, pieces, query_gain,
+            key_gain, segment_ids, sent, count,
+        )
+    )
+    sums, residual = run_heads(
+        place, step_sizes, arrived, embedded, scales, w_in, w_last, w_heads, shifts, gram, cross,
+        member, gains, bias, direct, earlier, inward, outward, rest,
     )
     parts = lax.all_to_all(sums, "tm", 0, 0)
-    direct = residual(place, step_sizes, kept, time_terms, w_in, w_last, member)
-    before = direct + jnp.sum(parts.astype(F32), axis=0)
+    before = residual + jnp.sum(parts.astype(F32), axis=0)
     return jnp.where(here == 0, latents[0], before)[None]
 
 

time: 93.1 us -> 94.4 us (1.014)
  waiting for transfers between devices: 30.5 us -> 33.3 us
  Pallas kernels: 30.7 us -> 28.5 us
    all_to_all x1, waiting for transfers between devices: 15 us -> 18 us  [local(): parts = lax.all_to_all(sums, 'tm', 0, 0)]
    pallas_call x2 -> x1, Pallas kernels: 16.3 us -> 13.8 us  [run_heads(): pl.pallas_call(heads_kernel, out_shape=(jax.ShapeDtypeStruct(outward.shap...]
  transfers between devices with their start and end apart: 3 -> 3, of which waited for: 3 -> 3; matrix products, arithmetic and copies ran while one was open for 0% -> 0% of each run, Pallas kernels for 17% -> 14%
where the time goes in v4:
time: 94.4 us; the launch traced here: 93.9 us
  waiting for transfers between devices  33.3 us (35%)
  starting transfers between devices  29.3 us (31%)
  Pallas kernels  28.5 us (30%)
  other arithmetic  1.43 us (2%)
  local copies, waits for them, and re-layouts  1.37 us (1%)
    all_to_all x1, waiting for transfers between devices, local(): parts = lax.all_to_all(sums, 'tm', 0, 0)  18 us
    all_to_all x1, starting transfers between devices, local(): arrived = lax.all_to_all(sent, 'tm', 0, 0)  15.2 us
    all_to_all x1, waiting for transfers between devices, local(): arrived = lax.all_to_all(sent, 'tm', 0, 0)  14.1 us
    pallas_call x1, Pallas kernels, run_heads(): pl.pallas_call(heads_kernel, out_shape=(jax.ShapeDtypeStruct(outward.shap...  13.8 us
    all_to_all x1, starting transfers between devices, local(): table = lax.all_to_all(copies, 'req', 0, 0)  7.32 us
    all_to_all x1, starting transfers between devices, local(): parts = lax.all_to_all(sums, 'tm', 0, 0)  6.73 us
    pallas_call x1, Pallas kernels, fold_inward(): pl.pallas_call(inward_kernel, out_shape=tuple((pltpu.HBM(*s) for s in sha...  6.63 us
    pallas_call x1, Pallas kernels, fold_outward(): pl.pallas_call(outward_kernel, out_shape=tuple((pltpu.HBM(*s) for s in sh...  6.36 us
  transfers between devices with their start and end apart: 3, of which 3 were waited for; matrix products, arithmetic and copies ran while one was open for 0% of the time, Pallas kernels for 14%

profile of v4, /device:TPU:32, one launch (start us, length us, event | category | flops | bytes accessed | tf_op | source)
XLA Modules:
  0.0 93.9 jit_solution(10130309468057175247)
XLA Ops:
  0.0 1.4 %broadcast_in_dim.12 = bf16[32,8,192]{2,1,0:T(8,128)(2,1)} broadcast(bf16[8,192]{1,0:T(8,128)(2,1)} %param.15), dimensions={1,2} | broadcast | bytes 101376 | tf_op jit(solution)/shard_map/broadcast_in_dim | solution.py:478
  1.4 7.3 %all-to-all-start = ((bf16[32,8,192]{2,1,0:T(8,128)(2,1)}), bf16[32,8,192]{2,1,0:T(8,128)(2,1)S(1)}, u32[]{:S(2)}, u32[]{:S(2)}) async-start(bf16[32,8,192]{2,1,0:T(8,128)(2,1)} %broadcast_in_dim.12), calls=%async_computation | async-start | bytes 262144 | tf_op jit(solution)/shard_map/all_to_all | solution.py:479
  8.7 0.0 copy-start
  8.7 6.6 %fold_inward.1 = (bf16[8,384,128]{2,1,0:T(8,128)(2,1)}, bf16[128,3072]{1,0:T(8,128)(2,1)}, bf16[16,256]{1,0:T(8,128)(2,1)}, f32[64,128]{1,0:T(8,128)}, bf16[16,80,128]{2,1,0:T(8,128)(2,1)}) custom-call(bf16[64,3072]{1,0:T(8,128)(2,1)} %w_in_h.1, f32[16,4,3072]{2,1,0:T(4,128)} %terms.3, bf16[3,3072,128]{2,1,0:T(8,128)(2,1)} %bitcast.13, ...), custom_call_target="tpu_custom_call" | custom-call | tf_op jit(solution)/shard_map/fold_inward/pallas_call | solution.py:343
  15.3 1.2 %all-to-all-done.table = bf16[32,8,192]{2,1,0:T(8,128)(2,1)S(1)} async-done(((bf16[32,8,192]{2,1,0:T(8,128)(2,1)}), bf16[32,8,192]{2,1,0:T(8,128)(2,1)S(1)}, u32[]{:S(2)}, u32[]{:S(2)}) %all-to-all-start) | async-done | bytes 98336 | tf_op jit(solution)/shard_map/all_to_all | solution.py:479
  16.5 1.6 %select.1.sent = bf16[16,80,128]{2,1,0:T(8,128)(2,1)} custom-call(bf16[32,8,192]{2,1,0:T(8,128)(2,1)S(1)} %all-to-all-done.table, bf16[16,256]{1,0:T(8,128)(2,1)} %get-tuple-element.23.pick, bf16[16,80,128]{2,1,0:T(8,128)(2,1)} %get-tuple-element.24.sent), custom_call_target="tpu_custom_call", output_to_operand_aliasing={{}: (2, {})} | custom-call | tf_op jit(solution)/shard_map/select/pallas_call | solution.py:371
  18.1 15.2 %all-to-all-start.1 = ((bf16[16,80,128]{2,1,0:T(8,128)(2,1)}), bf16[16,80,128]{2,1,0:T(8,128)(2,1)S(1)}, u32[]{:S(2)}, u32[]{:S(2)}) async-start(bf16[16,80,128]{2,1,0:T(8,128)(2,1)} %select.1.sent), calls=%async_computation.1 | async-start | bytes 655360 | tf_op jit(solution)/shard_map/all_to_all | solution.py:484
  33.4 0.0 copy-done
  33.4 6.4 %fold_outward.1 = (bf16[16,64,128]{2,1,0:T(8,128)(2,1)}, f32[16,384]{1,0:T(8,128)}, bf16[128,64]{1,0:T(8,128)(2,1)}, f32[16,64]{1,0:T(8,128)}, f32[16,3072]{1,0:...) custom-call(s32[1]{0:T(128)} %bitcast.1.here, ...), custom_call_target="tpu_custom_call" | custom-call | tf_op jit(solution)/shard_map/fold_outward/pallas_call | solution.py:406
  39.7 14.1 %all-to-all-done.1.arrived = bf16[16,80,128]{2,1,0:T(8,128)(2,1)S(1)} async-done(((bf16[16,80,128]{2,1,0:T(8,128)(2,1)}), bf16[16,80,128]{2,1,0:T(8,128)(2,1)S(1)}, u32[]{:S(2)}, u32[]{:S(2)}) %all-to-all-start.1) | async-done | bytes 327712 | tf_op jit(solution)/shard_map/all_to_all | solution.py:484
  53.9 0.0 copy-start.1
  53.9 13.8 %run_heads.1 = (bf16[16,64,128]{2,1,0:T(8,128)(2,1)}, f32[64,128]{1,0:T(8,128)}) custom-call(s32[1]{0:T(128)} %bitcast.1.here, f32[16]{0:T(128)S(1)} %copy-done, bf16[16,80,128]{2,1,0:T(8,128)(2,1)S(1)} %all-to-all-done.1.arrived, f32[16,3072]{1,0:T(8,128)} %get-tuple-element.26.embedded_h, f32[16,3072]{1,0:T(8,128)} %get-tuple-element.27.scales_h, ...), custom_call_target="tpu_custom_call" | custom-call | tf_op jit(solution)/shard_map/run_heads/pallas_call | solution.py:441
  67.7 6.7 %all-to-all-start.2 = ((bf16[16,64,128]{2,1,0:T(8,128)(2,1)}), bf16[16,64,128]{2,1,0:T(8,128)(2,1)S(1)}, u32[]{:S(2)}, u32[]{:S(2)}) async-start(bf16[16,64,128]{2,1,0:T(8,128)(2,1)} %get-tuple-element.40), calls=%async_computation.2 | async-start | bytes 524288 | tf_op jit(solution)/shard_map/all_to_all | solution.py:495
  74.5 18.0 %all-to-all-done.2 = bf16[16,64,128]{2,1,0:T(8,128)(2,1)S(1)} async-done(((bf16[16,64,128]{2,1,0:T(8,128)(2,1)}), bf16[16,64,128]{2,1,0:T(8,128)(2,1)S(1)}, u32[]{:S(2)}, u32[]{:S(2)}) %all-to-all-start.2) | async-done | bytes 262176 | tf_op jit(solution)/shard_map/all_to_all | solution.py:495
  92.5 0.0 copy-done.1
  92.5 1.4 %fusion = f32[1,64,128]{2,1,0:T(8,128)} fusion(f32[1,64,128]{2,1,0:T(8,128)S(1)} %copy-done.1, f32[64,128]{1,0:T(8,128)} %get-tuple-element.39, f32[64,128]{1,0:T(8,128)S(1)} %convert_reduce_fusion, pred[]{:T(512)S(6)} %eq.3), kind=kLoop, calls=%fused_computation.2 | loop fusion | flops 16384 | bytes 131073 | tf_op jit(solution)/shard_map/broadcast_in_dim | solution.py:497
  (1 shorter events, 0.0 us)
Async XLA Ops:
  1.4 15.1 %all-to-all-start = ((bf16[32,8,192]{2,1,0:T(8,128)(2,1)}), bf16[32,8,192]{2,1,0:T(8,128)(2,1)S(1)}, u32[]{:S(2)}, u32[]{:S(2)}) async-start(bf16[32,8,192]{2,1,0:T(8,128)(2,1)} %broadcast_in_dim.12), calls=%async_computation | async-start | bytes 262144 | tf_op jit(solution)/shard_map/all_to_all | solution.py:479
  8.7 24.7 %copy-start = (f32[16]{0:T(128)S(1)}, f32[16]{0:T(128)}, u32[]{:S(2)}) copy-start(f32[16]{0:T(128)} %steps.3) | copy-start | bytes 196
  18.1 35.7 %all-to-all-start.1 = ((bf16[16,80,128]{2,1,0:T(8,128)(2,1)}), bf16[16,80,128]{2,1,0:T(8,128)(2,1)S(1)}, u32[]{:S(2)}, u32[]{:S(2)}) async-start(bf16[16,80,128]{2,1,0:T(8,128)(2,1)} %select.1.sent), calls=%async_computation.1 | async-start | bytes 655360 | tf_op jit(solution)/shard_map/all_to_all | solution.py:484
  53.9 38.7 %copy-start.1 = (f32[1,64,128]{2,1,0:T(8,128)S(1)}, f32[1,64,128]{2,1,0:T(8,128)}, u32[]{:S(2)}) copy-start(f32[1,64,128]{2,1,0:T(8,128)} %latents.1) | copy-start | bytes 98308
  67.7 24.8 %all-to-all-start.2 = ((bf16[16,64,128]{2,1,0:T(8,128)(2,1)}), bf16[16,64,128]{2,1,0:T(8,128)(2,1)S(1)}, u32[]{:S(2)}, u32[]{:S(2)}) async-start(bf16[16,64,128]{2,1,0:T(8,128)(2,1)} %get-tuple-element.40), calls=%async_computation.2 | async-start | bytes 524288 | tf_op jit(solution)/shard_map/all_to_all | solution.py:495

commit v5 on v4

v5 whole, which is shorter than its diff:
```python
import jax
import jax.numpy as jnp
from jax import lax
from jax.experimental import pallas as pl
from jax.experimental.pallas import tpu as pltpu
from jax.sharding import PartitionSpec as P

EPS = 1e-06
MASKED = -1e30
LOG2E = 1.4426950408889634
BF16, F32 = jnp.bfloat16, jnp.float32
NN = (((1,), (0,)), ((), ()))
NT = (((1,), (1,)), ((), ()))
VMEM = pl.BlockSpec(memory_space=pltpu.VMEM)
SMEM = pl.BlockSpec(memory_space=pltpu.SMEM)
HBM = pl.BlockSpec(memory_space=pltpu.HBM)
PARAMS = pltpu.CompilerParams(vmem_limit_bytes=24 * 2**20)


def dot(left, right, dims=NN, precision=None):
    return lax.dot_general(left, right, dims, precision=precision, preferred_element_type=F32)


def two_parts(values):
    high = values.astype(BF16)
    return high, (values - high.astype(F32)).astype(BF16)


def stack_rows(*parts):
    return jnp.concatenate([p.astype(F32) for p in parts], axis=0).astype(BF16)


def centre(values):
    return values - jnp.mean(values, axis=-1, keepdims=True)


def pinned(*arrays):
    return tuple(pltpu.with_memory_space_constraint(a, pltpu.HBM) for a in arrays)


def fetch(pairs, sems):
    copies = [pltpu.make_async_copy(a, b, sems.at[i]) for i, (a, b) in enumerate(pairs)]
    for copy in copies:
        copy.start()
    return copies


def pack_kernel(
    latents, pack_docs,
    pick, rest, sent,
    latents_v, packs_v, pick_v, rest_v, lowered_v, sems, out_sems,
):
    times, chans = sent.shape[0], latents_v.shape[1]
    copies = fetch([(latents, latents_v), (pack_docs, packs_v)], sems)
    copies[0].wait()
    values = latents_v[0]
    high = values.astype(BF16)
    lowered_v[...] = high
    rest_v[...] = values - high.astype(F32)
    copies[1].wait()
    count = packs_v.shape[1]
    column = jnp.broadcast_to(packs_v[...].astype(F32), (count, count))
    eye = lax.broadcasted_iota(jnp.int32, (count, count), 0) == lax.broadcasted_iota(
        jnp.int32, (count, count), 1
    )
    column = jnp.sum(jnp.where(eye, column, 0.0), axis=1, keepdims=True)
    places = lax.broadcasted_iota(jnp.int32, (count, pick.shape[1]), 1).astype(F32)
    chosen = jnp.where(places == column, 1.0, 0.0)
    pick_v[...] = stack_rows(chosen, jnp.zeros_like(chosen))
    left = fetch(
        [(rest_v, rest), (pick_v, pick)]
        + [(lowered_v, sent.at[i, pl.ds(0, chans)]) for i in range(times)],
        out_sems,
    )
    for copy in left:
        copy.wait()


def select_kernel(table, pick, sent, out, pick_v, staged, sems):
    del sent
    size, rows, lanes = out.shape
    owners, count, piece = table.shape
    fetch([(pick, pick_v)], sems.at[pl.ds(size, 1)])[0].wait()
    chosen = dot(pick_v[...], table[...].reshape(owners * count, piece))[:count]
    tail = jnp.concatenate(
        [chosen[:, lanes:], jnp.zeros((count, 2 * lanes - piece), F32)], axis=1
    )
    staged[...] = stack_rows(chosen[:, :lanes], tail)
    head = rows - 2 * count
    copies = fetch([(staged, out.at[i, pl.ds(head, 2 * count)]) for i in range(size)], sems)
    for copy in copies:
        copy.wait()


def small_rows(times, chans, head, tokens, count):
    sizes = [
        ("query_gain", head), ("key_gain", head), ("bias", tokens), ("member", count),
        ("direct", chans), ("earlier", chans), ("cross", times), ("shifts", 3 * times),
    ]
    places, at = {}, 0
    for name, rows in sizes:
        places[name] = (at, at + rows)
        at += rows
    return places, at


def weights_kernel(
    here, steps, terms, w_in, w_qkv, w_final, w_proj, query_gain, key_gain, segments, sent,
    inward, outward, lines, gram, small,
    terms_v, w_in_v, w_qkv_v, w_final_v, w_proj_v, gains_v, segments_v,
    centred, pieces, rows, inward_v, outward_v, lines_v, gram_v, small_v, sems, out_sems,
):
    del sent
    times, chans, head = outward.shape
    tokens, count = segments_v.shape[1], 8
    wide = w_in_v.shape[1]
    places, _ = small_rows(times, chans, head, tokens, count)
    copies = fetch(
        [
            (w_in, w_in_v), (terms, terms_v), (w_qkv, w_qkv_v), (w_final, w_final_v),
            (w_proj, w_proj_v), (query_gain, gains_v.at[0]), (key_gain, gains_v.at[1]),
            (segments, segments_v),
        ],
        sems,
    )
    copies[0].wait()
    centred[...] = centre(w_in_v[...].astype(F32))
    high, low = two_parts(centred[...])
    pieces[:chans, :] = high
    pieces[chans:, :] = low
    copies[1].wait()
    left = []
    for step in range(times // 4):
        for j in range(4):
            scaled = centred[...] * (1.0 + terms_v[step * 4 + j, 2:3, :])
            rows[step % 2, j * chans : (j + 1) * chans, :] = scaled.astype(BF16)
        if step == 0:
            copies[2].wait()
        for c in range(3):
            turned = dot(rows[step % 2], w_qkv_v[c]).T.astype(BF16)
            inward_v[2 * step, c * head : (c + 1) * head, :] = turned[:, : 2 * chans]
            inward_v[2 * step + 1, c * head : (c + 1) * head, :] = turned[:, 2 * chans :]
    left += fetch([(inward_v, inward)], out_sems)
    copies[3].wait()
    copies[4].wait()
    for step in range(times // 4):
        for j in range(4):
            gated = w_final_v[...].astype(F32) * terms_v[step * 4 + j, 3:4, :]
            rows[step % 2, j * chans : (j + 1) * chans, :] = gated.astype(BF16)
        back = dot(rows[step % 2], w_proj_v[...], NT)
        for j in range(4):
            t = step * 4 + j
            outward_v[t] = (back[j * chans : (j + 1) * chans] * steps[t]).astype(BF16)
    left += fetch([(outward_v, outward)], out_sems.at[pl.ds(1, 1)])
    moved, means = [], []
    past = jnp.zeros((1, wide), F32)
    for t in range(times):
        moved.append(terms_v[t, 1:2, :])
        means.append(centre(terms_v[t, 0:1, :]))
        lines_v[times + t : times + t + 1, :] = 1.0 + terms_v[t, 2:3, :]
        past = past + jnp.where(t < here[0], steps[t], 0.0) * terms_v[t, 0:1, :]
    moved, means = jnp.concatenate(moved, axis=0), jnp.concatenate(means, axis=0)
    lines_v[:times, :] = means
    left += fetch([(lines_v, lines)], out_sems.at[pl.ds(2, 1)])

    def put(name, values):
        first, last = places[name]
        small_v[first:last, :] = jnp.concatenate(
            [values, jnp.zeros((values.shape[0], small_v.shape[1] - values.shape[1]), F32)], axis=1
        ) if values.shape[1] < small_v.shape[1] else values

    both = pieces[...]
    square = dot(both, both, NT)
    square = square[:chans, :chans] + square[chans:, :chans] + square[:chans, chans:]
    high, low = two_parts(square)
    gram_v[:chans, :] = high
    gram_v[chans:, :] = low
    left += fetch([(gram_v, gram)], out_sems.at[pl.ds(3, 1)])
    high, low = two_parts(means)
    mixed = dot(stack_rows(high, low), both, NT)
    put("cross", mixed[:times, :chans] + mixed[times:, :chans] + mixed[:times, chans:])
    high, low = two_parts(moved)
    split = stack_rows(high, low)
    shifts = []
    for c in range(3):
        shift = dot(split, w_qkv_v[c])
        shifts.append(shift[:times] + shift[times:])
    put("shifts", jnp.concatenate(shifts, axis=0))
    final = w_final_v[...]
    put("direct", dot(final, w_in_v[...], NT))
    high = past.astype(BF16)
    middle, low = two_parts(past - high.astype(F32))
    parts = stack_rows(high, middle, low, jnp.zeros((5, wide), F32))
    earlier = jnp.sum(dot(final, parts, NT), axis=-1, keepdims=True)
    put("earlier", jnp.broadcast_to(earlier, (chans, small_v.shape[1])))
    for copy in copies[5:]:
        copy.wait()
    put("query_gain", jnp.broadcast_to(gains_v[0] * (head**-0.5 * LOG2E), (head, head)).T)
    put("key_gain", jnp.broadcast_to(gains_v[1], (head, head)).T)
    ids = jnp.broadcast_to(segments_v[...].astype(F32), (tokens, tokens))
    put("bias", jnp.where(ids == ids.T, 0.0, MASKED))
    numbers = lax.broadcasted_iota(jnp.int32, (count, tokens), 0).astype(F32)
    put("member", jnp.where(numbers == ids[:count], 1.0, 0.0))
    left += fetch([(small_v, small)], out_sems.at[pl.ds(4, 1)])
    for copy in left:
        copy.wait()


def gather_documents(arrived, chans, count, piece):
    parts = []
    for i in range(arrived.shape[0]):
        block = arrived[i, chans:, :].astype(F32)
        parts.append(block[:count])
        parts.append(block[count:, : piece - block.shape[1]])
    return jnp.concatenate(parts, axis=1)


def heads_kernel(
    here, steps, arrived,
    lines_h, w_in_h, w_final_h, w_qkv_h, gram_h, small_h, inward_h, outward_h, rest_h,
    out, residual,
    lines, w_in, w_final, w_qkv, gram, small, inward, outward, rest,
    rows, residual_v, queries, keys, values, raised, mass, attended, sems,
):
    times, chans, head = outward.shape
    tokens = arrived.shape[2]
    count = (arrived.shape[1] - chans) // 2
    wide = w_in.shape[1]
    places, _ = small_rows(times, chans, head, tokens, count)
    copies = fetch(
        [
            (lines_h, lines), (w_in_h, w_in), (w_final_h, w_final), (w_qkv_h, w_qkv),
            (gram_h, gram), (small_h, small), (inward_h, inward), (outward_h, outward),
            (rest_h, rest),
        ],
        sems,
    )

    def table(name, lanes=None):
        first, last = places[name]
        return small[first:last, :lanes]

    documents = gather_documents(arrived, chans, count, wide // times)
    exact = stack_rows(documents, jnp.zeros_like(documents))
    documents = centre(documents)
    copies[0].wait()
    powers = []
    for t in range(0, times, 2):
        pair = []
        for j in range(2):
            row = documents + lines[t + j : t + j + 1, :]
            powers.append(jnp.sum(row * row, axis=-1, keepdims=True))
            pair.append(row * lines[times + t + j : times + t + j + 1, :])
        rows[t * count : (t + 2) * count, :] = jnp.concatenate(pair, axis=0).astype(BF16)
    copies[1].wait()
    copies[2].wait()
    narrow = dot(w_final[...], exact, NT)[:, :count]
    high, low = two_parts(documents)
    near = dot(stack_rows(high, low), w_in[...], NT)
    near = near[:count] + near[count:]
    copies[3].wait()
    base = jnp.concatenate([dot(rows[...], w_qkv[c]) for c in range(3)], axis=1)
    for copy in copies[4:]:
        copy.wait()
    shifts = table("shifts")
    shifts = jnp.concatenate([shifts[c * times : (c + 1) * times] for c in range(3)], axis=1)
    turned = []
    for half in range(2):
        span = slice(half * 8 * count, (half + 1) * 8 * count)
        block = [base[span], shifts[half * 8 : (half + 1) * 8, :]]
        left = head - 8 * count - 8
        block.append(jnp.zeros((left, 3 * head), F32))
        turned.append(jnp.concatenate(block, axis=0).T.astype(BF16))

    belongs = table("member")
    cross = table("cross", chans)
    past, whole = jnp.zeros((chans, tokens), F32), 0.0
    for t in range(times):
        weight = jnp.where(t < here[0], steps[t], 0.0)
        past = past + weight * arrived[t, :chans, :].astype(F32)
        whole = whole + weight
    highest = lax.Precision.HIGHEST
    near_docs = dot(whole * narrow + table("earlier", count), belongs, NN, highest)
    first_rest = jnp.where(here[0] == 0, rest[...], 0.0)
    residual_v[...] = (
        dot(table("direct", chans), past, NN, highest)
        + near_docs
        + arrived[0, :chans, :].astype(F32)
        + first_rest
    )
    last = pltpu.make_async_copy(residual_v, residual, sems.at[len(copies)])
    last.start()

    scaled_low, rates = [], []
    for t in range(times):
        mixed = 2.0 * (near + cross[t : t + 1, :])
        high, low = two_parts(mixed)
        left = jnp.concatenate([gram[...], stack_rows(high, low)], axis=0)
        block = arrived[t, :chans, :]
        product = dot(left, block)
        both = product[:chans] + product[chans : 2 * chans]
        block = block.astype(F32)
        other = product[2 * chans : 2 * chans + count] + product[2 * chans + count :]
        spread = jnp.sum(both * block, axis=0, keepdims=True) + jnp.sum(
            belongs * (other + powers[t]), axis=0, keepdims=True
        )
        rate = lax.rsqrt(spread / wide + EPS)
        rates.append(rate)
        scaled_low.append((block * rate).astype(BF16))

    def unit(block, gain):
        power = jnp.mean(block * block, axis=0, keepdims=True)
        return block * (lax.rsqrt(power + EPS) * gain)

    empty = jnp.zeros((chans, tokens), BF16)
    for t in range(times):
        half, j = divmod(t, 8)
        left = jnp.concatenate([inward[t // 2], turned[half]], axis=1)
        first = [scaled_low[t], empty] if t % 2 == 0 else [empty, scaled_low[t]]
        ones = lax.broadcasted_iota(jnp.int32, (8, tokens), 0) == j
        second = [jnp.zeros((j * count, tokens), F32)] if j else []
        second.append(belongs * rates[t])
        if j < 7:
            second.append(jnp.zeros(((7 - j) * count, tokens), F32))
        second.append(jnp.where(ones, 1.0, 0.0))
        second.append(jnp.zeros((head - 8 * count - 8, tokens), F32))
        second = jnp.concatenate(second, axis=0).astype(BF16)
        right = jnp.concatenate(first + [second], axis=0)
        queries[t] = unit(dot(left[:head], right), table("query_gain")).astype(BF16)
        keys[t] = unit(dot(left[head : 2 * head], right), table("key_gain")).T.astype(BF16)
        values[t] = dot(left[2 * head :], right).astype(BF16)
    for t in range(times):
        scores = dot(keys[t], queries[t]) + table("bias")
        powered = jnp.exp2(scores - jnp.max(scores, axis=0, keepdims=True))
        mass[t : t + 1, :] = 1.0 / jnp.sum(powered, axis=0, keepdims=True)
        raised[t] = powered.astype(BF16)
    for t in range(times):
        attended[t] = (dot(values[t], raised[t]) * mass[t : t + 1, :]).astype(BF16)
    out[0] = jnp.zeros((chans, tokens), BF16)
    total = first_rest
    for t in range(times - 1):
        total = total + dot(outward[t], attended[t])
        out[t + 1] = total.astype(BF16)
    last.wait()


def pack(latents, pack_docs, documents, times):
    block, count = latents.shape[1:], pack_docs.shape[1]
    return pl.pallas_call(
        pack_kernel,
        out_shape=(
            pltpu.HBM((2 * count, documents), BF16),
            pltpu.HBM(block, F32),
            pltpu.HBM((times, block[0] + 2 * count, block[1]), BF16),
        ),
        in_specs=[HBM] * 2,
        out_specs=(HBM,) * 3,
        scratch_shapes=[
            pltpu.VMEM(latents.shape, F32),
            pltpu.VMEM(pack_docs.shape, jnp.int32),
            pltpu.VMEM((2 * count, documents), BF16),
            pltpu.VMEM(block, F32),
            pltpu.VMEM(block, BF16),
            pltpu.SemaphoreType.DMA((2,)),
            pltpu.SemaphoreType.DMA((2 + times,)),
        ],
        compiler_params=PARAMS,
        name="pack",
    )(*pinned(latents, pack_docs))


def select(table, pick, sent):
    size = sent.shape[0]
    return pl.pallas_call(
        select_kernel,
        out_shape=pltpu.HBM(sent.shape, BF16),
        in_specs=[VMEM, HBM, HBM],
        out_specs=HBM,
        scratch_shapes=[
            pltpu.VMEM(pick.shape, BF16),
            pltpu.VMEM((pick.shape[0], sent.shape[2]), BF16),
            pltpu.SemaphoreType.DMA((size + 1,)),
        ],
        input_output_aliases={2: 0},
        compiler_params=PARAMS,
        name="select",
    )(table, *pinned(pick, sent))


def fold_weights(
    here, steps, terms, w_in, w_qkv, w_final, w_proj, query_gain, key_gain, segments, sent
):
    times, wide = terms.shape[0], terms.shape[2]
    chans, head, tokens = w_final.shape[0], w_proj.shape[0], segments.shape[1]
    count = (sent.shape[1] - chans) // 2
    shapes = [
        ((times // 2, 3 * head, 2 * chans), BF16),
        ((times, chans, head), BF16),
        ((2 * times, wide), F32),
        ((2 * chans, chans), BF16),
        ((small_rows(times, chans, head, tokens, count)[1], tokens), F32),
    ]
    return pl.pallas_call(
        weights_kernel,
        out_shape=tuple(pltpu.HBM(*s) for s in shapes),
        in_specs=[SMEM] * 2 + [HBM] * 9,
        out_specs=(HBM,) * 5,
        scratch_shapes=[
            pltpu.VMEM(a.shape, a.dtype) for a in (terms, w_in, w_qkv, w_final, w_proj)
        ]
        + [
            pltpu.VMEM((2,) + query_gain.shape, F32),
            pltpu.VMEM(segments.shape, jnp.int32),
            pltpu.VMEM((chans, wide), F32),
            pltpu.VMEM((2 * chans, wide), BF16),
            pltpu.VMEM((2, 4 * chans, wide), BF16),
        ]
        + [pltpu.VMEM(*s) for s in shapes]
        + [pltpu.SemaphoreType.DMA((8,)), pltpu.SemaphoreType.DMA((5,))],
        compiler_params=PARAMS,
        name="fold_weights",
    )(
        here,
        steps,
        *pinned(terms, w_in, w_qkv, w_final, w_proj, query_gain, key_gain, segments, sent),
    )


def run_heads(here, steps, arrived, *operands):
    outward, rest = operands[-2:]
    times, chans, head = outward.shape
    tokens = arrived.shape[2]
    rows = times * (arrived.shape[1] - chans) // 2
    wide = operands[0].shape[1]
    square = pltpu.VMEM((times, head, tokens), BF16)
    return pl.pallas_call(
        heads_kernel,
        out_shape=(jax.ShapeDtypeStruct(outward.shape, BF16), pltpu.HBM(rest.shape, F32)),
        in_specs=[SMEM, SMEM, VMEM] + [HBM] * len(operands),
        out_specs=(VMEM, HBM),
        scratch_shapes=[pltpu.VMEM(a.shape, a.dtype) for a in operands]
        + [
            pltpu.VMEM((rows, wide), BF16),
            pltpu.VMEM(rest.shape, F32),
            square, square, square, square,
            pltpu.VMEM((times, tokens), F32),
            square,
            pltpu.SemaphoreType.DMA((1 + len(operands),)),
        ],
        compiler_params=PARAMS,
        name="run_heads",
    )(here, steps, arrived, *pinned(*operands))


def local(
    latents,
    time_terms,
    step_sizes,
    doc_embed,
    pack_docs,
    segment_ids,
    w_in,
    w_qkv,
    query_gain,
    key_gain,
    w_proj,
    w_final,
):
    here = lax.axis_index("tm")
    place = here.astype(jnp.int32).reshape(1)
    times, owners = lax.axis_size("tm"), lax.axis_size("req")
    count, piece = doc_embed.shape
    w_heads = w_qkv[:, :, 0, :].transpose(1, 0, 2)
    w_last = w_final.T

    copies = jnp.broadcast_to(doc_embed[None], (owners, count, piece))
    table = lax.all_to_all(copies, "req", 0, 0)
    pick, rest, sent = pack(latents, pack_docs[None], owners * count, times)
    sent = select(table, pick, sent)
    arrived = lax.all_to_all(sent, "tm", 0, 0)
    inward, outward, lines, gram, small = fold_weights(
        place, step_sizes, time_terms, w_in, w_heads, w_last, w_proj[0], query_gain, key_gain,
        segment_ids, sent,
    )
    sums, residual = run_heads(
        place, step_sizes, arrived, lines, w_in, w_last, w_heads, gram, small, inward, outward,
        rest,
    )
    parts = lax.all_to_all(sums, "tm", 0, 0)
    return (residual + jnp.sum(parts.astype(F32), axis=0))[None]


def solution(mesh):
    in_specs = (
        P("tm", None, "req"),
        P(),
        P(),
        P("req", "tm"),
        P("req"),
        P("req", None),
        P(),
        P(None, None, "tm", None),
        P("tm", None),
        P("tm", None),
        P("tm", None, None),
        P(),
    )
    out_specs = P("tm", None, "req")
    return jax.shard_map(local, mesh=mesh, in_specs=in_specs, out_specs=out_specs, check_vma=False)
```

time: 94.4 us -> 85.8 us (0.909)
  blocking collectives: 0 us -> 24.6 us
  waiting for transfers between devices: 33.3 us -> 14.4 us
  Pallas kernels: 28.5 us -> 20.3 us
  starting transfers between devices: 29.3 us -> 22.5 us
    all_to_all x0 -> x1, blocking collectives: none -> 24.6 us  [local(): parts = lax.all_to_all(sums, 'tm', 0, 0)]
    all_to_all x1 -> x0, waiting for transfers between devices: 18 us -> none  [local(): parts = lax.all_to_all(sums, 'tm', 0, 0)]
    pallas_call x1, Pallas kernels: 13.8 us -> 5.41 us  [run_heads(): pl.pallas_call(heads_kernel, out_shape=(jax.ShapeDtypeStruct(outward.shap...]
    all_to_all x1 -> x0, starting transfers between devices: 6.73 us -> none  [local(): parts = lax.all_to_all(sums, 'tm', 0, 0)]
    all_to_all x1, waiting for transfers between devices: 14.1 us -> 8.32 us  [local(): arrived = lax.all_to_all(sent, 'tm', 0, 0)]
    all_to_all x1, waiting for transfers between devices: 1.15 us -> 6.08 us  [local(): table = lax.all_to_all(copies, 'req', 0, 0)]
  transfers between devices with their start and end apart: 3 -> 2, of which waited for: 3 -> 2; matrix products, arithmetic and copies ran while one was open for 0% -> 0% of each run, Pallas kernels for 14% -> 16%
where the time goes in v5:
time: 85.8 us; the launch traced here: 85.3 us
  blocking collectives  24.6 us (29%)
  starting transfers between devices  22.5 us (26%)
  Pallas kernels  20.3 us (24%)
  waiting for transfers between devices  14.4 us (17%)
  local copies, waits for them, and re-layouts  2 us (2%)
  other arithmetic  1.42 us (2%)
    all_to_all x1, blocking collectives, local(): parts = lax.all_to_all(sums, 'tm', 0, 0)  24.6 us
    all_to_all x1, starting transfers between devices, local(): arrived = lax.all_to_all(sent, 'tm', 0, 0)  15.2 us
    pallas_call x1, Pallas kernels, fold_weights(): pl.pallas_call(weights_kernel, out_shape=tuple((pltpu.HBM(*s) for s in sh...  11.5 us
    all_to_all x1, waiting for transfers between devices, local(): arrived = lax.all_to_all(sent, 'tm', 0, 0)  8.32 us
    all_to_all x1, starting transfers between devices, local(): table = lax.all_to_all(copies, 'req', 0, 0)  7.32 us
    all_to_all x1, waiting for transfers between devices, local(): table = lax.all_to_all(copies, 'req', 0, 0)  6.08 us
    pallas_call x1, Pallas kernels, run_heads(): pl.pallas_call(heads_kernel, out_shape=(jax.ShapeDtypeStruct(outward.shap...  5.41 us
  transfers between devices with their start and end apart: 2, of which 2 were waited for; matrix products, arithmetic and copies ran while one was open for 0% of the time, Pallas kernels for 16%

profile of v5, /device:TPU:32, one launch (start us, length us, event | category | flops | bytes accessed | tf_op | source)
XLA Modules:
  0.0 85.3 jit_solution(13711340098984564641)
XLA Ops:
  0.0 1.3 %broadcast_in_dim.12 = bf16[32,8,192]{2,1,0:T(8,128)(2,1)} broadcast(bf16[8,192]{1,0:T(8,128)(2,1)} %param.15), dimensions={1,2} | broadcast | bytes 101376 | tf_op jit(solution)/shard_map/broadcast_in_dim | solution.py:476
  1.3 7.3 %all-to-all-start = ((bf16[32,8,192]{2,1,0:T(8,128)(2,1)}), bf16[32,8,192]{2,1,0:T(8,128)(2,1)S(1)}, u32[]{:S(2)}, u32[]{:S(2)}) async-start(bf16[32,8,192]{2,1,0:T(8,128)(2,1)} %broadcast_in_dim.12), calls=%async_computation | async-start | bytes 262144 | tf_op jit(solution)/shard_map/all_to_all | solution.py:477
  8.7 1.7 %pack.1 = (bf16[16,256]{1,0:T(8,128)(2,1)}, f32[64,128]{1,0:T(8,128)}, bf16[16,80,128]{2,1,0:T(8,128)(2,1)}) custom-call(f32[1,64,128]{2,1,0:T(8,128)} %latents.1, s32[1,8]{1,0:T(1,128)} %bitcast.14), custom_call_target="tpu_custom_call" | custom-call | tf_op jit(solution)/shard_map/pack/pallas_call | solution.py:349
  10.4 6.1 %all-to-all-done.table = bf16[32,8,192]{2,1,0:T(8,128)(2,1)S(1)} async-done(((bf16[32,8,192]{2,1,0:T(8,128)(2,1)}), bf16[32,8,192]{2,1,0:T(8,128)(2,1)S(1)}, u32[]{:S(2)}, u32[]{:S(2)}) %all-to-all-start) | async-done | bytes 98336 | tf_op jit(solution)/shard_map/all_to_all | solution.py:477
  16.5 1.7 %select.1.sent = bf16[16,80,128]{2,1,0:T(8,128)(2,1)} custom-call(bf16[32,8,192]{2,1,0:T(8,128)(2,1)S(1)} %all-to-all-done.table, bf16[16,256]{1,0:T(8,128)(2,1)} %get-tuple-element.15.pick, bf16[16,80,128]{2,1,0:T(8,128)(2,1)} %get-tuple-element.16.sent), custom_call_target="tpu_custom_call", output_to_operand_aliasing={{}: (2, {})} | custom-call | tf_op jit(solution)/shard_map/select/pallas_call | solution.py:374
  18.1 15.2 %all-to-all-start.1 = ((bf16[16,80,128]{2,1,0:T(8,128)(2,1)}), bf16[16,80,128]{2,1,0:T(8,128)(2,1)S(1)}, u32[]{:S(2)}, u32[]{:S(2)}) async-start(bf16[16,80,128]{2,1,0:T(8,128)(2,1)} %select.1.sent), calls=%async_computation.1 | async-start | bytes 655360 | tf_op jit(solution)/shard_map/all_to_all | solution.py:480
  33.4 0.0 copy-start
  33.4 0.6 copy-done
  34.0 0.0 copy-start.1
  34.0 11.5 %fold_weights.1 = (bf16[8,384,128]{2,1,0:T(8,128)(2,1)}, bf16[16,64,128]{2,1,0:T(8,128)(2,1)}, f32[32,3072]{1,0:T(8,128)}, bf16[128,64]{1,0:T(8,128)(2,1)}, f32[584,128]{1,0:T(8,128)}) custom-call(s32[1]{0:T(128)} %bitcast.here, f32[16]{0:T(128)S(1)} %copy-done, f32[16,4,3072]{2,1,0:T(4,128)} %terms.1, bf16[64,3072]{1,0:T(8,128)(2,1)} %w_in_h.1, ...), custom_call_target="tpu_custom_call" | custom-call | tf_op jit(solution)/shard_map/fold_weights/pallas_call | solution.py:403
  45.6 8.3 %all-to-all-done.1.arrived = bf16[16,80,128]{2,1,0:T(8,128)(2,1)S(1)} async-done(((bf16[16,80,128]{2,1,0:T(8,128)(2,1)}), bf16[16,80,128]{2,1,0:T(8,128)(2,1)S(1)}, u32[]{:S(2)}, u32[]{:S(2)}) %all-to-all-start.1) | async-done | bytes 327712 | tf_op jit(solution)/shard_map/all_to_all | solution.py:480
  53.9 0.0 copy-done.1
  53.9 5.4 %run_heads.1 = (bf16[16,64,128]{2,1,0:T(8,128)(2,1)S(1)}, f32[64,128]{1,0:T(8,128)}) custom-call(s32[1]{0:T(128)} %bitcast.here, f32[16]{0:T(128)S(1)} %copy-done.1, bf16[16,80,128]{2,1,0:T(8,128)(2,1)S(1)} %all-to-all-done.1.arrived, f32[32,3072]{1,0:T(8,128)} %get-tuple-element.17.lines_h, bf16[64,3072]{1,0:T(8,128)(2,1)} %w_in_h.1, ...), custom_call_target="tpu_custom_call" | custom-call | tf_op jit(solution)/shard_map/run_heads/pallas_call | solution.py:436
  59.3 24.6 %all_to_all.15 = bf16[16,64,128]{2,1,0:T(8,128)(2,1)S(1)} all-to-all(bf16[16,64,128]{2,1,0:T(8,128)(2,1)S(1)} %get-tuple-element.24), channel_id=1, replica_groups=mesh['tm'=16,'req'=32] {'tm'}, dimensions={0} | all-to-all | bytes 524288 | tf_op jit(solution)/shard_map/all_to_all | solution.py:489
  83.9 1.4 %add_bitcast_fusion = f32[1,64,128]{2,1,0:T(8,128)} fusion(f32[64,128]{1,0:T(8,128)} %get-tuple-element.23, f32[64,128]{1,0:T(8,128)S(1)} %convert_reduce_fusion), kind=kLoop, calls=%fused_computation.1 | loop fusion | flops 8192 | bytes 98304 | tf_op jit(solution)/shard_map/broadcast_in_dim | solution.py:490
  (1 shorter events, 0.0 us)
Async XLA Ops:
  1.3 15.1 %all-to-all-start = ((bf16[32,8,192]{2,1,0:T(8,128)(2,1)}), bf16[32,8,192]{2,1,0:T(8,128)(2,1)S(1)}, u32[]{:S(2)}, u32[]{:S(2)}) async-start(bf16[32,8,192]{2,1,0:T(8,128)(2,1)} %broadcast_in_dim.12), calls=%async_computation | async-start | bytes 262144 | tf_op jit(solution)/shard_map/all_to_all | solution.py:477
  18.1 35.7 %all-to-all-start.1 = ((bf16[16,80,128]{2,1,0:T(8,128)(2,1)}), bf16[16,80,128]{2,1,0:T(8,128)(2,1)S(1)}, u32[]{:S(2)}, u32[]{:S(2)}) async-start(bf16[16,80,128]{2,1,0:T(8,128)(2,1)} %select.1.sent), calls=%async_computation.1 | async-start | bytes 655360 | tf_op jit(solution)/shard_map/all_to_all | solution.py:480
  33.4 0.7 copy-start
  34.0 19.9 %copy-start.1 = (f32[16]{0:T(128)S(1)}, f32[16]{0:T(128)}, u32[]{:S(2)}) copy-start(f32[16]{0:T(128)} %steps.3) | copy-start | bytes 196

commit v6 on v5

--- a/solution.py
+++ b/solution.py
@@ -45,50 +45,43 @@
     return copies
 
 
-def pack_kernel(
-    latents, pack_docs,
-    pick, rest, sent,
-    latents_v, packs_v, pick_v, rest_v, lowered_v, sems, out_sems,
+def select_kernel(
+    table, latents, pack_docs,
+    sent, rest,
+    latents_v, packs_v, rest_v, lowered_v, chosen_v, sems, out_sems,
 ):
-    times, chans = sent.shape[0], latents_v.shape[1]
+    times, rows, lanes = sent.shape
+    chans = latents_v.shape[1]
+    owners, count, piece = table.shape
     copies = fetch([(latents, latents_v), (pack_docs, packs_v)], sems)
     copies[0].wait()
     values = latents_v[0]
     high = values.astype(BF16)
     lowered_v[...] = high
     rest_v[...] = values - high.astype(F32)
+    left = fetch(
+        [(rest_v, rest)] + [(lowered_v, sent.at[i, pl.ds(0, chans)]) for i in range(times)],
+        out_sems,
+    )
     copies[1].wait()
-    count = packs_v.shape[1]
     column = jnp.broadcast_to(packs_v[...].astype(F32), (count, count))
     eye = lax.broadcasted_iota(jnp.int32, (count, count), 0) == lax.broadcasted_iota(
         jnp.int32, (count, count), 1
     )
     column = jnp.sum(jnp.where(eye, column, 0.0), axis=1, keepdims=True)
-    places = lax.broadcasted_iota(jnp.int32, (count, pick.shape[1]), 1).astype(F32)
-    chosen = jnp.where(places == column, 1.0, 0.0)
-    pick_v[...] = stack_rows(chosen, jnp.zeros_like(chosen))
-    left = fetch(
-        [(rest_v, rest), (pick_v, pick)]
-        + [(lowered_v, sent.at[i, pl.ds(0, chans)]) for i in range(times)],
-        out_sems,
-    )
-    for copy in left:
-        copy.wait()
-
-
-def select_kernel(table, pick, sent, out, pick_v, staged, sems):
-    del sent
-    size, rows, lanes = out.shape
-    owners, count, piece = table.shape
-    fetch([(pick, pick_v)], sems.at[pl.ds(size, 1)])[0].wait()
-    chosen = dot(pick_v[...], table[...].reshape(owners * count, piece))[:count]
+    places = lax.broadcasted_iota(jnp.int32, (count, owners * count), 1).astype(F32)
+    pick = jnp.where(places == column, 1.0, 0.0)
+    pick = stack_rows(pick, jnp.zeros_like(pick))
+    chosen = dot(pick, table[...].reshape(owners * count, piece))[:count]
     tail = jnp.concatenate(
         [chosen[:, lanes:], jnp.zeros((count, 2 * lanes - piece), F32)], axis=1
     )
-    staged[...] = stack_rows(chosen[:, :lanes], tail)
-    head = rows - 2 * count
-    copies = fetch([(staged, out.at[i, pl.ds(head, 2 * count)]) for i in range(size)], sems)
-    for copy in copies:
+    chosen_v[...] = stack_rows(chosen[:, :lanes], tail)
+    left += fetch(
+        [(chosen_v, sent.at[i, pl.ds(chans, 2 * count)]) for i in range(times)],
+        out_sems.at[pl.ds(1 + times, times)],
+    )
+    for copy in left:
         copy.wait()
 
 
@@ -96,6 +89,7 @@
     sizes = [
         ("query_gain", head), ("key_gain", head), ("bias", tokens), ("member", count),
         ("direct", chans), ("earlier", chans), ("cross", times), ("shifts", 3 * times),
+        ("rest", chans), ("weights", times),
     ]
     places, at = {}, 0
     for name, rows in sizes:
@@ -105,12 +99,11 @@
 
 
 def weights_kernel(
-    here, steps, terms, w_in, w_qkv, w_final, w_proj, query_gain, key_gain, segments, sent,
+    here, steps, terms, w_in, w_qkv, w_final, w_proj, query_gain, key_gain, segments, rest,
     inward, outward, lines, gram, small,
-    terms_v, w_in_v, w_qkv_v, w_final_v, w_proj_v, gains_v, segments_v,
+    terms_v, w_in_v, w_qkv_v, w_final_v, w_proj_v, gains_v, segments_v, rest_v,
     centred, pieces, rows, inward_v, outward_v, lines_v, gram_v, small_v, sems, out_sems,
 ):
-    del sent
     times, chans, head = outward.shape
     tokens, count = segments_v.shape[1], 8
     wide = w_in_v.shape[1]
@@ -119,7 +112,7 @@
         [
             (w_in, w_in_v), (terms, terms_v), (w_qkv, w_qkv_v), (w_final, w_final_v),
             (w_proj, w_proj_v), (query_gain, gains_v.at[0]), (key_gain, gains_v.at[1]),
-            (segments, segments_v),
+            (segments, segments_v), (rest, rest_v),
         ],
         sems,
     )
@@ -200,6 +193,10 @@
     ids = jnp.broadcast_to(segments_v[...].astype(F32), (tokens, tokens))
     put("bias", jnp.where(ids == ids.T, 0.0, MASKED))
     numbers = lax.broadcasted_iota(jnp.int32, (count, tokens), 0).astype(F32)
+    put("rest", jnp.where(here[0] == 0, rest_v[...], 0.0))
+    ones = jnp.ones((1, tokens), F32)
+    passed = [ones * jnp.where(t < here[0], steps[t], 0.0) for t in range(times)]
+    put("weights", jnp.concatenate(passed, axis=0))
     put("member", jnp.where(numbers == ids[:count], 1.0, 0.0))
     left += fetch([(small_v, small)], out_sems.at[pl.ds(4, 1)])
     for copy in left:
@@ -216,10 +213,10 @@
 
 
 def heads_kernel(
-    here, steps, arrived,
-    lines_h, w_in_h, w_final_h, w_qkv_h, gram_h, small_h, inward_h, outward_h, rest_h,
+    arrived,
+    lines_h, w_in_h, w_final_h, w_qkv_h, gram_h, small_h, inward_h, outward_h,
     out, residual,
-    lines, w_in, w_final, w_qkv, gram, small, inward, outward, rest,
+    lines, w_in, w_final, w_qkv, gram, small, inward, outward,
     rows, residual_v, queries, keys, values, raised, mass, attended, sems,
 ):
     times, chans, head = outward.shape
@@ -231,7 +228,6 @@
         [
             (lines_h, lines), (w_in_h, w_in), (w_final_h, w_final), (w_qkv_h, w_qkv),
             (gram_h, gram), (small_h, small), (inward_h, inward), (outward_h, outward),
-            (rest_h, rest),
         ],
         sems,
     )
@@ -274,14 +270,14 @@
 
     belongs = table("member")
     cross = table("cross", chans)
-    past, whole = jnp.zeros((chans, tokens), F32), 0.0
-    for t in range(times):
-        weight = jnp.where(t < here[0], steps[t], 0.0)
-        past = past + weight * arrived[t, :chans, :].astype(F32)
-        whole = whole + weight
+    weights = table("weights")
+    past = jnp.zeros((chans, tokens), F32)
+    for t in range(times):
+        past = past + weights[t : t + 1, :] * arrived[t, :chans, :].astype(F32)
+    whole = jnp.sum(weights[:, :count], axis=0, keepdims=True)
     highest = lax.Precision.HIGHEST
     near_docs = dot(whole * narrow + table("earlier", count), belongs, NN, highest)
-    first_rest = jnp.where(here[0] == 0, rest[...], 0.0)
+    first_rest = table("rest")
     residual_v[...] = (
         dot(table("direct", chans), past, NN, highest)
         + near_docs
@@ -344,55 +340,36 @@
     last.wait()
 
 
-def pack(latents, pack_docs, documents, times):
+def select(table, latents, pack_docs, times):
     block, count = latents.shape[1:], pack_docs.shape[1]
     return pl.pallas_call(
-        pack_kernel,
+        select_kernel,
         out_shape=(
-            pltpu.HBM((2 * count, documents), BF16),
+            pltpu.HBM((times, block[0] + 2 * count, block[1]), BF16),
             pltpu.HBM(block, F32),
-            pltpu.HBM((times, block[0] + 2 * count, block[1]), BF16),
         ),
-        in_specs=[HBM] * 2,
-        out_specs=(HBM,) * 3,
+        in_specs=[VMEM, HBM, HBM],
+        out_specs=(HBM, HBM),
         scratch_shapes=[
             pltpu.VMEM(latents.shape, F32),
             pltpu.VMEM(pack_docs.shape, jnp.int32),
-            pltpu.VMEM((2 * count, documents), BF16),
             pltpu.VMEM(block, F32),
             pltpu.VMEM(block, BF16),
+            pltpu.VMEM((2 * count, block[1]), BF16),
             pltpu.SemaphoreType.DMA((2,)),
-            pltpu.SemaphoreType.DMA((2 + times,)),
+            pltpu.SemaphoreType.DMA((1 + 2 * times,)),
         ],
         compiler_params=PARAMS,
-        name="pack",
-    )(*pinned(latents, pack_docs))
-
-
-def select(table, pick, sent):
-    size = sent.shape[0]
-    return pl.pallas_call(
-        select_kernel,
-        out_shape=pltpu.HBM(sent.shape, BF16),
-        in_specs=[VMEM, HBM, HBM],
-        out_specs=HBM,
-        scratch_shapes=[
-            pltpu.VMEM(pick.shape, BF16),
-            pltpu.VMEM((pick.shape[0], sent.shape[2]), BF16),
-            pltpu.SemaphoreType.DMA((size + 1,)),
-        ],
-        input_output_aliases={2: 0},
-        compiler_params=PARAMS,
         name="select",
-    )(table, *pinned(pick, sent))
+    )(table, *pinned(latents, pack_docs))
 
 
 def fold_weights(
-    here, steps, terms, w_in, w_qkv, w_final, w_proj, query_gain, key_gain, segments, sent
+    here, steps, terms, w_in, w_qkv, w_final, w_proj, query_gain, key_gain, segments, rest
 ):
     times, wide = terms.shape[0], terms.shape[2]
     chans, head, tokens = w_final.shape[0], w_proj.shape[0], segments.shape[1]
-    count = (sent.shape[1] - chans) // 2
+    count = 8
     shapes = [
         ((times // 2, 3 * head, 2 * chans), BF16),
         ((times, chans, head), BF16),
@@ -411,23 +388,24 @@
         + [
             pltpu.VMEM((2,) + query_gain.shape, F32),
             pltpu.VMEM(segments.shape, jnp.int32),
+            pltpu.VMEM(rest.shape, F32),
             pltpu.VMEM((chans, wide), F32),
             pltpu.VMEM((2 * chans, wide), BF16),
             pltpu.VMEM((2, 4 * chans, wide), BF16),
         ]
         + [pltpu.VMEM(*s) for s in shapes]
-        + [pltpu.SemaphoreType.DMA((8,)), pltpu.SemaphoreType.DMA((5,))],
+        + [pltpu.SemaphoreType.DMA((9,)), pltpu.SemaphoreType.DMA((5,))],
         compiler_params=PARAMS,
         name="fold_weights",
     )(
         here,
         steps,
-        *pinned(terms, w_in, w_qkv, w_final, w_proj, query_gain, key_gain, segments, sent),
-    )
-
-
-def run_heads(here, steps, arrived, *operands):
-    outward, rest = operands[-2:]
+        *pinned(terms, w_in, w_qkv, w_final, w_proj, query_gain, key_gain, segments, rest),
+    )
+
+
+def run_heads(arrived, *operands):
+    outward = operands[-1]
     times, chans, head = outward.shape
     tokens = arrived.shape[2]
     rows = times * (arrived.shape[1] - chans) // 2
@@ -435,13 +413,16 @@
     square = pltpu.VMEM((times, head, tokens), BF16)
     return pl.pallas_call(
         heads_kernel,
-        out_shape=(jax.ShapeDtypeStruct(outward.shape, BF16), pltpu.HBM(rest.shape, F32)),
-        in_specs=[SMEM, SMEM, VMEM] + [HBM] * len(operands),
+        out_shape=(
+            jax.ShapeDtypeStruct((times, chans, tokens), BF16),
+            pltpu.HBM((chans, tokens), F32),
+        ),
+        in_specs=[VMEM] + [HBM] * len(operands),
         out_specs=(VMEM, HBM),
         scratch_shapes=[pltpu.VMEM(a.shape, a.dtype) for a in operands]
         + [
             pltpu.VMEM((rows, wide), BF16),
-            pltpu.VMEM(rest.shape, F32),
+            pltpu.VMEM((chans, tokens), F32),
             square, square, square, square,
             pltpu.VMEM((times, tokens), F32),
             square,
@@ -449,7 +430,7 @@
         ],
         compiler_params=PARAMS,
         name="run_heads",
-    )(here, steps, arrived, *pinned(*operands))
+    )(arrived, *pinned(*operands))
 
 
 def local(
@@ -475,16 +456,14 @@
 
     copies = jnp.broadcast_to(doc_embed[None], (owners, count, piece))
     table = lax.all_to_all(copies, "req", 0, 0)
-    pick, rest, sent = pack(latents, pack_docs[None], owners * count, times)
-    sent = select(table, pick, sent)
+    sent, rest = select(table, latents, pack_docs[None], times)
     arrived = lax.all_to_all(sent, "tm", 0, 0)
     inward, outward, lines, gram, small = fold_weights(
         place, step_sizes, time_terms, w_in, w_heads, w_last, w_proj[0], query_gain, key_gain,
-        segment_ids, sent,
+        segment_ids, rest,
     )
     sums, residual = run_heads(
-        place, step_sizes, arrived, lines, w_in, w_last, w_heads, gram, small, inward, outward,
-        rest,
+        arrived, lines, w_in, w_last, w_heads, gram, small, inward, outward
     )
     parts = lax.all_to_all(sums, "tm", 0, 0)
     return (residual + jnp.sum(parts.astype(F32), axis=0))[None]

time: 85.8 us -> 84.6 us (0.986)
  blocking collectives: 24.6 us -> 39.4 us
  starting transfers between devices: 22.5 us -> 15.2 us
  waiting for transfers between devices: 14.4 us -> 8.25 us
  Pallas kernels: 20.3 us -> 18.4 us
    all_to_all x0 -> x1, blocking collectives: none -> 14.9 us  [local(): table = lax.all_to_all(copies, 'req', 0, 0)]
    all_to_all x1 -> x0, starting transfers between devices: 7.32 us -> none  [local(): table = lax.all_to_all(copies, 'req', 0, 0)]
    all_to_all x1 -> x0, waiting for transfers between devices: 6.08 us -> none  [local(): table = lax.all_to_all(copies, 'req', 0, 0)]
    pallas_call x3 -> x2, Pallas kernels: 8.78 us -> 6.84 us  [the longest x1 4.92 us: run_heads(): pl.pallas_call(heads_kernel, out_shape=(jax.ShapeDtypeStruct((times, chan...]
  transfers between devices with their start and end apart: 2 -> 1, of which waited for: 2 -> 1; matrix products, arithmetic and copies ran while one was open for 0% -> 0% of each run, Pallas kernels for 16% -> 14%
where the time goes in v6:
time: 84.6 us; the launch traced here: 84.2 us
  blocking collectives  39.4 us (47%)
  Pallas kernels  18.4 us (22%)
  starting transfers between devices  15.2 us (18%)
  waiting for transfers between devices  8.25 us (10%)
  other arithmetic  1.43 us (2%)
  local copies, waits for them, and re-layouts  1.34 us (2%)
    all_to_all x1, blocking collectives, local(): parts = lax.all_to_all(sums, 'tm', 0, 0)  24.5 us
    all_to_all x1, starting transfers between devices, local(): arrived = lax.all_to_all(sent, 'tm', 0, 0)  15.2 us
    all_to_all x1, blocking collectives, local(): table = lax.all_to_all(copies, 'req', 0, 0)  14.9 us
    pallas_call x1, Pallas kernels, fold_weights(): pl.pallas_call(weights_kernel, out_shape=tuple((pltpu.HBM(*s) for s in sh...  11.6 us
    all_to_all x1, waiting for transfers between devices, local(): arrived = lax.all_to_all(sent, 'tm', 0, 0)  8.25 us
    pallas_call x1, Pallas kernels, run_heads(): pl.pallas_call(heads_kernel, out_shape=(jax.ShapeDtypeStruct((times, chan...  4.92 us
    pallas_call x1, Pallas kernels, select(): pl.pallas_call(select_kernel, out_shape=(pltpu.HBM((times, block[0] + 2 *...  1.92 us
  transfers between devices with their start and end apart: 1, of which 1 were waited for; matrix products, arithmetic and copies ran while one was open for 0% of the time, Pallas kernels for 14%

profile of v6, /device:TPU:32, one launch (start us, length us, event | category | flops | bytes accessed | tf_op | source)
XLA Modules:
  0.0 84.2 jit_solution(6277854369088645785)
XLA Ops:
  0.0 0.7 broadcast_in_dim.12
  0.7 14.9 %all_to_all.15.table = bf16[32,8,192]{2,1,0:T(8,128)(2,1)S(1)} all-to-all(bf16[32,8,192]{2,1,0:T(8,128)(2,1)S(1)} %broadcast_in_dim.12), channel_id=1, replica_groups=mesh['tm'=16,'req'=32] {'req'}, dimensions={0} | all-to-all | bytes 196608 | tf_op jit(solution)/shard_map/all_to_all | solution.py:458
  15.6 1.9 %select.1 = (bf16[16,80,128]{2,1,0:T(8,128)(2,1)}, f32[64,128]{1,0:T(8,128)}) custom-call(bf16[32,8,192]{2,1,0:T(8,128)(2,1)S(1)} %all_to_all.15.table, f32[1,64,128]{2,1,0:T(8,128)} %latents.1, s32[1,8]{1,0:T(1,128)} %bitcast.14), custom_call_target="tpu_custom_call" | custom-call | tf_op jit(solution)/shard_map/select/pallas_call | solution.py:345
  17.5 15.2 %all-to-all-start.1 = ((bf16[16,80,128]{2,1,0:T(8,128)(2,1)}), bf16[16,80,128]{2,1,0:T(8,128)(2,1)S(1)}, u32[]{:S(2)}, u32[]{:S(2)}) async-start(bf16[16,80,128]{2,1,0:T(8,128)(2,1)} %get-tuple-element.14), calls=%async_computation.1 | async-start | bytes 655360 | tf_op jit(solution)/shard_map/all_to_all | solution.py:460
  32.8 0.0 copy-start
  32.8 0.6 copy-done
  33.4 11.6 %fold_weights.1 = (bf16[8,384,128]{2,1,0:T(8,128)(2,1)}, bf16[16,64,128]{2,1,0:T(8,128)(2,1)}, f32[32,3072]{1,0:T(8,128)}, bf16[128,64]{1,0:T(8,128)(2,1)}, f32[664,128]{1,0:T(8,128)}) custom-call(s32[1]{0:T(128)} %bitcast.1.here, f32[16]{0:T(128)S(1)} %copy-done, f32[16,4,3072]{2,1,0:T(4,128)} %terms.1, bf16[64,3072]{1,0:T(8,128)(2,1)} %w_in_h.1, ...), custom_call_target="tpu_custom_call" | custom-call | tf_op jit(solution)/shard_map/fold_weights/pallas_call | solution.py:380
  45.0 8.3 %all-to-all-done.1.arrived = bf16[16,80,128]{2,1,0:T(8,128)(2,1)S(1)} async-done(((bf16[16,80,128]{2,1,0:T(8,128)(2,1)}), bf16[16,80,128]{2,1,0:T(8,128)(2,1)S(1)}, u32[]{:S(2)}, u32[]{:S(2)}) %all-to-all-start.1) | async-done | bytes 327712 | tf_op jit(solution)/shard_map/all_to_all | solution.py:460
  53.3 4.9 %run_heads.1 = (bf16[16,64,128]{2,1,0:T(8,128)(2,1)S(1)}, f32[64,128]{1,0:T(8,128)}) custom-call(bf16[16,80,128]{2,1,0:T(8,128)(2,1)S(1)} %all-to-all-done.1.arrived, f32[32,3072]{1,0:T(8,128)} %get-tuple-element.16.lines_h, bf16[64,3072]{1,0:T(8,128)(2,1)} %w_in_h.1, bf16[64,3072]{1,0:T(8,128)(2,1)} %bitcast.12, bf16[3,3072,128]{2,1,0:T(8,128)(2,1)} %bitcast.10, ...), custom_call_target="tpu_custom_call" | custom-call | tf_op jit(solution)/shard_map/run_heads/pallas_call | solution.py:414
  58.2 24.5 %all_to_all.16 = bf16[16,64,128]{2,1,0:T(8,128)(2,1)S(1)} all-to-all(bf16[16,64,128]{2,1,0:T(8,128)(2,1)S(1)} %get-tuple-element.22), channel_id=1, replica_groups=mesh['tm'=16,'req'=32] {'tm'}, dimensions={0} | all-to-all | bytes 524288 | tf_op jit(solution)/shard_map/all_to_all | solution.py:468
  82.8 1.4 %add_bitcast_fusion = f32[1,64,128]{2,1,0:T(8,128)} fusion(f32[64,128]{1,0:T(8,128)} %get-tuple-element.21, f32[64,128]{1,0:T(8,128)S(1)} %convert_reduce_fusion), kind=kLoop, calls=%fused_computation.1 | loop fusion | flops 8192 | bytes 98304 | tf_op jit(solution)/shard_map/broadcast_in_dim | solution.py:469
  (1 shorter events, 0.0 us)
Async XLA Ops:
  17.5 35.7 %all-to-all-start.1 = ((bf16[16,80,128]{2,1,0:T(8,128)(2,1)}), bf16[16,80,128]{2,1,0:T(8,128)(2,1)S(1)}, u32[]{:S(2)}, u32[]{:S(2)}) async-start(bf16[16,80,128]{2,1,0:T(8,128)(2,1)} %get-tuple-element.14), calls=%async_computation.1 | async-start | bytes 655360 | tf_op jit(solution)/shard_map/all_to_all | solution.py:460
  32.8 0.7 copy-start

commit v7 on v6

--- a/solution.py
+++ b/solution.py
@@ -45,15 +45,39 @@
     return copies
 
 
+def first_core():
+    return lax.rem(lax.axis_index("req"), 2) == 0
+
+
+def fold_inward(centred, terms, w_qkv, rows, inward):
+    chans, head = centred.shape[0], w_qkv.shape[2]
+    for step in range(terms.shape[0] // 4):
+        for j in range(4):
+            scaled = centred[...] * (1.0 + terms[step * 4 + j, 2:3, :])
+            rows[step % 2, j * chans : (j + 1) * chans, :] = scaled.astype(BF16)
+        for c in range(3):
+            turned = dot(rows[step % 2], w_qkv[c]).T.astype(BF16)
+            inward[2 * step, c * head : (c + 1) * head, :] = turned[:, : 2 * chans]
+            inward[2 * step + 1, c * head : (c + 1) * head, :] = turned[:, 2 * chans :]
+
+
 def select_kernel(
-    table, latents, pack_docs,
-    sent, rest,
+    table, latents, pack_docs, w_in, terms, w_qkv,
+    sent, rest, inward,
     latents_v, packs_v, rest_v, lowered_v, chosen_v, sems, out_sems,
+    w_in_v, terms_v, w_qkv_v, centred, line_rows, inward_v, fold_sems,
 ):
+    early = first_core()
+    folds = [(w_in, w_in_v), (terms, terms_v), (w_qkv, w_qkv_v)]
     times, rows, lanes = sent.shape
     chans = latents_v.shape[1]
     owners, count, piece = table.shape
     copies = fetch([(latents, latents_v), (pack_docs, packs_v)], sems)
+
+    @pl.when(early)
+    def _():
+        fetch(folds, fold_sems)
+
     copies[0].wait()
     values = latents_v[0]
     high = values.astype(BF16)
@@ -81,6 +105,15 @@
         [(chosen_v, sent.at[i, pl.ds(chans, 2 * count)]) for i in range(times)],
         out_sems.at[pl.ds(1 + times, times)],
     )
+
+    @pl.when(early)
+    def _():
+        for i, (source, target) in enumerate(folds):
+            pltpu.make_async_copy(source, target, fold_sems.at[i]).wait()
+        centred[...] = centre(w_in_v[...].astype(F32))
+        fold_inward(centred, terms_v, w_qkv_v, line_rows, inward_v)
+        fetch([(inward_v, inward)], fold_sems)[0].wait()
+
     for copy in left:
         copy.wait()
 
@@ -100,10 +133,11 @@
 
 def weights_kernel(
     here, steps, terms, w_in, w_qkv, w_final, w_proj, query_gain, key_gain, segments, rest,
-    inward, outward, lines, gram, small,
+    begun, inward, outward, lines, gram, small,
     terms_v, w_in_v, w_qkv_v, w_final_v, w_proj_v, gains_v, segments_v, rest_v,
     centred, pieces, rows, inward_v, outward_v, lines_v, gram_v, small_v, sems, out_sems,
 ):
+    del begun
     times, chans, head = outward.shape
     tokens, count = segments_v.shape[1], 8
     wide = w_in_v.shape[1]
@@ -122,18 +156,14 @@
     pieces[:chans, :] = high
     pieces[chans:, :] = low
     copies[1].wait()
+    copies[2].wait()
     left = []
-    for step in range(times // 4):
-        for j in range(4):
-            scaled = centred[...] * (1.0 + terms_v[step * 4 + j, 2:3, :])
-            rows[step % 2, j * chans : (j + 1) * chans, :] = scaled.astype(BF16)
-        if step == 0:
-            copies[2].wait()
-        for c in range(3):
-            turned = dot(rows[step % 2], w_qkv_v[c]).T.astype(BF16)
-            inward_v[2 * step, c * head : (c + 1) * head, :] = turned[:, : 2 * chans]
-            inward_v[2 * step + 1, c * head : (c + 1) * head, :] = turned[:, 2 * chans :]
-    left += fetch([(inward_v, inward)], out_sems)
+
+    @pl.when(jnp.logical_not(first_core()))
+    def _():
+        fold_inward(centred, terms_v, w_qkv_v, rows, inward_v)
+        fetch([(inward_v, inward)], out_sems)[0].wait()
+
     copies[3].wait()
     copies[4].wait()
     for step in range(times // 4):
@@ -217,7 +247,7 @@
     lines_h, w_in_h, w_final_h, w_qkv_h, gram_h, small_h, inward_h, outward_h,
     out, residual,
     lines, w_in, w_final, w_qkv, gram, small, inward, outward,
-    rows, residual_v, queries, keys, values, raised, mass, attended, sems,
+    rows, queries, keys, values, raised, mass, attended, sems,
 ):
     times, chans, head = outward.shape
     tokens = arrived.shape[2]
@@ -278,14 +308,12 @@
     highest = lax.Precision.HIGHEST
     near_docs = dot(whole * narrow + table("earlier", count), belongs, NN, highest)
     first_rest = table("rest")
-    residual_v[...] = (
+    residual[...] = (
         dot(table("direct", chans), past, NN, highest)
         + near_docs
         + arrived[0, :chans, :].astype(F32)
         + first_rest
     )
-    last = pltpu.make_async_copy(residual_v, residual, sems.at[len(copies)])
-    last.start()
 
     scaled_low, rates = [], []
     for t in range(times):
@@ -322,9 +350,10 @@
         second.append(jnp.zeros((head - 8 * count - 8, tokens), F32))
         second = jnp.concatenate(second, axis=0).astype(BF16)
         right = jnp.concatenate(first + [second], axis=0)
-        queries[t] = unit(dot(left[:head], right), table("query_gain")).astype(BF16)
-        keys[t] = unit(dot(left[head : 2 * head], right), table("key_gain")).T.astype(BF16)
-        values[t] = dot(left[2 * head :], right).astype(BF16)
+        mixed = dot(left, right)
+        queries[t] = unit(mixed[:head], table("query_gain")).astype(BF16)
+        keys[t] = unit(mixed[head : 2 * head], table("key_gain")).astype(BF16).T
+        values[t] = mixed[2 * head :].astype(BF16)
     for t in range(times):
         scores = dot(keys[t], queries[t]) + table("bias")
         powered = jnp.exp2(scores - jnp.max(scores, axis=0, keepdims=True))
@@ -337,19 +366,21 @@
     for t in range(times - 1):
         total = total + dot(outward[t], attended[t])
         out[t + 1] = total.astype(BF16)
-    last.wait()
-
-
-def select(table, latents, pack_docs, times):
+
+
+def select(table, latents, pack_docs, w_in, terms, w_qkv):
     block, count = latents.shape[1:], pack_docs.shape[1]
+    times, (chans, wide), head = terms.shape[0], w_in.shape, w_qkv.shape[2]
+    folded = ((times // 2, 3 * head, 2 * chans), BF16)
     return pl.pallas_call(
         select_kernel,
         out_shape=(
             pltpu.HBM((times, block[0] + 2 * count, block[1]), BF16),
             pltpu.HBM(block, F32),
+            pltpu.HBM(*folded),
         ),
-        in_specs=[VMEM, HBM, HBM],
-        out_specs=(HBM, HBM),
+        in_specs=[VMEM] + [HBM] * 5,
+        out_specs=(HBM,) * 3,
         scratch_shapes=[
             pltpu.VMEM(latents.shape, F32),
             pltpu.VMEM(pack_docs.shape, jnp.int32),
@@ -358,14 +389,21 @@
             pltpu.VMEM((2 * count, block[1]), BF16),
             pltpu.SemaphoreType.DMA((2,)),
             pltpu.SemaphoreType.DMA((1 + 2 * times,)),
+            pltpu.VMEM(w_in.shape, BF16),
+            pltpu.VMEM(terms.shape, F32),
+            pltpu.VMEM(w_qkv.shape, BF16),
+            pltpu.VMEM(w_in.shape, F32),
+            pltpu.VMEM((2, 4 * chans, wide), BF16),
+            pltpu.VMEM(*folded),
+            pltpu.SemaphoreType.DMA((3,)),
         ],
         compiler_params=PARAMS,
         name="select",
-    )(table, *pinned(latents, pack_docs))
+    )(table, *pinned(latents, pack_docs, w_in, terms, w_qkv))
 
 
 def fold_weights(
-    here, steps, terms, w_in, w_qkv, w_final, w_proj, query_gain, key_gain, segments, rest
+    here, steps, terms, w_in, w_qkv, w_final, w_proj, query_gain, key_gain, segments, rest, inward
 ):
     times, wide = terms.shape[0], terms.shape[2]
     chans, head, tokens = w_final.shape[0], w_proj.shape[0], segments.shape[1]
@@ -380,8 +418,9 @@
     return pl.pallas_call(
         weights_kernel,
         out_shape=tuple(pltpu.HBM(*s) for s in shapes),
-        in_specs=[SMEM] * 2 + [HBM] * 9,
+        in_specs=[SMEM] * 2 + [HBM] * 10,
         out_specs=(HBM,) * 5,
+        input_output_aliases={11: 0},
         scratch_shapes=[
             pltpu.VMEM(a.shape, a.dtype) for a in (terms, w_in, w_qkv, w_final, w_proj)
         ]
@@ -400,7 +439,7 @@
     )(
         here,
         steps,
-        *pinned(terms, w_in, w_qkv, w_final, w_proj, query_gain, key_gain, segments, rest),
+        *pinned(terms, w_in, w_qkv, w_final, w_proj, query_gain, key_gain, segments, rest, inward),
     )
 
 
@@ -415,18 +454,17 @@
         heads_kernel,
         out_shape=(
             jax.ShapeDtypeStruct((times, chans, tokens), BF16),
-            pltpu.HBM((chans, tokens), F32),
+            jax.ShapeDtypeStruct((chans, tokens), F32),
         ),
         in_specs=[VMEM] + [HBM] * len(operands),
-        out_specs=(VMEM, HBM),
+        out_specs=(VMEM, VMEM),
         scratch_shapes=[pltpu.VMEM(a.shape, a.dtype) for a in operands]
         + [
             pltpu.VMEM((rows, wide), BF16),
-            pltpu.VMEM((chans, tokens), F32),
             square, square, square, square,
             pltpu.VMEM((times, tokens), F32),
             square,
-            pltpu.SemaphoreType.DMA((1 + len(operands),)),
+            pltpu.SemaphoreType.DMA((len(operands),)),
         ],
         compiler_params=PARAMS,
         name="run_heads",
@@ -449,18 +487,20 @@
 ):
     here = lax.axis_index("tm")
     place = here.astype(jnp.int32).reshape(1)
-    times, owners = lax.axis_size("tm"), lax.axis_size("req")
+    owners = lax.axis_size("req")
     count, piece = doc_embed.shape
     w_heads = w_qkv[:, :, 0, :].transpose(1, 0, 2)
     w_last = w_final.T
 
     copies = jnp.broadcast_to(doc_embed[None], (owners, count, piece))
     table = lax.all_to_all(copies, "req", 0, 0)
-    sent, rest = select(table, latents, pack_docs[None], times)
+    sent, rest, inward = select(
+        table, latents, pack_docs[None], w_in, time_terms, w_heads
+    )
     arrived = lax.all_to_all(sent, "tm", 0, 0)
     inward, outward, lines, gram, small = fold_weights(
         place, step_sizes, time_terms, w_in, w_heads, w_last, w_proj[0], query_gain, key_gain,
-        segment_ids, rest,
+        segment_ids, rest, inward,
     )
     sums, residual = run_heads(
         arrived, lines, w_in, w_last, w_heads, gram, small, inward, outward

time: 84.6 us -> 82 us (0.969)
  the two profiles are of different devices: /device:TPU:32 before, /device:TPU:2 now
where the time goes in v7:
time: 82 us; the launch traced here: 81.7 us
  blocking collectives  38 us (46%)
  Pallas kernels  20.4 us (25%)
  starting transfers between devices  14 us (17%)
  waiting for transfers between devices  7.94 us (10%)
    all_to_all x1, blocking collectives, local(): parts = lax.all_to_all(sums, 'tm', 0, 0)  22.7 us
    all_to_all x1, blocking collectives, local(): table = lax.all_to_all(copies, 'req', 0, 0)  15.3 us
    all_to_all x1, starting transfers between devices, local(): arrived = lax.all_to_all(sent, 'tm', 0, 0)  14 us
    pallas_call x1, Pallas kernels, select(): pl.pallas_call(select_kernel, out_shape=(pltpu.HBM((times, block[0] + 2 *...  8.74 us
    all_to_all x1, waiting for transfers between devices, local(): arrived = lax.all_to_all(sent, 'tm', 0, 0)  7.94 us
    pallas_call x1, Pallas kernels, fold_weights(): pl.pallas_call(weights_kernel, out_shape=tuple((pltpu.HBM(*s) for s in sh...  6.8 us
    pallas_call x1, Pallas kernels, run_heads(): pl.pallas_call(heads_kernel, out_shape=(jax.ShapeDtypeStruct((times, chan...  4.84 us
  transfers between devices with their start and end apart: 1, of which 1 were waited for; matrix products, arithmetic and copies ran while one was open for 0% of the time, Pallas kernels for 8%

profile of v7, /device:TPU:2, one launch (start us, length us, event | category | flops | bytes accessed | tf_op | source)
XLA Modules:
  0.0 81.7 jit_solution(4121270658850392607)
XLA Ops:
  0.0 0.0 copy-start
  0.0 0.7 broadcast_in_dim.12
  0.7 15.3 %all_to_all.15.table = bf16[32,8,192]{2,1,0:T(8,128)(2,1)S(1)} all-to-all(bf16[32,8,192]{2,1,0:T(8,128)(2,1)S(1)} %broadcast_in_dim.12), channel_id=1, replica_groups=mesh['tm'=16,'req'=32] {'req'}, dimensions={0} | all-to-all | bytes 196608 | tf_op jit(solution)/shard_map/all_to_all | solution.py:496
  16.0 8.7 %select.1 = (bf16[16,80,128]{2,1,0:T(8,128)(2,1)}, f32[64,128]{1,0:T(8,128)}, bf16[8,384,128]{2,1,0:T(8,128)(2,1)}) custom-call(bf16[32,8,192]{2,1,0:T(8,128)(2,1)S(1)} %all_to_all.15.table, f32[1,64,128]{2,1,0:T(8,128)} %latents.1, s32[1,8]{1,0:T(1,128)} %bitcast.15, bf16[64,3072]{1,0:T(8,128)(2,1)} %w_in_h.1, f32[16,4,3072]{2,1,0:T(4,128)} %terms.3, ...), custom_call_target="tpu_custom_call" | custom-call | tf_op jit(solution)/shard_map/select/pallas_call | solution.py:375
  24.7 14.0 %all-to-all-start.1 = ((bf16[16,80,128]{2,1,0:T(8,128)(2,1)}), bf16[16,80,128]{2,1,0:T(8,128)(2,1)S(1)}, u32[]{:S(2)}, u32[]{:S(2)}) async-start(bf16[16,80,128]{2,1,0:T(8,128)(2,1)} %get-tuple-element.15), calls=%async_computation.1 | async-start | bytes 655360 | tf_op jit(solution)/shard_map/all_to_all | solution.py:500
  38.7 0.0 copy-done
  38.7 6.8 %fold_weights.1 = (bf16[8,384,128]{2,1,0:T(8,128)(2,1)}, bf16[16,64,128]{2,1,0:T(8,128)(2,1)}, f32[32,3072]{1,0:T(8,128)}, bf16[128,64]{1,0:T(8,128)(2,1)}, f32[664,128]{1,0:T(8,128)}) custom-call(s32[1]{0:T(128)} %bitcast.3.here, f32[16]{0:T(128)S(1)} %copy-done, f32[16,4,3072]{2,1,0:T(4,128)} %terms.3, ...), custom_call_target="tpu_custom_call", output_to_operand_aliasing={{0}: (11, {})} | custom-call | tf_op jit(solution)/shard_map/fold_weights/pallas_call | solution.py:418
  45.5 7.9 %all-to-all-done.1.arrived = bf16[16,80,128]{2,1,0:T(8,128)(2,1)S(1)} async-done(((bf16[16,80,128]{2,1,0:T(8,128)(2,1)}), bf16[16,80,128]{2,1,0:T(8,128)(2,1)S(1)}, u32[]{:S(2)}, u32[]{:S(2)}) %all-to-all-start.1) | async-done | bytes 327712 | tf_op jit(solution)/shard_map/all_to_all | solution.py:500
  53.5 4.8 %run_heads.1 = (bf16[16,64,128]{2,1,0:T(8,128)(2,1)S(1)}, f32[64,128]{1,0:T(8,128)S(1)}) custom-call(bf16[16,80,128]{2,1,0:T(8,128)(2,1)S(1)} %all-to-all-done.1.arrived, f32[32,3072]{1,0:T(8,128)} %get-tuple-element.18.lines_h, bf16[64,3072]{1,0:T(8,128)(2,1)} %w_in_h.1, bf16[64,3072]{1,0:T(8,128)(2,1)} %bitcast.13, bf16[3,3072,128]{2,1,0:T(8,128)(2,1)} %bitcast.11, ...), custom_call_target="tpu_custom_call" | custom-call | tf_op jit(solution)/shard_map/run_heads/pallas_call | solution.py:453
  58.3 22.7 %all_to_all.16 = bf16[16,64,128]{2,1,0:T(8,128)(2,1)S(1)} all-to-all(bf16[16,64,128]{2,1,0:T(8,128)(2,1)S(1)} %get-tuple-element.24), channel_id=1, replica_groups=mesh['tm'=16,'req'=32] {'tm'}, dimensions={0} | all-to-all | bytes 524288 | tf_op jit(solution)/shard_map/all_to_all | solution.py:508
  81.1 0.6 add_bitcast_fusion
  (1 shorter events, 0.0 us)
Async XLA Ops:
  0.0 38.7 %copy-start = (f32[16]{0:T(128)S(1)}, f32[16]{0:T(128)}, u32[]{:S(2)}) copy-start(f32[16]{0:T(128)} %steps.1) | copy-start | bytes 196
  24.7 28.7 %all-to-all-start.1 = ((bf16[16,80,128]{2,1,0:T(8,128)(2,1)}), bf16[16,80,128]{2,1,0:T(8,128)(2,1)S(1)}, u32[]{:S(2)}, u32[]{:S(2)}) async-start(bf16[16,80,128]{2,1,0:T(8,128)(2,1)} %get-tuple-element.15), calls=%async_computation.1 | async-start | bytes 655360 | tf_op jit(solution)/shard_map/all_to_all | solution.py:500

commit v8 on v7

--- a/solution.py
+++ b/solution.py
@@ -6,6 +6,7 @@
 from jax.sharding import PartitionSpec as P
 
 EPS = 1e-06
+EARLY = 3
 MASKED = -1e30
 LOG2E = 1.4426950408889634
 BF16, F32 = jnp.bfloat16, jnp.float32
@@ -49,9 +50,9 @@
     return lax.rem(lax.axis_index("req"), 2) == 0
 
 
-def fold_inward(centred, terms, w_qkv, rows, inward):
+def fold_inward(steps, centred, terms, w_qkv, rows, inward):
     chans, head = centred.shape[0], w_qkv.shape[2]
-    for step in range(terms.shape[0] // 4):
+    for step in steps:
         for j in range(4):
             scaled = centred[...] * (1.0 + terms[step * 4 + j, 2:3, :])
             rows[step % 2, j * chans : (j + 1) * chans, :] = scaled.astype(BF16)
@@ -111,8 +112,9 @@
         for i, (source, target) in enumerate(folds):
             pltpu.make_async_copy(source, target, fold_sems.at[i]).wait()
         centred[...] = centre(w_in_v[...].astype(F32))
-        fold_inward(centred, terms_v, w_qkv_v, line_rows, inward_v)
-        fetch([(inward_v, inward)], fold_sems)[0].wait()
+        fold_inward(range(EARLY), centred, terms_v, w_qkv_v, line_rows, inward_v)
+        done = pl.ds(0, 2 * EARLY)
+        fetch([(inward_v.at[done], inward.at[done])], fold_sems)[0].wait()
 
     for copy in left:
         copy.wait()
@@ -159,9 +161,15 @@
     copies[2].wait()
     left = []
 
+    @pl.when(first_core())
+    def _():
+        fold_inward(range(EARLY, times // 4), centred, terms_v, w_qkv_v, rows, inward_v)
+        done = pl.ds(2 * EARLY, times // 2 - 2 * EARLY)
+        fetch([(inward_v.at[done], inward.at[done])], out_sems)[0].wait()
+
     @pl.when(jnp.logical_not(first_core()))
     def _():
-        fold_inward(centred, terms_v, w_qkv_v, rows, inward_v)
+        fold_inward(range(times // 4), centred, terms_v, w_qkv_v, rows, inward_v)
         fetch([(inward_v, inward)], out_sems)[0].wait()
 
     copies[3].wait()

time: 82 us -> 81.4 us (level)
  the two profiles are of different devices: /device:TPU:2 before, /device:TPU:32 now
where the time goes in v8:
time: 81.4 us; the launch traced here: 81.1 us
  blocking collectives  36 us (44%)
  Pallas kernels  21 us (26%)
  starting transfers between devices  15.2 us (19%)
  waiting for transfers between devices  7.5 us (9%)
    all_to_all x1, blocking collectives, local(): parts = lax.all_to_all(sums, 'tm', 0, 0)  21.1 us
    all_to_all x1, starting transfers between devices, local(): arrived = lax.all_to_all(sent, 'tm', 0, 0)  15.2 us
    all_to_all x1, blocking collectives, local(): table = lax.all_to_all(copies, 'req', 0, 0)  14.9 us
    pallas_call x1, Pallas kernels, fold_weights(): pl.pallas_call(weights_kernel, out_shape=tuple((pltpu.HBM(*s) for s in sh...  8.68 us
    all_to_all x1, waiting for transfers between devices, local(): arrived = lax.all_to_all(sent, 'tm', 0, 0)  7.5 us
    pallas_call x1, Pallas kernels, select(): pl.pallas_call(select_kernel, out_shape=(pltpu.HBM((times, block[0] + 2 *...  7.44 us
    pallas_call x1, Pallas kernels, run_heads(): pl.pallas_call(heads_kernel, out_shape=(jax.ShapeDtypeStruct((times, chan...  4.84 us
  transfers between devices with their start and end apart: 1, of which 1 were waited for; matrix products, arithmetic and copies ran while one was open for 0% of the time, Pallas kernels for 11%

profile of v8, /device:TPU:32, one launch (start us, length us, event | category | flops | bytes accessed | tf_op | source)
XLA Modules:
  0.0 81.1 jit_solution(16513823776535703)
XLA Ops:
  0.0 0.0 copy-start
  0.0 0.7 broadcast_in_dim.12
  0.7 14.9 %all_to_all.15.table = bf16[32,8,192]{2,1,0:T(8,128)(2,1)S(1)} all-to-all(bf16[32,8,192]{2,1,0:T(8,128)(2,1)S(1)} %broadcast_in_dim.12), channel_id=1, replica_groups=mesh['tm'=16,'req'=32] {'req'}, dimensions={0} | all-to-all | bytes 196608 | tf_op jit(solution)/shard_map/all_to_all | solution.py:504
  15.6 7.4 %select.1 = (bf16[16,80,128]{2,1,0:T(8,128)(2,1)}, f32[64,128]{1,0:T(8,128)}, bf16[8,384,128]{2,1,0:T(8,128)(2,1)}) custom-call(bf16[32,8,192]{2,1,0:T(8,128)(2,1)S(1)} %all_to_all.15.table, f32[1,64,128]{2,1,0:T(8,128)} %latents.1, s32[1,8]{1,0:T(1,128)} %bitcast.15, bf16[64,3072]{1,0:T(8,128)(2,1)} %w_in_h.1, f32[16,4,3072]{2,1,0:T(4,128)} %terms.3, ...), custom_call_target="tpu_custom_call" | custom-call | tf_op jit(solution)/shard_map/select/pallas_call | solution.py:383
  23.1 15.2 %all-to-all-start.1 = ((bf16[16,80,128]{2,1,0:T(8,128)(2,1)}), bf16[16,80,128]{2,1,0:T(8,128)(2,1)S(1)}, u32[]{:S(2)}, u32[]{:S(2)}) async-start(bf16[16,80,128]{2,1,0:T(8,128)(2,1)} %get-tuple-element.15), calls=%async_computation.1 | async-start | bytes 655360 | tf_op jit(solution)/shard_map/all_to_all | solution.py:508
  38.3 0.0 copy-done
  38.3 8.7 %fold_weights.1 = (bf16[8,384,128]{2,1,0:T(8,128)(2,1)}, bf16[16,64,128]{2,1,0:T(8,128)(2,1)}, f32[32,3072]{1,0:T(8,128)}, bf16[128,64]{1,0:T(8,128)(2,1)}, f32[664,128]{1,0:T(8,128)}) custom-call(s32[1]{0:T(128)} %bitcast.3.here, f32[16]{0:T(128)S(1)} %copy-done, f32[16,4,3072]{2,1,0:T(4,128)} %terms.3, ...), custom_call_target="tpu_custom_call", output_to_operand_aliasing={{0}: (11, {})} | custom-call | tf_op jit(solution)/shard_map/fold_weights/pallas_call | solution.py:426
  47.0 7.5 %all-to-all-done.1.arrived = bf16[16,80,128]{2,1,0:T(8,128)(2,1)S(1)} async-done(((bf16[16,80,128]{2,1,0:T(8,128)(2,1)}), bf16[16,80,128]{2,1,0:T(8,128)(2,1)S(1)}, u32[]{:S(2)}, u32[]{:S(2)}) %all-to-all-start.1) | async-done | bytes 327712 | tf_op jit(solution)/shard_map/all_to_all | solution.py:508
  54.5 4.8 %run_heads.1 = (bf16[16,64,128]{2,1,0:T(8,128)(2,1)S(1)}, f32[64,128]{1,0:T(8,128)S(1)}) custom-call(bf16[16,80,128]{2,1,0:T(8,128)(2,1)S(1)} %all-to-all-done.1.arrived, f32[32,3072]{1,0:T(8,128)} %get-tuple-element.18.lines_h, bf16[64,3072]{1,0:T(8,128)(2,1)} %w_in_h.1, bf16[64,3072]{1,0:T(8,128)(2,1)} %bitcast.13, bf16[3,3072,128]{2,1,0:T(8,128)(2,1)} %bitcast.11, ...), custom_call_target="tpu_custom_call" | custom-call | tf_op jit(solution)/shard_map/run_heads/pallas_call | solution.py:461
  59.3 21.1 %all_to_all.16 = bf16[16,64,128]{2,1,0:T(8,128)(2,1)S(1)} all-to-all(bf16[16,64,128]{2,1,0:T(8,128)(2,1)S(1)} %get-tuple-element.24), channel_id=1, replica_groups=mesh['tm'=16,'req'=32] {'tm'}, dimensions={0} | all-to-all | bytes 524288 | tf_op jit(solution)/shard_map/all_to_all | solution.py:516
  80.5 0.6 add_bitcast_fusion
  (1 shorter events, 0.0 us)
Async XLA Ops:
  0.0 38.3 %copy-start = (f32[16]{0:T(128)S(1)}, f32[16]{0:T(128)}, u32[]{:S(2)}) copy-start(f32[16]{0:T(128)} %steps.1) | copy-start | bytes 196
  23.1 31.4 %all-to-all-start.1 = ((bf16[16,80,128]{2,1,0:T(8,128)(2,1)}), bf16[16,80,128]{2,1,0:T(8,128)(2,1)S(1)}, u32[]{:S(2)}, u32[]{:S(2)}) async-start(bf16[16,80,128]{2,1,0:T(8,128)(2,1)} %get-tuple-element.15), calls=%async_computation.1 | async-start | bytes 655360 | tf_op jit(solution)/shard_map/all_to_all | solution.py:508

commit v9 on v8

--- a/solution.py
+++ b/solution.py
@@ -293,7 +293,7 @@
     near = dot(stack_rows(high, low), w_in[...], NT)
     near = near[:count] + near[count:]
     copies[3].wait()
-    base = jnp.concatenate([dot(rows[...], w_qkv[c]) for c in range(3)], axis=1)
+    base = dot(rows[...], jnp.concatenate([w_qkv[c] for c in range(3)], axis=1))
     for copy in copies[4:]:
         copy.wait()
     shifts = table("shifts")
@@ -324,44 +324,57 @@
     )
 
     scaled_low, rates = [], []
-    for t in range(times):
-        mixed = 2.0 * (near + cross[t : t + 1, :])
-        high, low = two_parts(mixed)
-        left = jnp.concatenate([gram[...], stack_rows(high, low)], axis=0)
-        block = arrived[t, :chans, :]
-        product = dot(left, block)
-        both = product[:chans] + product[chans : 2 * chans]
-        block = block.astype(F32)
-        other = product[2 * chans : 2 * chans + count] + product[2 * chans + count :]
-        spread = jnp.sum(both * block, axis=0, keepdims=True) + jnp.sum(
-            belongs * (other + powers[t]), axis=0, keepdims=True
-        )
-        rate = lax.rsqrt(spread / wide + EPS)
-        rates.append(rate)
-        scaled_low.append((block * rate).astype(BF16))
+    for pair in range(0, times, 2):
+        left = [gram[...]]
+        for t in (pair, pair + 1):
+            high, low = two_parts(2.0 * (near + cross[t : t + 1, :]))
+            left.append(stack_rows(high, low))
+        blocks = [arrived[t, :chans, :] for t in (pair, pair + 1)]
+        products = dot(jnp.concatenate(left, axis=0), jnp.concatenate(blocks, axis=1))
+        for k in range(2):
+            product = products[:, k * tokens : (k + 1) * tokens]
+            both = product[:chans] + product[chans : 2 * chans]
+            block = blocks[k].astype(F32)
+            at = 2 * chans + 2 * k * count
+            other = product[at : at + count] + product[at + count : at + 2 * count]
+            spread = jnp.sum(both * block, axis=0, keepdims=True) + jnp.sum(
+                belongs * (other + powers[pair + k]), axis=0, keepdims=True
+            )
+            rate = lax.rsqrt(spread / wide + EPS)
+            rates.append(rate)
+            scaled_low.append((block * rate).astype(BF16))
 
     def unit(block, gain):
         power = jnp.mean(block * block, axis=0, keepdims=True)
         return block * (lax.rsqrt(power + EPS) * gain)
 
     empty = jnp.zeros((chans, tokens), BF16)
-    for t in range(times):
-        half, j = divmod(t, 8)
-        left = jnp.concatenate([inward[t // 2], turned[half]], axis=1)
-        first = [scaled_low[t], empty] if t % 2 == 0 else [empty, scaled_low[t]]
-        ones = lax.broadcasted_iota(jnp.int32, (8, tokens), 0) == j
-        second = [jnp.zeros((j * count, tokens), F32)] if j else []
-        second.append(belongs * rates[t])
-        if j < 7:
-            second.append(jnp.zeros(((7 - j) * count, tokens), F32))
-        second.append(jnp.where(ones, 1.0, 0.0))
-        second.append(jnp.zeros((head - 8 * count - 8, tokens), F32))
-        second = jnp.concatenate(second, axis=0).astype(BF16)
-        right = jnp.concatenate(first + [second], axis=0)
-        mixed = dot(left, right)
-        queries[t] = unit(mixed[:head], table("query_gain")).astype(BF16)
-        keys[t] = unit(mixed[head : 2 * head], table("key_gain")).astype(BF16).T
-        values[t] = mixed[2 * head :].astype(BF16)
+    for pair in range(0, times, 2):
+        left = jnp.concatenate([inward[pair // 2], turned[pair // 8]], axis=1)
+        columns = []
+        for t in (pair, pair + 1):
+            j = t % 8
+            first = [scaled_low[t], empty] if t == pair else [empty, scaled_low[t]]
+            ones = lax.broadcasted_iota(jnp.int32, (8, tokens), 0) == j
+            second = [jnp.zeros((j * count, tokens), F32)] if j else []
+            second.append(belongs * rates[t])
+            if j < 7:
+                second.append(jnp.zeros(((7 - j) * count, tokens), F32))
+            second.append(jnp.where(ones, 1.0, 0.0))
+            second.append(jnp.zeros((head - 8 * count - 8, tokens), F32))
+            second = jnp.concatenate(second, axis=0).astype(BF16)
+            columns.append(jnp.concatenate(first + [second], axis=0))
+        right = jnp.concatenate(columns, axis=1)
+        for c in range(3):
+            products = dot(left[c * head : (c + 1) * head], right)
+            for k in range(2):
+                block = products[:, k * tokens : (k + 1) * tokens]
+                if c == 0:
+                    queries[pair + k] = unit(block, table("query_gain")).astype(BF16)
+                elif c == 1:
+                    keys[pair + k] = unit(block, table("key_gain")).astype(BF16).T
+                else:
+                    values[pair + k] = block.astype(BF16)
     for t in range(times):
         scores = dot(keys[t], queries[t]) + table("bias")
         powered = jnp.exp2(scores - jnp.max(scores, axis=0, keepdims=True))

time: 81.4 us -> 80.8 us (level)
  no operation moved by 1% of the time
where the time goes in v9:
time: 80.8 us; the launch traced here: 80.5 us
  blocking collectives  36 us (45%)
  Pallas kernels  20.4 us (25%)
  starting transfers between devices  15.2 us (19%)
  waiting for transfers between devices  7.5 us (9%)
    all_to_all x1, blocking collectives, local(): parts = lax.all_to_all(sums, 'tm', 0, 0)  21.1 us
    all_to_all x1, starting transfers between devices, local(): arrived = lax.all_to_all(sent, 'tm', 0, 0)  15.2 us
    all_to_all x1, blocking collectives, local(): table = lax.all_to_all(copies, 'req', 0, 0)  14.9 us
    pallas_call x1, Pallas kernels, fold_weights(): pl.pallas_call(weights_kernel, out_shape=tuple((pltpu.HBM(*s) for s in sh...  8.68 us
    all_to_all x1, waiting for transfers between devices, local(): arrived = lax.all_to_all(sent, 'tm', 0, 0)  7.5 us
    pallas_call x1, Pallas kernels, select(): pl.pallas_call(select_kernel, out_shape=(pltpu.HBM((times, block[0] + 2 *...  7.44 us
    pallas_call x1, Pallas kernels, run_heads(): pl.pallas_call(heads_kernel, out_shape=(jax.ShapeDtypeStruct((times, chan...  4.26 us
  transfers between devices with their start and end apart: 1, of which 1 were waited for; matrix products, arithmetic and copies ran while one was open for 0% of the time, Pallas kernels for 11%

profile of v9, /device:TPU:32, one launch (start us, length us, event | category | flops | bytes accessed | tf_op | source)
XLA Modules:
  0.0 80.5 jit_solution(16049851282980565991)
XLA Ops:
  0.0 0.0 copy-start
  0.0 0.7 broadcast_in_dim.12
  0.7 14.9 %all_to_all.15.table = bf16[32,8,192]{2,1,0:T(8,128)(2,1)S(1)} all-to-all(bf16[32,8,192]{2,1,0:T(8,128)(2,1)S(1)} %broadcast_in_dim.12), channel_id=1, replica_groups=mesh['tm'=16,'req'=32] {'req'}, dimensions={0} | all-to-all | bytes 196608 | tf_op jit(solution)/shard_map/all_to_all | solution.py:517
  15.6 7.4 %select.1 = (bf16[16,80,128]{2,1,0:T(8,128)(2,1)}, f32[64,128]{1,0:T(8,128)}, bf16[8,384,128]{2,1,0:T(8,128)(2,1)}) custom-call(bf16[32,8,192]{2,1,0:T(8,128)(2,1)S(1)} %all_to_all.15.table, f32[1,64,128]{2,1,0:T(8,128)} %latents.1, s32[1,8]{1,0:T(1,128)} %bitcast.15, bf16[64,3072]{1,0:T(8,128)(2,1)} %w_in_h.1, f32[16,4,3072]{2,1,0:T(4,128)} %terms.3, ...), custom_call_target="tpu_custom_call" | custom-call | tf_op jit(solution)/shard_map/select/pallas_call | solution.py:396
  23.1 15.2 %all-to-all-start.1 = ((bf16[16,80,128]{2,1,0:T(8,128)(2,1)}), bf16[16,80,128]{2,1,0:T(8,128)(2,1)S(1)}, u32[]{:S(2)}, u32[]{:S(2)}) async-start(bf16[16,80,128]{2,1,0:T(8,128)(2,1)} %get-tuple-element.15), calls=%async_computation.1 | async-start | bytes 655360 | tf_op jit(solution)/shard_map/all_to_all | solution.py:521
  38.3 0.0 copy-done
  38.3 8.7 %fold_weights.1 = (bf16[8,384,128]{2,1,0:T(8,128)(2,1)}, bf16[16,64,128]{2,1,0:T(8,128)(2,1)}, f32[32,3072]{1,0:T(8,128)}, bf16[128,64]{1,0:T(8,128)(2,1)}, f32[664,128]{1,0:T(8,128)}) custom-call(s32[1]{0:T(128)} %bitcast.3.here, f32[16]{0:T(128)S(1)} %copy-done, f32[16,4,3072]{2,1,0:T(4,128)} %terms.3, ...), custom_call_target="tpu_custom_call", output_to_operand_aliasing={{0}: (11, {})} | custom-call | tf_op jit(solution)/shard_map/fold_weights/pallas_call | solution.py:439
  47.0 7.5 %all-to-all-done.1.arrived = bf16[16,80,128]{2,1,0:T(8,128)(2,1)S(1)} async-done(((bf16[16,80,128]{2,1,0:T(8,128)(2,1)}), bf16[16,80,128]{2,1,0:T(8,128)(2,1)S(1)}, u32[]{:S(2)}, u32[]{:S(2)}) %all-to-all-start.1) | async-done | bytes 327712 | tf_op jit(solution)/shard_map/all_to_all | solution.py:521
  54.5 4.3 %run_heads.1 = (bf16[16,64,128]{2,1,0:T(8,128)(2,1)S(1)}, f32[64,128]{1,0:T(8,128)S(1)}) custom-call(bf16[16,80,128]{2,1,0:T(8,128)(2,1)S(1)} %all-to-all-done.1.arrived, f32[32,3072]{1,0:T(8,128)} %get-tuple-element.18.lines_h, bf16[64,3072]{1,0:T(8,128)(2,1)} %w_in_h.1, bf16[64,3072]{1,0:T(8,128)(2,1)} %bitcast.13, bf16[3,3072,128]{2,1,0:T(8,128)(2,1)} %bitcast.11, ...), custom_call_target="tpu_custom_call" | custom-call | tf_op jit(solution)/shard_map/run_heads/pallas_call | solution.py:474
  58.8 21.1 %all_to_all.16 = bf16[16,64,128]{2,1,0:T(8,128)(2,1)S(1)} all-to-all(bf16[16,64,128]{2,1,0:T(8,128)(2,1)S(1)} %get-tuple-element.24), channel_id=1, replica_groups=mesh['tm'=16,'req'=32] {'tm'}, dimensions={0} | all-to-all | bytes 524288 | tf_op jit(solution)/shard_map/all_to_all | solution.py:529
  79.9 0.6 add_bitcast_fusion
  (1 shorter events, 0.0 us)
Async XLA Ops:
  0.0 38.3 %copy-start = (f32[16]{0:T(128)S(1)}, f32[16]{0:T(128)}, u32[]{:S(2)}) copy-start(f32[16]{0:T(128)} %steps.1) | copy-start | bytes 196
  23.1 31.4 %all-to-all-start.1 = ((bf16[16,80,128]{2,1,0:T(8,128)(2,1)}), bf16[16,80,128]{2,1,0:T(8,128)(2,1)S(1)}, u32[]{:S(2)}, u32[]{:S(2)}) async-start(bf16[16,80,128]{2,1,0:T(8,128)(2,1)} %get-tuple-element.15), calls=%async_computation.1 | async-start | bytes 655360 | tf_op jit(solution)/shard_map/all_to_all | solution.py:521

commit v10 on v9

--- a/solution.py
+++ b/solution.py
@@ -65,7 +65,7 @@
 def select_kernel(
     table, latents, pack_docs, w_in, terms, w_qkv,
     sent, rest, inward,
-    latents_v, packs_v, rest_v, lowered_v, chosen_v, sems, out_sems,
+    latents_v, packs_v, rest_v, staged, sems, out_sems,
     w_in_v, terms_v, w_qkv_v, centred, line_rows, inward_v, fold_sems,
 ):
     early = first_core()
@@ -82,11 +82,11 @@
     copies[0].wait()
     values = latents_v[0]
     high = values.astype(BF16)
-    lowered_v[...] = high
+    for i in range(times):
+        staged[i, :chans, :] = high
     rest_v[...] = values - high.astype(F32)
     left = fetch(
-        [(rest_v, rest)] + [(lowered_v, sent.at[i, pl.ds(0, chans)]) for i in range(times)],
-        out_sems,
+        [(rest_v, rest), (staged.at[:, pl.ds(0, chans)], sent.at[:, pl.ds(0, chans)])], out_sems
     )
     copies[1].wait()
     column = jnp.broadcast_to(packs_v[...].astype(F32), (count, count))
@@ -101,11 +101,11 @@
     tail = jnp.concatenate(
         [chosen[:, lanes:], jnp.zeros((count, 2 * lanes - piece), F32)], axis=1
     )
-    chosen_v[...] = stack_rows(chosen[:, :lanes], tail)
-    left += fetch(
-        [(chosen_v, sent.at[i, pl.ds(chans, 2 * count)]) for i in range(times)],
-        out_sems.at[pl.ds(1 + times, times)],
-    )
+    chosen = stack_rows(chosen[:, :lanes], tail)
+    for i in range(times):
+        staged[i, chans:, :] = chosen
+    last = pl.ds(chans, 2 * count)
+    left += fetch([(staged.at[:, last], sent.at[:, last])], out_sems.at[pl.ds(2, 1)])
 
     @pl.when(early)
     def _():
@@ -406,10 +406,9 @@
             pltpu.VMEM(latents.shape, F32),
             pltpu.VMEM(pack_docs.shape, jnp.int32),
             pltpu.VMEM(block, F32),
-            pltpu.VMEM(block, BF16),
-            pltpu.VMEM((2 * count, block[1]), BF16),
+            pltpu.VMEM((times, block[0] + 2 * count, block[1]), BF16),
             pltpu.SemaphoreType.DMA((2,)),
-            pltpu.SemaphoreType.DMA((1 + 2 * times,)),
+            pltpu.SemaphoreType.DMA((3,)),
             pltpu.VMEM(w_in.shape, BF16),
             pltpu.VMEM(terms.shape, F32),
             pltpu.VMEM(w_qkv.shape, BF16),

time: 80.8 us -> 80.6 us (level)
  no operation moved by 1% of the time
where the time goes in v10:
time: 80.6 us; the launch traced here: 80.2 us
  blocking collectives  36 us (45%)
  Pallas kernels  20.1 us (25%)
  starting transfers between devices  15.2 us (19%)
  waiting for transfers between devices  7.55 us (9%)
    all_to_all x1, blocking collectives, local(): parts = lax.all_to_all(sums, 'tm', 0, 0)  21.1 us
    all_to_all x1, starting transfers between devices, local(): arrived = lax.all_to_all(sent, 'tm', 0, 0)  15.2 us
    all_to_all x1, blocking collectives, local(): table = lax.all_to_all(copies, 'req', 0, 0)  14.9 us
    pallas_call x1, Pallas kernels, fold_weights(): pl.pallas_call(weights_kernel, out_shape=tuple((pltpu.HBM(*s) for s in sh...  8.68 us
    all_to_all x1, waiting for transfers between devices, local(): arrived = lax.all_to_all(sent, 'tm', 0, 0)  7.55 us
    pallas_call x1, Pallas kernels, select(): pl.pallas_call(select_kernel, out_shape=(pltpu.HBM((times, block[0] + 2 *...  7.12 us
    pallas_call x1, Pallas kernels, run_heads(): pl.pallas_call(heads_kernel, out_shape=(jax.ShapeDtypeStruct((times, chan...  4.26 us
  transfers between devices with their start and end apart: 1, of which 1 were waited for; matrix products, arithmetic and copies ran while one was open for 0% of the time, Pallas kernels for 11%

profile of v10, /device:TPU:32, one launch (start us, length us, event | category | flops | bytes accessed | tf_op | source)
XLA Modules:
  0.0 80.2 jit_solution(3222702742185626146)
XLA Ops:
  0.0 0.0 copy-start
  0.0 0.7 broadcast_in_dim.12
  0.7 14.9 %all_to_all.15.table = bf16[32,8,192]{2,1,0:T(8,128)(2,1)S(1)} all-to-all(bf16[32,8,192]{2,1,0:T(8,128)(2,1)S(1)} %broadcast_in_dim.12), channel_id=1, replica_groups=mesh['tm'=16,'req'=32] {'req'}, dimensions={0} | all-to-all | bytes 196608 | tf_op jit(solution)/shard_map/all_to_all | solution.py:516
  15.6 7.1 %select.1 = (bf16[16,80,128]{2,1,0:T(8,128)(2,1)}, f32[64,128]{1,0:T(8,128)}, bf16[8,384,128]{2,1,0:T(8,128)(2,1)}) custom-call(bf16[32,8,192]{2,1,0:T(8,128)(2,1)S(1)} %all_to_all.15.table, f32[1,64,128]{2,1,0:T(8,128)} %latents.1, s32[1,8]{1,0:T(1,128)} %bitcast.15, bf16[64,3072]{1,0:T(8,128)(2,1)} %w_in_h.1, f32[16,4,3072]{2,1,0:T(4,128)} %terms.3, ...), custom_call_target="tpu_custom_call" | custom-call | tf_op jit(solution)/shard_map/select/pallas_call | solution.py:396
  22.8 15.2 %all-to-all-start.1 = ((bf16[16,80,128]{2,1,0:T(8,128)(2,1)}), bf16[16,80,128]{2,1,0:T(8,128)(2,1)S(1)}, u32[]{:S(2)}, u32[]{:S(2)}) async-start(bf16[16,80,128]{2,1,0:T(8,128)(2,1)} %get-tuple-element.15), calls=%async_computation.1 | async-start | bytes 655360 | tf_op jit(solution)/shard_map/all_to_all | solution.py:520
  38.0 0.0 copy-done
  38.0 8.7 %fold_weights.1 = (bf16[8,384,128]{2,1,0:T(8,128)(2,1)}, bf16[16,64,128]{2,1,0:T(8,128)(2,1)}, f32[32,3072]{1,0:T(8,128)}, bf16[128,64]{1,0:T(8,128)(2,1)}, f32[664,128]{1,0:T(8,128)}) custom-call(s32[1]{0:T(128)} %bitcast.3.here, f32[16]{0:T(128)S(1)} %copy-done, f32[16,4,3072]{2,1,0:T(4,128)} %terms.3, ...), custom_call_target="tpu_custom_call", output_to_operand_aliasing={{0}: (11, {})} | custom-call | tf_op jit(solution)/shard_map/fold_weights/pallas_call | solution.py:438
  46.7 7.6 %all-to-all-done.1.arrived = bf16[16,80,128]{2,1,0:T(8,128)(2,1)S(1)} async-done(((bf16[16,80,128]{2,1,0:T(8,128)(2,1)}), bf16[16,80,128]{2,1,0:T(8,128)(2,1)S(1)}, u32[]{:S(2)}, u32[]{:S(2)}) %all-to-all-start.1) | async-done | bytes 327712 | tf_op jit(solution)/shard_map/all_to_all | solution.py:520
  54.2 4.3 %run_heads.1 = (bf16[16,64,128]{2,1,0:T(8,128)(2,1)S(1)}, f32[64,128]{1,0:T(8,128)S(1)}) custom-call(bf16[16,80,128]{2,1,0:T(8,128)(2,1)S(1)} %all-to-all-done.1.arrived, f32[32,3072]{1,0:T(8,128)} %get-tuple-element.18.lines_h, bf16[64,3072]{1,0:T(8,128)(2,1)} %w_in_h.1, bf16[64,3072]{1,0:T(8,128)(2,1)} %bitcast.13, bf16[3,3072,128]{2,1,0:T(8,128)(2,1)} %bitcast.11, ...), custom_call_target="tpu_custom_call" | custom-call | tf_op jit(solution)/shard_map/run_heads/pallas_call | solution.py:473
  58.5 21.1 %all_to_all.16 = bf16[16,64,128]{2,1,0:T(8,128)(2,1)S(1)} all-to-all(bf16[16,64,128]{2,1,0:T(8,128)(2,1)S(1)} %get-tuple-element.24), channel_id=1, replica_groups=mesh['tm'=16,'req'=32] {'tm'}, dimensions={0} | all-to-all | bytes 524288 | tf_op jit(solution)/shard_map/all_to_all | solution.py:528
  79.6 0.6 add_bitcast_fusion
  (1 shorter events, 0.0 us)
Async XLA Ops:
  0.0 38.0 %copy-start = (f32[16]{0:T(128)S(1)}, f32[16]{0:T(128)}, u32[]{:S(2)}) copy-start(f32[16]{0:T(128)} %steps.1) | copy-start | bytes 196
  22.8 31.5 %all-to-all-start.1 = ((bf16[16,80,128]{2,1,0:T(8,128)(2,1)}), bf16[16,80,128]{2,1,0:T(8,128)(2,1)S(1)}, u32[]{:S(2)}, u32[]{:S(2)}) async-start(bf16[16,80,128]{2,1,0:T(8,128)(2,1)} %get-tuple-element.15), calls=%async_computation.1 | async-start | bytes 655360 | tf_op jit(solution)/shard_map/all_to_all | solution.py:520

commit v11 on v10

--- a/solution.py
+++ b/solution.py
@@ -6,7 +6,7 @@
 from jax.sharding import PartitionSpec as P
 
 EPS = 1e-06
-EARLY = 3
+EARLY = 2
 MASKED = -1e30
 LOG2E = 1.4426950408889634
 BF16, F32 = jnp.bfloat16, jnp.float32

time: 80.6 us -> 82.2 us (1.020)
  blocking collectives: 36 us -> 37.3 us
    pallas_call x1, Pallas kernels: 8.68 us -> 10 us  [fold_weights(): pl.pallas_call(weights_kernel, out_shape=tuple((pltpu.HBM(*s) for s in sh...]
    all_to_all x1, blocking collectives: 21.1 us -> 22.4 us  [local(): parts = lax.all_to_all(sums, 'tm', 0, 0)]
    pallas_call x1, Pallas kernels: 7.12 us -> 5.82 us  [select(): pl.pallas_call(select_kernel, out_shape=(pltpu.HBM((times, block[0] + 2 *...]
  transfers between devices with their start and end apart: 1 -> 1, of which waited for: 1 -> 1; matrix products, arithmetic and copies ran while one was open for 0% -> 0% of each run, Pallas kernels for 11% -> 12%
where the time goes in v11:
time: 82.2 us; the launch traced here: 81.8 us
  blocking collectives  37.3 us (45%)
  Pallas kernels  20.1 us (24%)
  starting transfers between devices  15.2 us (18%)
  waiting for transfers between devices  7.81 us (10%)
    all_to_all x1, blocking collectives, local(): parts = lax.all_to_all(sums, 'tm', 0, 0)  22.4 us
    all_to_all x1, starting transfers between devices, local(): arrived = lax.all_to_all(sent, 'tm', 0, 0)  15.2 us
    all_to_all x1, blocking collectives, local(): table = lax.all_to_all(copies, 'req', 0, 0)  14.9 us
    pallas_call x1, Pallas kernels, fold_weights(): pl.pallas_call(weights_kernel, out_shape=tuple((pltpu.HBM(*s) for s in sh...  10 us
    all_to_all x1, waiting for transfers between devices, local(): arrived = lax.all_to_all(sent, 'tm', 0, 0)  7.81 us
    pallas_call x1, Pallas kernels, select(): pl.pallas_call(select_kernel, out_shape=(pltpu.HBM((times, block[0] + 2 *...  5.82 us
    pallas_call x1, Pallas kernels, run_heads(): pl.pallas_call(heads_kernel, out_shape=(jax.ShapeDtypeStruct((times, chan...  4.26 us
  transfers between devices with their start and end apart: 1, of which 1 were waited for; matrix products, arithmetic and copies ran while one was open for 0% of the time, Pallas kernels for 12%

profile of v11, /device:TPU:32, one launch (start us, length us, event | category | flops | bytes accessed | tf_op | source)
XLA Modules:
  0.0 81.8 jit_solution(16667616505483855737)
XLA Ops:
  0.0 0.0 copy-start
  0.0 0.7 broadcast_in_dim.12
  0.7 14.9 %all_to_all.15.table = bf16[32,8,192]{2,1,0:T(8,128)(2,1)S(1)} all-to-all(bf16[32,8,192]{2,1,0:T(8,128)(2,1)S(1)} %broadcast_in_dim.12), channel_id=1, replica_groups=mesh['tm'=16,'req'=32] {'req'}, dimensions={0} | all-to-all | bytes 196608 | tf_op jit(solution)/shard_map/all_to_all | solution.py:516
  15.6 5.8 %select.1 = (bf16[16,80,128]{2,1,0:T(8,128)(2,1)}, f32[64,128]{1,0:T(8,128)}, bf16[8,384,128]{2,1,0:T(8,128)(2,1)}) custom-call(bf16[32,8,192]{2,1,0:T(8,128)(2,1)S(1)} %all_to_all.15.table, f32[1,64,128]{2,1,0:T(8,128)} %latents.1, s32[1,8]{1,0:T(1,128)} %bitcast.15, bf16[64,3072]{1,0:T(8,128)(2,1)} %w_in_h.1, f32[16,4,3072]{2,1,0:T(4,128)} %terms.3, ...), custom_call_target="tpu_custom_call" | custom-call | tf_op jit(solution)/shard_map/select/pallas_call | solution.py:396
  21.5 15.2 %all-to-all-start.1 = ((bf16[16,80,128]{2,1,0:T(8,128)(2,1)}), bf16[16,80,128]{2,1,0:T(8,128)(2,1)S(1)}, u32[]{:S(2)}, u32[]{:S(2)}) async-start(bf16[16,80,128]{2,1,0:T(8,128)(2,1)} %get-tuple-element.15), calls=%async_computation.1 | async-start | bytes 655360 | tf_op jit(solution)/shard_map/all_to_all | solution.py:520
  36.7 0.0 copy-done
  36.7 10.0 %fold_weights.1 = (bf16[8,384,128]{2,1,0:T(8,128)(2,1)}, bf16[16,64,128]{2,1,0:T(8,128)(2,1)}, f32[32,3072]{1,0:T(8,128)}, bf16[128,64]{1,0:T(8,128)(2,1)}, f32[664,128]{1,0:T(8,128)}) custom-call(s32[1]{0:T(128)} %bitcast.3.here, f32[16]{0:T(128)S(1)} %copy-done, f32[16,4,3072]{2,1,0:T(4,128)} %terms.3, ...), custom_call_target="tpu_custom_call", output_to_operand_aliasing={{0}: (11, {})} | custom-call | tf_op jit(solution)/shard_map/fold_weights/pallas_call | solution.py:438
  46.7 7.8 %all-to-all-done.1.arrived = bf16[16,80,128]{2,1,0:T(8,128)(2,1)S(1)} async-done(((bf16[16,80,128]{2,1,0:T(8,128)(2,1)}), bf16[16,80,128]{2,1,0:T(8,128)(2,1)S(1)}, u32[]{:S(2)}, u32[]{:S(2)}) %all-to-all-start.1) | async-done | bytes 327712 | tf_op jit(solution)/shard_map/all_to_all | solution.py:520
  54.5 4.3 %run_heads.1 = (bf16[16,64,128]{2,1,0:T(8,128)(2,1)S(1)}, f32[64,128]{1,0:T(8,128)S(1)}) custom-call(bf16[16,80,128]{2,1,0:T(8,128)(2,1)S(1)} %all-to-all-done.1.arrived, f32[32,3072]{1,0:T(8,128)} %get-tuple-element.18.lines_h, bf16[64,3072]{1,0:T(8,128)(2,1)} %w_in_h.1, bf16[64,3072]{1,0:T(8,128)(2,1)} %bitcast.13, bf16[3,3072,128]{2,1,0:T(8,128)(2,1)} %bitcast.11, ...), custom_call_target="tpu_custom_call" | custom-call | tf_op jit(solution)/shard_map/run_heads/pallas_call | solution.py:473
  58.8 22.4 %all_to_all.16 = bf16[16,64,128]{2,1,0:T(8,128)(2,1)S(1)} all-to-all(bf16[16,64,128]{2,1,0:T(8,128)(2,1)S(1)} %get-tuple-element.24), channel_id=1, replica_groups=mesh['tm'=16,'req'=32] {'tm'}, dimensions={0} | all-to-all | bytes 524288 | tf_op jit(solution)/shard_map/all_to_all | solution.py:528
  81.2 0.6 add_bitcast_fusion
  (1 shorter events, 0.0 us)
Async XLA Ops:
  0.0 36.7 %copy-start = (f32[16]{0:T(128)S(1)}, f32[16]{0:T(128)}, u32[]{:S(2)}) copy-start(f32[16]{0:T(128)} %steps.1) | copy-start | bytes 196
  21.5 33.1 %all-to-all-start.1 = ((bf16[16,80,128]{2,1,0:T(8,128)(2,1)}), bf16[16,80,128]{2,1,0:T(8,128)(2,1)S(1)}, u32[]{:S(2)}, u32[]{:S(2)}) async-start(bf16[16,80,128]{2,1,0:T(8,128)(2,1)} %get-tuple-element.15), calls=%async_computation.1 | async-start | bytes 655360 | tf_op jit(solution)/shard_map/all_to_all | solution.py:520

commit v12 on v10

--- a/solution.py
+++ b/solution.py
@@ -51,15 +51,15 @@
 
 
 def fold_inward(steps, centred, terms, w_qkv, rows, inward):
-    chans, head = centred.shape[0], w_qkv.shape[2]
+    chans = centred.shape[0]
     for step in steps:
         for j in range(4):
             scaled = centred[...] * (1.0 + terms[step * 4 + j, 2:3, :])
             rows[step % 2, j * chans : (j + 1) * chans, :] = scaled.astype(BF16)
-        for c in range(3):
-            turned = dot(rows[step % 2], w_qkv[c]).T.astype(BF16)
-            inward[2 * step, c * head : (c + 1) * head, :] = turned[:, : 2 * chans]
-            inward[2 * step + 1, c * head : (c + 1) * head, :] = turned[:, 2 * chans :]
+        wide = jnp.concatenate([w_qkv[c] for c in range(3)], axis=1)
+        turned = dot(rows[step % 2], wide).T.astype(BF16)
+        inward[2 * step] = turned[:, : 2 * chans]
+        inward[2 * step + 1] = turned[:, 2 * chans :]
 
 
 def select_kernel(

time: 80.6 us -> 82.2 us (1.020)
  waiting for transfers between devices: 7.55 us -> 9.5 us
  Pallas kernels: 20.1 us -> 18.4 us
  blocking collectives: 36 us -> 37.3 us
    all_to_all x1, waiting for transfers between devices: 7.55 us -> 9.5 us  [local(): arrived = lax.all_to_all(sent, 'tm', 0, 0)]
    all_to_all x1, blocking collectives: 21.1 us -> 22.4 us  [local(): parts = lax.all_to_all(sums, 'tm', 0, 0)]
    pallas_call x1, Pallas kernels: 7.12 us -> 5.89 us  [select(): pl.pallas_call(select_kernel, out_shape=(pltpu.HBM((times, block[0] + 2 *...]
  transfers between devices with their start and end apart: 1 -> 1, of which waited for: 1 -> 1; matrix products, arithmetic and copies ran while one was open for 0% -> 0% of each run, Pallas kernels for 11% -> 10%
where the time goes in v12:
time: 82.2 us; the launch traced here: 81.8 us
  blocking collectives  37.3 us (45%)
  Pallas kernels  18.4 us (22%)
  starting transfers between devices  15.2 us (18%)
  waiting for transfers between devices  9.5 us (12%)
    all_to_all x1, blocking collectives, local(): parts = lax.all_to_all(sums, 'tm', 0, 0)  22.4 us
    all_to_all x1, starting transfers between devices, local(): arrived = lax.all_to_all(sent, 'tm', 0, 0)  15.2 us
    all_to_all x1, blocking collectives, local(): table = lax.all_to_all(copies, 'req', 0, 0)  14.9 us
    all_to_all x1, waiting for transfers between devices, local(): arrived = lax.all_to_all(sent, 'tm', 0, 0)  9.5 us
    pallas_call x1, Pallas kernels, fold_weights(): pl.pallas_call(weights_kernel, out_shape=tuple((pltpu.HBM(*s) for s in sh...  8.24 us
    pallas_call x1, Pallas kernels, select(): pl.pallas_call(select_kernel, out_shape=(pltpu.HBM((times, block[0] + 2 *...  5.89 us
    pallas_call x1, Pallas kernels, run_heads(): pl.pallas_call(heads_kernel, out_shape=(jax.ShapeDtypeStruct((times, chan...  4.26 us
  transfers between devices with their start and end apart: 1, of which 1 were waited for; matrix products, arithmetic and copies ran while one was open for 0% of the time, Pallas kernels for 10%

profile of v12, /device:TPU:32, one launch (start us, length us, event | category | flops | bytes accessed | tf_op | source)
XLA Modules:
  0.0 81.8 jit_solution(5807146972322190200)
XLA Ops:
  0.0 0.0 copy-start
  0.0 0.7 broadcast_in_dim.12
  0.7 14.9 %all_to_all.15.table = bf16[32,8,192]{2,1,0:T(8,128)(2,1)S(1)} all-to-all(bf16[32,8,192]{2,1,0:T(8,128)(2,1)S(1)} %broadcast_in_dim.12), channel_id=1, replica_groups=mesh['tm'=16,'req'=32] {'req'}, dimensions={0} | all-to-all | bytes 196608 | tf_op jit(solution)/shard_map/all_to_all | solution.py:516
  15.6 5.9 %select.1 = (bf16[16,80,128]{2,1,0:T(8,128)(2,1)}, f32[64,128]{1,0:T(8,128)}, bf16[8,384,128]{2,1,0:T(8,128)(2,1)}) custom-call(bf16[32,8,192]{2,1,0:T(8,128)(2,1)S(1)} %all_to_all.15.table, f32[1,64,128]{2,1,0:T(8,128)} %latents.1, s32[1,8]{1,0:T(1,128)} %bitcast.15, bf16[64,3072]{1,0:T(8,128)(2,1)} %w_in_h.1, f32[16,4,3072]{2,1,0:T(4,128)} %terms.3, ...), custom_call_target="tpu_custom_call" | custom-call | tf_op jit(solution)/shard_map/select/pallas_call | solution.py:396
  21.5 15.2 %all-to-all-start.1 = ((bf16[16,80,128]{2,1,0:T(8,128)(2,1)}), bf16[16,80,128]{2,1,0:T(8,128)(2,1)S(1)}, u32[]{:S(2)}, u32[]{:S(2)}) async-start(bf16[16,80,128]{2,1,0:T(8,128)(2,1)} %get-tuple-element.15), calls=%async_computation.1 | async-start | bytes 655360 | tf_op jit(solution)/shard_map/all_to_all | solution.py:520
  36.8 0.0 copy-done
  36.8 8.2 %fold_weights.1 = (bf16[8,384,128]{2,1,0:T(8,128)(2,1)}, bf16[16,64,128]{2,1,0:T(8,128)(2,1)}, f32[32,3072]{1,0:T(8,128)}, bf16[128,64]{1,0:T(8,128)(2,1)}, f32[664,128]{1,0:T(8,128)}) custom-call(s32[1]{0:T(128)} %bitcast.3.here, f32[16]{0:T(128)S(1)} %copy-done, f32[16,4,3072]{2,1,0:T(4,128)} %terms.3, ...), custom_call_target="tpu_custom_call", output_to_operand_aliasing={{0}: (11, {})} | custom-call | tf_op jit(solution)/shard_map/fold_weights/pallas_call | solution.py:438
  45.0 9.5 %all-to-all-done.1.arrived = bf16[16,80,128]{2,1,0:T(8,128)(2,1)S(1)} async-done(((bf16[16,80,128]{2,1,0:T(8,128)(2,1)}), bf16[16,80,128]{2,1,0:T(8,128)(2,1)S(1)}, u32[]{:S(2)}, u32[]{:S(2)}) %all-to-all-start.1) | async-done | bytes 327712 | tf_op jit(solution)/shard_map/all_to_all | solution.py:520
  54.5 4.3 %run_heads.1 = (bf16[16,64,128]{2,1,0:T(8,128)(2,1)S(1)}, f32[64,128]{1,0:T(8,128)S(1)}) custom-call(bf16[16,80,128]{2,1,0:T(8,128)(2,1)S(1)} %all-to-all-done.1.arrived, f32[32,3072]{1,0:T(8,128)} %get-tuple-element.18.lines_h, bf16[64,3072]{1,0:T(8,128)(2,1)} %w_in_h.1, bf16[64,3072]{1,0:T(8,128)(2,1)} %bitcast.13, bf16[3,3072,128]{2,1,0:T(8,128)(2,1)} %bitcast.11, ...), custom_call_target="tpu_custom_call" | custom-call | tf_op jit(solution)/shard_map/run_heads/pallas_call | solution.py:473
  58.8 22.4 %all_to_all.16 = bf16[16,64,128]{2,1,0:T(8,128)(2,1)S(1)} all-to-all(bf16[16,64,128]{2,1,0:T(8,128)(2,1)S(1)} %get-tuple-element.24), channel_id=1, replica_groups=mesh['tm'=16,'req'=32] {'tm'}, dimensions={0} | all-to-all | bytes 524288 | tf_op jit(solution)/shard_map/all_to_all | solution.py:528
  81.2 0.6 add_bitcast_fusion
  (1 shorter events, 0.0 us)
Async XLA Ops:
  0.0 36.8 %copy-start = (f32[16]{0:T(128)S(1)}, f32[16]{0:T(128)}, u32[]{:S(2)}) copy-start(f32[16]{0:T(128)} %steps.1) | copy-start | bytes 196
  21.5 33.0 %all-to-all-start.1 = ((bf16[16,80,128]{2,1,0:T(8,128)(2,1)}), bf16[16,80,128]{2,1,0:T(8,128)(2,1)S(1)}, u32[]{:S(2)}, u32[]{:S(2)}) async-start(bf16[16,80,128]{2,1,0:T(8,128)(2,1)} %get-tuple-element.15), calls=%async_computation.1 | async-start | bytes 655360 | tf_op jit(solution)/shard_map/all_to_all | solution.py:520
